TPU v7x, 32 devices: a whole 2x2x4 slice. The times are simulated.
32 devices in a mesh: groups: 2 (over y), seq: 8 (over z, x), tensor: 2 (over core).
Axes of the slice: x: 2, y: 2, z: 4, core: 2. Of those that a mesh axis runs over, the one named last changes fastest.
Arguments:
- inputs: bfloat16 [2048, 14336], P(('groups', 'seq'), 'tensor'), parts along dimension 0
- out_grads: bfloat16 [2048, 8192], P(('groups', 'seq'), 'tensor'), parts along dimension 0
- proj_in: bfloat16 [14336, 64], P('tensor'), may hold values from -0.046875 to 0.046875
- proj_out: bfloat16 [8192, 64], P('tensor'), may hold values from -0.0625 to 0.0625
- queries: bfloat16 [512, 4096], P(('groups', 'seq', 'tensor')), parts along dimension 0, may hold values from -6 to 6
- lengths: int32 [4], P('groups'), parts along dimension 0, may hold values from 1 to 512, 768 in all
Outputs:
- scores: float32 [512, 2], P(('groups', 'seq', 'tensor')), parts along dimension 0
There are 2 independent parts, one for each index of `groups`. A program takes and returns all parts, laid end to end along the dimension named above; an argument that names none is the same for every part. Nothing has to cross between parts.
Inputs may be any that keep to these rules, and one draw needn't show every extreme that they name: lengths sum to 768.
All inputs are finite; a program needn't handle non-finite values.
Results may differ from a plain program's by a relative error of at most 0.035.
Values may be sent and summed in bfloat16 or wider, within the bound.
No kernel may reach another device: no remote copies, remote signals or barrier semaphores. Data moves between devices by JAX's collectives and lax.ppermute only.
A program may use at most 64 MiB of HBM per device.

v0:
```python
import math

import jax
import jax.numpy as jnp
from jax import lax
from jax.sharding import PartitionSpec as P

LEN = 512


damping = 0.1


def factor_inverse(moment, total, width):
    eye_mat = jnp.eye(width, dtype=jnp.float32)
    matrix = moment / total + damping * eye_mat
    lower = jnp.linalg.cholesky(matrix)
    return jax.scipy.linalg.cho_solve((lower, True), eye_mat)


def precondition(query_rows, inverse_out, inverse_in):
    width = inverse_in.shape[0]
    square = query_rows.astype(jnp.float32).reshape(query_rows.shape[0], width, width)
    mixed = jnp.einsum(
        "ij,qjk,kl->qil", inverse_out, square, inverse_in, precision=lax.Precision.HIGHEST
    )
    return mixed.reshape(query_rows.shape[0], width * width).astype(jnp.bfloat16)


def shards(inputs, out_grads, proj_in, proj_out, queries, lengths):
    width = proj_in.shape[1]
    seq_count = lengths.shape[0]
    token_rows = inputs.shape[0]
    partial_x = jnp.dot(inputs, proj_in, preferred_element_type=jnp.float32)
    partial_g = jnp.dot(out_grads, proj_out, preferred_element_type=jnp.float32)
    summed = lax.psum_scatter(
        jnp.concatenate([partial_x, partial_g], axis=1), "tensor", scatter_dimension=0, tiled=True
    )
    proj_x = summed[:, :width]
    proj_g = summed[:, width:]
    my_rows = summed.shape[0]
    device = lax.axis_index(("seq", "tensor"))
    first_token = device * my_rows
    positions = first_token + jnp.arange(my_rows, dtype=jnp.int32)
    own_seq = first_token // LEN
    seq_length = lax.dynamic_index_in_dim(lengths, own_seq, 0, keepdims=False)
    valid = (positions % LEN < seq_length).astype(jnp.float32)[:, None]
    masked_x = proj_x * valid
    masked_g = proj_g * valid
    local_in = jnp.dot(masked_x.T, proj_x, precision=lax.Precision.HIGHEST)
    local_out = jnp.dot(masked_g.T, proj_g, precision=lax.Precision.HIGHEST)
    moment_in, moment_out = lax.psum((local_in, local_out), ("seq", "tensor"))
    total = jnp.sum(lengths).astype(jnp.float32)
    inverse_in = factor_inverse(moment_in, total, width)
    inverse_out = factor_inverse(moment_out, total, width)
    flat_grad = jnp.dot(masked_g.T, proj_x, precision=lax.Precision.HIGHEST).reshape(width * width)
    scaling = 1.0 / (width * math.sqrt(LEN))
    every_query = lax.all_gather(
        precondition(queries, inverse_out, inverse_in), ("seq", "tensor"), axis=0, tiled=True
    )
    products = jnp.dot(every_query.astype(jnp.float32), flat_grad, precision=lax.Precision.HIGHEST)
    seq_devices = lax.axis_size("seq")
    by_owner = products.reshape(seq_devices, products.shape[0] // seq_devices)
    received = lax.all_to_all(by_owner, "seq", split_axis=0, concat_axis=0, tiled=True)
    block = lax.psum_scatter(received, "tensor", scatter_dimension=1, tiled=True)
    owners = jnp.arange(seq_devices, dtype=jnp.int32) * token_rows // LEN
    hits = (owners[:, None] == jnp.arange(seq_count, dtype=jnp.int32)[None, :]).astype(jnp.float32)
    scores = jnp.dot(block.T, hits, precision=lax.Precision.HIGHEST)
    return scores * scaling


def solution(mesh):
    placed = (
        P(("groups", "seq"), "tensor"),
        P(("groups", "seq"), "tensor"),
        P("tensor", None),
        P("tensor", None),
        P(("groups", "seq", "tensor"), None),
        P("groups"),
    )
    return jax.shard_map(
        shards,
        mesh=mesh,
        in_specs=placed,
        out_specs=P(("groups", "seq", "tensor"), None),
        check_vma=False,
    )
```

profile of v0, /device:TPU:0, one launch (start us, length us, event | category | flops | bytes accessed | tf_op | source)
XLA Modules:
  0.0 181.6 jit_solution(3572672202958789278)
XLA Ops:
  6.5 0.0 copy-start
  6.5 0.0 reduce-scatter.7.cloned.1.call-start
  6.6 1.4 copy-done
  8.0 1.9 %fusion.28 = f32[128,64]{0,1:T(8,128)S(1)} fusion(bf16[128,7168]{1,0:T(8,128)(2,1)S(1)} %copy-done, bf16[7168,64]{0,1:T(8,128)(2,1)} %param.11), kind=kOutput, calls=%fused_computation.57 | convolution fusion | flops 117440512 | bytes 2785280 | tf_op jit(solution)/shard_map/dot_general | solution.py:34
  10.0 0.0 copy-done.3
  10.0 0.5 fusion.29
  10.5 0.7 copy.18
  11.2 0.0 reduce-scatter.7.cloned.1.call-update
  11.2 0.0 all-gather.2.cloned.1.call-start
  11.3 0.6 reduce_sum.9
  12.6 0.6 dynamic_slice.4
  13.2 0.2 reshape.58
  13.4 0.7 compare_convert_fusion
  14.1 7.4 %reduce-scatter.7.cloned.1.call-done = f32[64,128]{1,0:T(8,128)} async-done(((f32[128,128]{1,0:T(8,128)}), f32[64,128]{1,0:T(8,128)}) %reduce-scatter.7.cloned.1.call-update) | async-done | bytes 32784
  21.5 0.9 fusion.27
  22.5 0.1 copy.23
  22.5 0.1 copy.22
  22.6 1.0 fusion.12
  23.6 1.1 fusion.16
  24.7 62.0 %all-reduce = (f32[64,64]{0,1:T(8,128)S(1)}, f32[64,64]{0,1:T(8,128)S(1)}) all-reduce(f32[64,64]{0,1:T(8,128)S(1)} %fusion.16, f32[64,64]{0,1:T(8,128)S(1)} %fusion.12), channel_id=1, replica_groups=mesh['groups'=2,'seq'=8,'tensor'=2] {'seq','tensor'}, use_global_device_ids=true, to_apply=%region_1.2 | all-reduce | flops 8192 | bytes 65536 | tf_op jit(solution)/shard_map/psum | solution.py:52
  86.7 0.1 copy.14
  86.8 5.8 %cholesky.55 = f32[64,64]{1,0:T(8,128)S(1)} custom-call(f32[64,64]{1,0:T(8,128)S(1)} %fusion.8), custom_call_target="Cholesky" | custom-call | tf_op jit(solution)/shard_map/jit(cholesky)/cholesky | solution.py:17
  92.7 0.6 compare_reduce_fusion
  93.4 0.7 fusion.5
  94.0 4.9 %custom-call.9 = f32[1,64,64]{1,2,0:T(8,128)S(1)} custom-call(f32[1,64,64]{2,1,0:T(8,128)S(1)} %fusion.5), custom_call_target="InvertDiagBlocksLowerTriangular" | custom-call | tf_op jit(solution)/shard_map/jit(_cho_solve)/triangular_solve | solution.py:18
  98.9 0.3 fusion
  99.2 0.2 convolution_bitcast_fusion.1
  99.4 0.1 copy.12
  99.4 5.9 %cholesky.44 = f32[64,64]{1,0:T(8,128)S(1)} custom-call(f32[64,64]{1,0:T(8,128)S(1)} %fusion.11), custom_call_target="Cholesky" | custom-call | tf_op jit(solution)/shard_map/jit(cholesky)/cholesky | solution.py:17
  105.3 0.6 compare_reduce_fusion.1
  106.0 0.7 fusion.4
  106.6 4.9 %custom-call.8 = f32[1,64,64]{1,2,0:T(8,128)S(1)} custom-call(f32[1,64,64]{2,1,0:T(8,128)S(1)} %fusion.4), custom_call_target="InvertDiagBlocksLowerTriangular" | custom-call | tf_op jit(solution)/shard_map/jit(_cho_solve)/triangular_solve | solution.py:18
  111.5 0.2 fusion.2
  111.8 0.2 convolution_bitcast_fusion.2
  112.0 0.3 convolution_bitcast_fusion
  112.3 0.6 convolution_convert_fusion
  112.9 0.9 convert_element_type.29
  113.8 0.0 all-gather.2.cloned.1.call-update
  113.8 0.0 reduce-scatter.9.cloned.1.call-start
  113.9 0.2 fusion.14
  114.1 0.1 reshape.62
  114.2 38.5 %all-gather.2.cloned.1.call-done = bf16[256,4096]{1,0:T(8,128)(2,1)} async-done(((bf16[16,4096]{1,0:T(8,128)(2,1)}), bf16[256,4096]{1,0:T(8,128)(2,1)}) %all-gather.2.cloned.1.call-update) | async-done | bytes 2097168 | tf_op jit(solution)/shard_map/all_gather | solution.py:58
  152.6 5.7 %convolution_bitcast_fusion.3 = f32[8,1,32]{2,1,0:T(1,128)S(1)} fusion(bf16[8,32,4096]{2,1,0:T(8,128)(2,1)} %bitcast.52, f32[4096,1,1]{0,1,2:T(1,128)S(1)} %reshape.62), kind=kOutput, calls=%fused_computation.4 | convolution fusion | flops 12582912 | bytes 2114560 | tf_op jit(solution)/shard_map/dot_general | solution.py:61
  158.4 9.6 %all_to_all.12 = f32[8,1,32]{2,1,0:T(1,128)S(1)} all-to-all(f32[8,1,32]{2,1,0:T(1,128)S(1)} %convolution_bitcast_fusion.3), channel_id=1, replica_groups=mesh['groups'=2,'seq'=8,'tensor'=2] {'seq'}, dimensions={0} | all-to-all | bytes 2048 | tf_op jit(solution)/shard_map/all_to_all | solution.py:64
  168.0 0.7 copy.20
  168.7 0.0 reduce-scatter.9.cloned.1.call-update
  168.7 4.8 %reduce-scatter.9.cloned.1.call-done = f32[16,8]{1,0:T(8,128)} async-done(((f32[32,8]{1,0:T(8,128)}), f32[16,8]{1,0:T(8,128)}) %reduce-scatter.9.cloned.1.call-update) | async-done | bytes 528
  173.5 1.5 convolution_multiply_fusion
  (16 shorter events, 0.1 us)
Async XLA Ops:
  6.5 1.5 copy-start
  6.5 3.4 %copy-start.3 = (bf16[4096,64]{0,1:T(8,128)(2,1)S(1)}, bf16[4096,64]{0,1:T(8,128)(2,1)}, u32[]{:S(2)}) copy-start(bf16[4096,64]{0,1:T(8,128)(2,1)} %param.12) | copy-start | bytes 1572868
  6.5 3.4 %copy-start.1 = (bf16[128,4096]{1,0:T(8,128)(2,1)S(1)}, bf16[128,4096]{1,0:T(8,128)(2,1)}, u32[]{:S(2)}) copy-start(bf16[128,4096]{1,0:T(8,128)(2,1)} %param.10) | copy-start | bytes 3145732
  6.5 4.8 %copy-start.5 = (s32[2]{0:T(128)S(1)}, s32[2]{0:T(128)}, u32[]{:S(2)}) copy-start(s32[2]{0:T(128)} %param.14) | copy-start | bytes 28
  6.5 6.7 %copy-start.4 = (bf16[16,4096]{1,0:T(8,128)(2,1)S(1)}, bf16[16,4096]{1,0:T(8,128)(2,1)}, u32[]{:S(2)}) copy-start(bf16[16,4096]{1,0:T(8,128)(2,1)} %param.13) | copy-start | bytes 393220
  6.5 15.0 %reduce-scatter.7.cloned.1.call-start = ((), (), s32[]{:S(2)}) async-start(), calls=%async_computation.4 | async-start | bytes 98304
  11.2 141.4 %all-gather.2.cloned.1.call-start = ((), (), s32[]{:S(2)}) async-start(), calls=%async_computation.3 | async-start | bytes 2228224 | tf_op jit(solution)/shard_map/all_gather | solution.py:58
  21.5 92.4 %copy-start.2 = (f32[64,128]{1,0:T(8,128)S(1)}, f32[64,128]{1,0:T(8,128)}, u32[]{:S(2)}) copy-start(f32[64,128]{1,0:T(8,128)} %reduce-scatter.7.cloned.1.call-done) | copy-start | bytes 98308
  113.8 59.7 %reduce-scatter.9.cloned.1.call-start = ((), (), s32[]{:S(2)}) async-start(), calls=%async_computation.5 | async-start | bytes 24576
Sparse Core Ops, SparseCore 0:
  11.4 10.1 reduce-scatter.6
  114.0 38.6 all-gather.1
  168.8 4.6 reduce-scatter.8
where the time goes:
time: 182 us
  blocking collectives  71.7 us (39%)
  waiting for transfers between devices  50.7 us (28%)
  other arithmetic  25.5 us (14%)
  between operations  14 us (8%)
  matrix products  13.6 us (7%)
  local copies, waits for them, and re-layouts  5.94 us (3%)
    psum x1, blocking collectives, shards(): moment_in, moment_out = lax.psum((local_in, local_out), ('seq', 'tensor'))  62 us
    all_gather x1, waiting for transfers between devices, shards(): lax.all_gather(precondition(queries, inverse_out, inverse_in), ('seq', 't...  38.5 us
    another operation x6, other arithmetic, factor_inverse(): lower = jnp.linalg.cholesky(matrix)  13 us
    unnamed x5, waiting for transfers between devices  12.3 us
    another operation x4, other arithmetic, factor_inverse(): return jax.scipy.linalg.cho_solve((lower, True), eye_mat)  11.1 us
    all_to_all x1, blocking collectives, shards(): lax.all_to_all(by_owner, 'seq', split_axis=0, concat_axis=0, tiled=True)  9.64 us
    dot_general x1, matrix products, shards(): jnp.dot(every_query.astype(jnp.float32), flat_grad, precision=lax.Precisi...  5.73 us
    unnamed x17, local copies, waits for them, and re-layouts  3.94 us
  transfers between devices with their start and end apart: 3, of which 3 were waited for; matrix products, arithmetic and copies ran while one was open for 1% of the time, Pallas kernels for 0%

commit v1 on v0

v1 whole, which is shorter than its diff:
```python
import functools
import math

import jax
import jax.numpy as jnp
from jax import lax
from jax.experimental import pallas as pl
from jax.experimental.pallas import tpu as pltpu
from jax.sharding import PartitionSpec as P

LEN = 512
DAMPING = 0.1
PANEL = 8
VMEM = pl.BlockSpec(memory_space=pltpu.VMEM)
HBM = pl.BlockSpec(memory_space=pltpu.HBM)
NT = (((1,), (1,)), ((), ()))
F32 = jnp.float32


def half(shape):
    return lax.broadcasted_iota(jnp.int32, shape, 1) < shape[1] // 2


def project(chunks, lengths, inputs, grads, proj_in, proj_out, out, *scratch):
    x_buf, g_buf, px_buf, pg_buf, count, sems = scratch
    width, tokens = px_buf.shape[0], x_buf.shape[0]
    jobs, sem = [], 0
    for rows, row_buf, mat, mat_buf, parts, lo in (
        (inputs, x_buf, proj_in, px_buf, chunks[0], 0),
        (grads, g_buf, proj_out, pg_buf, chunks[1], width),
    ):
        step = rows.shape[1] // parts
        for part in range(parts):
            cols = pl.ds(part * step, step)
            pair = []
            for src, dst in ((mat, mat_buf), (rows, row_buf)):
                pair.append(pltpu.make_async_copy(src.at[:, cols], dst.at[:, cols], sems.at[sem]))
                pair[-1].start()
                sem += 1
            jobs.append((pair, mat_buf, row_buf, cols, lo))
    scalars = pltpu.make_async_copy(lengths, count, sems.at[sem])
    scalars.start()
    totals = {}
    for pair, mat_buf, row_buf, cols, lo in jobs:
        for copy in pair:
            copy.wait()
        part = lax.dot_general(mat_buf[:, cols], row_buf[:, cols], NT, preferred_element_type=F32)
        totals[lo] = part if lo not in totals else totals[lo] + part
    scalars.wait()
    first = lax.axis_index("seq") * tokens
    valid = lax.broadcasted_iota(jnp.int32, (width, tokens), 1) + first % LEN < count[first // LEN]
    for lo, total in totals.items():
        out[lo : lo + width, :] = jnp.where(valid, total, 0.0)


def moments(tokens, mine, other, out):
    z = mine[...] + other[...]
    square = lax.dot_general(z, z, NT, preferred_element_type=F32, precision=lax.Precision.HIGHEST)
    width = square.shape[0] // 2
    top, bottom = square[:width], square[width:]
    left = half(top.shape)
    is_moment = lax.axis_index("tensor") == 1
    own = lax.axis_index("seq") * tokens // LEN
    twice = jnp.where(left, bottom, pltpu.roll(bottom, width, 1))
    for slab in range(out.shape[0]):
        side = jnp.where(left, 2 * slab, 2 * slab + 1)
        cross = jnp.where(side == own, twice, 0.0)
        moment = jnp.where(left, top, bottom) if slab == 0 else jnp.zeros_like(top)
        out[slab] = jnp.where(is_moment, moment, cross)


def invert(matrix):
    width = matrix.shape[0]
    blocks = width // 8
    lane = lax.broadcasted_iota(jnp.int32, (8, 2 * width), 1)
    row_of = lax.broadcasted_iota(jnp.int32, (8, 2 * width), 0)
    column = lane % width
    right = lane - column
    rows = [matrix[8 * b : 8 * b + 8] for b in range(blocks)]
    for panel in range(blocks):
        first = 8 * panel
        cols = []
        for t in range(8):
            index = right + (first + t)
            cols.append([jnp.take_along_axis(rows[b], index, axis=1) for b in range(blocks)])
        inside = (column >= first) & (column < first + 8)
        rows = [jnp.where(inside, 0.0, r) for r in rows]
        for t in range(8):
            unit = jnp.where(column[:1] == first + t, 1.0, 0.0)
            inverse = 1.0 / cols[t][panel][t : t + 1]
            pivot = (rows[panel][t : t + 1] + unit) * inverse
            for b in range(blocks):
                rows[b] = rows[b] - cols[t][b] * pivot
            rows[panel] = jnp.where(row_of == t, pivot, rows[panel])
            for j in range(t + 1, 8):
                scaled = cols[j][panel][t : t + 1] * inverse
                cols[j] = [cols[j][b] - cols[t][b] * scaled for b in range(blocks)]
                cols[j][panel] = jnp.where(row_of == t, scaled, cols[j][panel])
    return jnp.concatenate(rows, axis=0)


def inverses(total, mine, other, out):
    out[...] = mine[...] + other[...]

    @pl.when(lax.axis_index("tensor") == 1)
    def _():
        both = out[0]
        width = both.shape[0]
        lane = lax.broadcasted_iota(jnp.int32, both.shape, 1)
        row = lax.broadcasted_iota(jnp.int32, both.shape, 0)
        damped = both * (1.0 / total) + jnp.where(lane % width == row, DAMPING, 0.0)
        out[0] = invert(damped)


def score(scaling, mine, other, queries, out, weights):
    is_moment = lax.axis_index("tensor") == 1
    inv = jnp.where(is_moment, mine[0], other[0])
    width = inv.shape[0]
    inv_out = pltpu.roll(inv, width, 1)[:, :width]
    left = half(inv.shape)
    inv_twice = jnp.where(left, inv, pltpu.roll(inv, width, 1))
    upper = jnp.where(left, inv_twice, 0.0)
    lower = jnp.where(left, 0.0, inv_twice)
    diagonal = jnp.concatenate([upper, lower], axis=0)
    dot = functools.partial(jnp.dot, preferred_element_type=F32, precision=lax.Precision.HIGHEST)
    for slab in range(mine.shape[0]):
        grads = jnp.where(is_moment, other[slab], mine[slab])
        weights[...] = dot(dot(inv_out, grads), diagonal) * scaling
        even = weights[pl.ds(0, width // 2, 2), :]
        odd = weights[pl.ds(1, width // 2, 2), :]
        pair = left[: width // 2]
        flat = (
            jnp.where(pair, even, pltpu.roll(odd, width, 1)),
            jnp.where(pair, pltpu.roll(even, width, 1), odd),
        )
        sums = [jnp.zeros((queries.shape[0], 2 * width), F32) for _ in flat]
        for m in range(width // 2):
            block = queries[:, 2 * width * m : 2 * width * (m + 1)].astype(F32)
            for s in range(2):
                sums[s] = sums[s] + block * flat[s][m : m + 1]
        for s in range(2):
            if 2 * slab + s < out.shape[1]:
                out[:, 2 * slab + s : 2 * slab + s + 1] = jnp.sum(sums[s], axis=1, keepdims=True)


def swap(array):
    return lax.ppermute(array, "tensor", [(0, 1), (1, 0)])


def exchange(array, distance, devices):
    pairs = [(2 * i + c, 2 * (i ^ distance) + c) for i in range(devices) for c in range(2)]
    return lax.ppermute(array, ("seq", "tensor"), pairs)


def shards(inputs, out_grads, proj_in, proj_out, queries, lengths):
    width = proj_in.shape[1]
    tokens = inputs.shape[0]
    seq_count = lengths.shape[0]
    slabs = (seq_count + 1) // 2
    chunks = (4, 2)
    params = pltpu.CompilerParams(vmem_limit_bytes=16 << 20)
    partial_z = pl.pallas_call(
        functools.partial(project, chunks),
        out_shape=jax.ShapeDtypeStruct((2 * width, tokens), F32),
        in_specs=[HBM] * 5,
        out_specs=VMEM,
        scratch_shapes=[
            pltpu.VMEM(inputs.shape, inputs.dtype),
            pltpu.VMEM(out_grads.shape, out_grads.dtype),
            pltpu.VMEM(proj_in.shape[::-1], proj_in.dtype),
            pltpu.VMEM(proj_out.shape[::-1], proj_out.dtype),
            pltpu.SMEM(lengths.shape, lengths.dtype),
            pltpu.SemaphoreType.DMA((2 * sum(chunks) + 1,)),
        ],
        compiler_params=params,
        name="project",
    )(lengths, inputs, out_grads, proj_in.T, proj_out.T)
    payload_shape = jax.ShapeDtypeStruct((slabs, width, 2 * width), F32)
    payload = pl.pallas_call(
        functools.partial(moments, tokens),
        out_shape=payload_shape,
        in_specs=[VMEM] * 2,
        out_specs=VMEM,
        compiler_params=params,
        name="moments",
    )(partial_z, swap(partial_z))
    devices = lax.axis_size("seq")
    distance = 1
    while 2 * distance < devices:
        payload = payload + exchange(payload, distance, devices)
        distance *= 2
    total = 3 * seq_count * LEN // 4
    ready = pl.pallas_call(
        functools.partial(inverses, float(total)),
        out_shape=payload_shape,
        in_specs=[VMEM] * 2,
        out_specs=VMEM,
        compiler_params=params,
        name="inverses",
    )(payload, exchange(payload, distance, devices))
    scaling = 1.0 / (width * math.sqrt(LEN))
    return pl.pallas_call(
        functools.partial(score, scaling),
        out_shape=jax.ShapeDtypeStruct((queries.shape[0], seq_count), F32),
        in_specs=[VMEM] * 3,
        out_specs=VMEM,
        scratch_shapes=[pltpu.VMEM((width, 2 * width), F32)],
        compiler_params=params,
        name="score",
    )(ready, swap(ready), queries)


def solution(mesh):
    placed = (
        P(("groups", "seq"), "tensor"),
        P(("groups", "seq"), "tensor"),
        P("tensor", None),
        P("tensor", None),
        P(("groups", "seq", "tensor"), None),
        P("groups"),
    )
    return jax.shard_map(
        shards,
        mesh=mesh,
        in_specs=placed,
        out_specs=P(("groups", "seq", "tensor"), None),
        check_vma=False,
    )
```

time: 182 us -> 26.2 us (0.14)
  blocking collectives: 71.7 us -> 0 us
  waiting for transfers between devices: 50.7 us -> 7.78 us
  other arithmetic: 25.5 us -> 0.01 us
  between operations: 14 us -> 0.03 us
  matrix products: 13.6 us -> 0 us
  starting transfers between devices: 0.12 us -> 8.57 us
  Pallas kernels: 0 us -> 3.33 us
    psum x1 -> x0, blocking collectives: 62 us -> none  [shards(): moment_in, moment_out = lax.psum((local_in, local_out), ('seq', 'tensor'))]
    all_gather x1 -> x0, waiting for transfers between devices: 38.5 us -> none  [shards(): lax.all_gather(precondition(queries, inverse_out, inverse_in), ('seq', 't...]
    another operation x10 -> x0, other arithmetic: 24.2 us -> none  [the longest x6 13 us: factor_inverse(): lower = jnp.linalg.cholesky(matrix)]
    dot_general x9 -> x0, matrix products: 12.8 us -> none  [the longest x1 5.73 us: shards(): jnp.dot(every_query.astype(jnp.float32), flat_grad, precision=lax.Precisi...]
    unnamed x5 -> x0, waiting for transfers between devices: 12.3 us -> none
    all_to_all x1 -> x0, blocking collectives: 9.64 us -> none  [shards(): lax.all_to_all(by_owner, 'seq', split_axis=0, concat_axis=0, tiled=True)]
    ppermute x0 -> x5, starting transfers between devices: none -> 8.57 us  [the longest x3 8.05 us: exchange(): return lax.ppermute(array, ('seq', 'tensor'), pairs)]
    ppermute x0 -> x5, waiting for transfers between devices: none -> 7.78 us  [the longest x3 5.68 us: exchange(): return lax.ppermute(array, ('seq', 'tensor'), pairs)]
  transfers between devices with their start and end apart: 3 -> 5, of which waited for: 3 -> 5; matrix products, arithmetic and copies ran while one was open for 1% -> 0% of each run, Pallas kernels for 0% -> 0%
where the time goes in v1:
time: 26.2 us; the launch traced here: 26 us
  starting transfers between devices  8.57 us (33%)
  waiting for transfers between devices  7.78 us (30%)
  local copies, waits for them, and re-layouts  6.24 us (24%)
  Pallas kernels  3.33 us (13%)
    ppermute x3, starting transfers between devices, exchange(): return lax.ppermute(array, ('seq', 'tensor'), pairs)  8.05 us
    ppermute x3, waiting for transfers between devices, exchange(): return lax.ppermute(array, ('seq', 'tensor'), pairs)  5.68 us
    unnamed x12, local copies, waits for them, and re-layouts  5.6 us
    pallas_call x1, Pallas kernels, shards(): pl.pallas_call(functools.partial(project, chunks), out_shape=jax.ShapeDty...  2.37 us
    ppermute x2, waiting for transfers between devices, swap(): return lax.ppermute(array, 'tensor', [(0, 1), (1, 0)])  2.1 us
    pallas_call x1, local copies, waits for them, and re-layouts, shards(): pl.pallas_call(functools.partial(score, scaling), out_shape=jax.ShapeDtyp...  0.64 us
    pallas_call x1, Pallas kernels, shards(): pl.pallas_call(functools.partial(score, scaling), out_shape=jax.ShapeDtyp...  0.62 us
  transfers between devices with their start and end apart: 5, of which 5 were waited for; matrix products, arithmetic and copies ran while one was open for 0% of the time, Pallas kernels for 0%

profile of v1, /device:TPU:0, one launch (start us, length us, event | category | flops | bytes accessed | tf_op | source)
XLA Modules:
  0.0 26.0 jit_solution(5537754435798354430)
XLA Ops:
  0.0 0.0 copy-start
  0.0 1.5 %copy-done = bf16[128,7168]{1,0:T(8,128)(2,1)S(1)} copy-done((bf16[128,7168]{1,0:T(8,128)(2,1)S(1)}, bf16[128,7168]{1,0:T(8,128)(2,1)}, u32[]{:S(2)}) %copy-start) | copy-done | bytes 1835032
  1.5 0.0 copy-start.1
  1.5 1.2 %copy-done.1 = bf16[128,4096]{1,0:T(8,128)(2,1)S(1)} copy-done((bf16[128,4096]{1,0:T(8,128)(2,1)S(1)}, bf16[128,4096]{1,0:T(8,128)(2,1)}, u32[]{:S(2)}) %copy-start.1) | copy-done | bytes 1048600
  2.7 0.0 copy-start.2
  2.7 1.2 %copy-done.2 = bf16[7168,64]{0,1:T(8,128)(2,1)S(1)} copy-done((bf16[7168,64]{0,1:T(8,128)(2,1)S(1)}, bf16[7168,64]{0,1:T(8,128)(2,1)}, u32[]{:S(2)}) %copy-start.2) | copy-done | bytes 917528
  3.9 0.0 copy-start.3
  3.9 1.0 %copy-done.3 = bf16[4096,64]{0,1:T(8,128)(2,1)S(1)} copy-done((bf16[4096,64]{0,1:T(8,128)(2,1)S(1)}, bf16[4096,64]{0,1:T(8,128)(2,1)}, u32[]{:S(2)}) %copy-start.3) | copy-done | bytes 524312
  4.9 0.0 copy-start.5
  4.9 0.7 %copy-done.5 = s32[2]{0:T(128)S(1)} copy-done((s32[2]{0:T(128)S(1)}, s32[2]{0:T(128)}, u32[]{:S(2)}) %copy-start.5) | copy-done | bytes 32
  5.6 0.0 copy-start.4
  5.6 2.4 %project.1.mine = f32[128,128]{1,0:T(8,128)S(1)} custom-call(s32[2]{0:T(128)S(1)} %copy-done.5, bf16[128,7168]{1,0:T(8,128)(2,1)S(1)} %copy-done, bf16[128,4096]{1,0:T(8,128)(2,1)S(1)} %copy-done.1, bf16[64,7168]{1,0:T(8,128)(2,1)S(1)} %bitcast.2, bf16[64,4096]{1,0:T(8,128)(2,1)S(1)} %bitcast.3), custom_call_target="tpu_custom_call" | custom-call | tf_op jit(solution)/shard_map/project/pallas_call | solution.py:162
  8.0 0.5 %collective-permute-start = (f32[128,128]{1,0:T(8,128)S(1)}, f32[128,128]{1,0:T(8,128)S(1)}, u32[]{:S(2)}, u32[]{:S(2)}) collective-permute-start(f32[128,128]{1,0:T(8,128)S(1)} %project.1.mine), channel_id=1, source_target_pairs={{0,1},{1,0},{2,3},{3,2},{4,5},{5,4},{6,7},{7,6},{8,9},{9,8},{10,11... | collective-permute-start | bytes 196616 | tf_op jit(solution)/shard_map/ppermute | solution.py:147
  8.5 0.9 %collective-permute-done.other = f32[128,128]{1,0:T(8,128)S(1)} collective-permute-done((f32[128,128]{1,0:T(8,128)S(1)}, f32[128,128]{1,0:T(8,128)S(1)}, u32[]{:S(2)}, u32[]{:S(2)}) %collective-permute-start) | collective-permute-done | bytes 65568 | tf_op jit(solution)/shard_map/ppermute | solution.py:147
  9.4 0.3 %moments.1 = f32[1,64,128]{2,1,0:T(8,128)S(1)} custom-call(f32[128,128]{1,0:T(8,128)S(1)} %project.1.mine, f32[128,128]{1,0:T(8,128)S(1)} %collective-permute-done.other), custom_call_target="tpu_custom_call" | custom-call | tf_op jit(solution)/shard_map/moments/pallas_call | solution.py:179
  9.7 2.9 %collective-permute-start.1 = (f32[1,64,128]{2,1,0:T(8,128)S(1)}, f32[1,64,128]{2,1,0:T(8,128)S(1)}, u32[]{:S(2)}, u32[]{:S(2)}) collective-permute-start(f32[1,64,128]{2,1,0:T(8,128)S(1)} %moments.1), channel_id=1, source_target_pairs={{0,2},{1,3},{2,0},{3,1},{4,6},{5,7},{6,4},{7,5},{8,10},{9,11},{10,... | collective-permute-start | bytes 98312 | tf_op jit(solution)/shard_map/ppermute | solution.py:152
  12.6 1.9 %collective-permute-done.1 = f32[1,64,128]{2,1,0:T(8,128)S(1)} collective-permute-done((f32[1,64,128]{2,1,0:T(8,128)S(1)}, f32[1,64,128]{2,1,0:T(8,128)S(1)}, u32[]{:S(2)}, u32[]{:S(2)}) %collective-permute-start.1) | collective-permute-done | bytes 32800 | tf_op jit(solution)/shard_map/ppermute | solution.py:152
  14.5 2.1 %collective-permute-start.2 = (f32[1,64,128]{2,1,0:T(8,128)S(1)}, f32[1,64,128]{2,1,0:T(8,128)S(1)}, u32[]{:S(2)}, u32[]{:S(2)}) collective-permute-start(f32[1,64,128]{2,1,0:T(8,128)S(1)} %add.6), channel_id=1, source_target_pairs={{0,4},{1,5},{2,6},{3,7},{4,0},{5,1},{6,2},{7,3},{8,12},{9,13},{10,... | collective-permute-start | bytes 98312 | tf_op jit(solution)/shard_map/ppermute | solution.py:152
  16.6 1.9 %collective-permute-done.2 = f32[1,64,128]{2,1,0:T(8,128)S(1)} collective-permute-done((f32[1,64,128]{2,1,0:T(8,128)S(1)}, f32[1,64,128]{2,1,0:T(8,128)S(1)}, u32[]{:S(2)}, u32[]{:S(2)}) %collective-permute-start.2) | collective-permute-done | bytes 32800 | tf_op jit(solution)/shard_map/ppermute | solution.py:152
  18.5 3.0 %collective-permute-start.3 = (f32[1,64,128]{2,1,0:T(8,128)S(1)}, f32[1,64,128]{2,1,0:T(8,128)S(1)}, u32[]{:S(2)}, u32[]{:S(2)}) collective-permute-start(f32[1,64,128]{2,1,0:T(8,128)S(1)} %add.7.mine), channel_id=1, source_target_pairs={{0,8},{1,9},{2,10},{3,11},{4,12},{5,13},{6,14},{7,15},{8,0},{9,1},... | collective-permute-start | bytes 98312 | tf_op jit(solution)/shard_map/ppermute | solution.py:152
  21.6 1.9 %collective-permute-done.3.other = f32[1,64,128]{2,1,0:T(8,128)S(1)} collective-permute-done((f32[1,64,128]{2,1,0:T(8,128)S(1)}, f32[1,64,128]{2,1,0:T(8,128)S(1)}, u32[]{:S(2)}, u32[]{:S(2)}) %collective-permute-start.3) | collective-permute-done | bytes 32800 | tf_op jit(solution)/shard_map/ppermute | solution.py:152
  23.5 0.0 collective-permute-start.4
  23.5 1.2 %collective-permute-done.4.other = f32[1,64,128]{2,1,0:T(8,128)S(1)} collective-permute-done((f32[1,64,128]{2,1,0:T(8,128)S(1)}, f32[1,64,128]{2,1,0:T(8,128)S(1)}, u32[]{:S(2)}, u32[]{:S(2)}) %collective-permute-start.4) | collective-permute-done | bytes 32800 | tf_op jit(solution)/shard_map/ppermute | solution.py:147
  24.7 0.0 copy-done.4
  24.7 0.6 %score.1 = f32[16,2]{1,0:T(8,128)S(1)} custom-call(f32[1,64,128]{2,1,0:T(8,128)S(1)} %inverses.1.mine, f32[1,64,128]{2,1,0:T(8,128)S(1)} %collective-permute-done.4.other, bf16[16,4096]{1,0:T(8,128)(2,1)S(1)} %copy-done.4), custom_call_target="tpu_custom_call" | custom-call | tf_op jit(solution)/shard_map/score/pallas_call | solution.py:202
  25.3 0.6 %copy.7 = f32[16,2]{0,1:T(2,128)} copy(f32[16,2]{1,0:T(8,128)S(1)} %score.1) | data formatting | bytes 256 | tf_op jit(solution)/shard_map/score/pallas_call | solution.py:202
  (3 shorter events, 0.0 us)
Async XLA Ops:
  0.0 1.5 %copy-start = (bf16[128,7168]{1,0:T(8,128)(2,1)S(1)}, bf16[128,7168]{1,0:T(8,128)(2,1)}, u32[]{:S(2)}) copy-start(bf16[128,7168]{1,0:T(8,128)(2,1)} %inputs.1) | copy-start | bytes 5505028
  1.5 1.2 %copy-start.1 = (bf16[128,4096]{1,0:T(8,128)(2,1)S(1)}, bf16[128,4096]{1,0:T(8,128)(2,1)}, u32[]{:S(2)}) copy-start(bf16[128,4096]{1,0:T(8,128)(2,1)} %grads.1) | copy-start | bytes 3145732
  2.7 1.2 %copy-start.2 = (bf16[7168,64]{0,1:T(8,128)(2,1)S(1)}, bf16[7168,64]{0,1:T(8,128)(2,1)}, u32[]{:S(2)}) copy-start(bf16[7168,64]{0,1:T(8,128)(2,1)} %param.8) | copy-start | bytes 2752516
  3.9 1.0 %copy-start.3 = (bf16[4096,64]{0,1:T(8,128)(2,1)S(1)}, bf16[4096,64]{0,1:T(8,128)(2,1)}, u32[]{:S(2)}) copy-start(bf16[4096,64]{0,1:T(8,128)(2,1)} %param.9) | copy-start | bytes 1572868
  4.9 0.7 %copy-start.5 = (s32[2]{0:T(128)S(1)}, s32[2]{0:T(128)}, u32[]{:S(2)}) copy-start(s32[2]{0:T(128)} %lengths.1) | copy-start | bytes 28
  5.6 19.1 %copy-start.4 = (bf16[16,4096]{1,0:T(8,128)(2,1)S(1)}, bf16[16,4096]{1,0:T(8,128)(2,1)}, u32[]{:S(2)}) copy-start(bf16[16,4096]{1,0:T(8,128)(2,1)} %queries.1) | copy-start | bytes 393220
  8.0 1.4 %collective-permute-start = (f32[128,128]{1,0:T(8,128)S(1)}, f32[128,128]{1,0:T(8,128)S(1)}, u32[]{:S(2)}, u32[]{:S(2)}) collective-permute-start(f32[128,128]{1,0:T(8,128)S(1)} %project.1.mine), channel_id=1, source_target_pairs={{0,1},{1,0},{2,3},{3,2},{4,5},{5,4},{6,7},{7,6},{8,9},{9,8},{10,11... | collective-permute-start | bytes 196616 | tf_op jit(solution)/shard_map/ppermute | solution.py:147
  9.7 4.8 %collective-permute-start.1 = (f32[1,64,128]{2,1,0:T(8,128)S(1)}, f32[1,64,128]{2,1,0:T(8,128)S(1)}, u32[]{:S(2)}, u32[]{:S(2)}) collective-permute-start(f32[1,64,128]{2,1,0:T(8,128)S(1)} %moments.1), channel_id=1, source_target_pairs={{0,2},{1,3},{2,0},{3,1},{4,6},{5,7},{6,4},{7,5},{8,10},{9,11},{10,... | collective-permute-start | bytes 98312 | tf_op jit(solution)/shard_map/ppermute | solution.py:152
  14.5 4.0 %collective-permute-start.2 = (f32[1,64,128]{2,1,0:T(8,128)S(1)}, f32[1,64,128]{2,1,0:T(8,128)S(1)}, u32[]{:S(2)}, u32[]{:S(2)}) collective-permute-start(f32[1,64,128]{2,1,0:T(8,128)S(1)} %add.6), channel_id=1, source_target_pairs={{0,4},{1,5},{2,6},{3,7},{4,0},{5,1},{6,2},{7,3},{8,12},{9,13},{10,... | collective-permute-start | bytes 98312 | tf_op jit(solution)/shard_map/ppermute | solution.py:152
  18.5 4.9 %collective-permute-start.3 = (f32[1,64,128]{2,1,0:T(8,128)S(1)}, f32[1,64,128]{2,1,0:T(8,128)S(1)}, u32[]{:S(2)}, u32[]{:S(2)}) collective-permute-start(f32[1,64,128]{2,1,0:T(8,128)S(1)} %add.7.mine), channel_id=1, source_target_pairs={{0,8},{1,9},{2,10},{3,11},{4,12},{5,13},{6,14},{7,15},{8,0},{9,1},... | collective-permute-start | bytes 98312 | tf_op jit(solution)/shard_map/ppermute | solution.py:152
  23.5 1.2 %collective-permute-start.4 = (f32[1,64,128]{2,1,0:T(8,128)S(1)}, f32[1,64,128]{2,1,0:T(8,128)S(1)}, u32[]{:S(2)}, u32[]{:S(2)}) collective-permute-start(f32[1,64,128]{2,1,0:T(8,128)S(1)} %inverses.1.mine), channel_id=1, source_target_pairs={{0,1},{1,0},{2,3},{3,2},{4,5},{5,4},{6,7},{7,6},{8,9},{9,8},{10,11... | collective-permute-start | bytes 98312 | tf_op jit(solution)/shard_map/ppermute | solution.py:147

commit v2 on v1

--- a/solution.py
+++ b/solution.py
@@ -139,8 +139,16 @@
             for s in range(2):
                 sums[s] = sums[s] + block * flat[s][m : m + 1]
         for s in range(2):
-            if 2 * slab + s < out.shape[1]:
-                out[:, 2 * slab + s : 2 * slab + s + 1] = jnp.sum(sums[s], axis=1, keepdims=True)
+            if 2 * slab + s < out.shape[0]:
+                ones = jnp.ones((8, 2 * width), F32)
+                total = lax.dot_general(
+                    ones, sums[s], NT, preferred_element_type=F32, precision=lax.Precision.HIGHEST
+                )
+                out[2 * slab + s : 2 * slab + s + 1, :] = total[:1]
+
+
+def stay(array):
+    return pltpu.with_memory_space_constraint(array, pltpu.HBM)
 
 
 def swap(array):
@@ -174,7 +182,7 @@
         ],
         compiler_params=params,
         name="project",
-    )(lengths, inputs, out_grads, proj_in.T, proj_out.T)
+    )(*map(stay, (lengths, inputs, out_grads, proj_in.T, proj_out.T)))
     payload_shape = jax.ShapeDtypeStruct((slabs, width, 2 * width), F32)
     payload = pl.pallas_call(
         functools.partial(moments, tokens),
@@ -199,15 +207,16 @@
         name="inverses",
     )(payload, exchange(payload, distance, devices))
     scaling = 1.0 / (width * math.sqrt(LEN))
-    return pl.pallas_call(
+    scores = pl.pallas_call(
         functools.partial(score, scaling),
-        out_shape=jax.ShapeDtypeStruct((queries.shape[0], seq_count), F32),
+        out_shape=jax.ShapeDtypeStruct((seq_count, queries.shape[0]), F32),
         in_specs=[VMEM] * 3,
         out_specs=VMEM,
         scratch_shapes=[pltpu.VMEM((width, 2 * width), F32)],
         compiler_params=params,
         name="score",
     )(ready, swap(ready), queries)
+    return scores.T
 
 
 def solution(mesh):

time: 26.2 us -> 21.4 us (0.82)
  local copies, waits for them, and re-layouts: 6.24 us -> 0.01 us
  Pallas kernels: 3.33 us -> 4.89 us
    unnamed x12 -> x2, local copies, waits for them, and re-layouts: 5.6 us -> 0.01 us
    pallas_call x1, Pallas kernels: 2.37 us -> 3.26 us  [shards(): pl.pallas_call(functools.partial(project, chunks), out_shape=jax.ShapeDty...]
    pallas_call x1, Pallas kernels: 0.62 us -> 1.29 us  [shards(): pl.pallas_call(functools.partial(score, scaling), out_shape=jax.ShapeDtyp...]
    pallas_call x1 -> x0, local copies, waits for them, and re-layouts: 0.64 us -> none  [shards(): pl.pallas_call(functools.partial(score, scaling), out_shape=jax.ShapeDtyp...]
where the time goes in v2:
time: 21.4 us; the launch traced here: 21.3 us
  starting transfers between devices  8.57 us (40%)
  waiting for transfers between devices  7.78 us (36%)
  Pallas kernels  4.89 us (23%)
    ppermute x3, starting transfers between devices, exchange(): return lax.ppermute(array, ('seq', 'tensor'), pairs)  8.04 us
    ppermute x3, waiting for transfers between devices, exchange(): return lax.ppermute(array, ('seq', 'tensor'), pairs)  5.68 us
    pallas_call x1, Pallas kernels, shards(): pl.pallas_call(functools.partial(project, chunks), out_shape=jax.ShapeDty...  3.26 us
    ppermute x2, waiting for transfers between devices, swap(): return lax.ppermute(array, 'tensor', [(0, 1), (1, 0)])  2.1 us
    pallas_call x1, Pallas kernels, shards(): pl.pallas_call(functools.partial(score, scaling), out_shape=jax.ShapeDtyp...  1.29 us
    ppermute x2, starting transfers between devices, swap(): return lax.ppermute(array, 'tensor', [(0, 1), (1, 0)])  0.53 us
  transfers between devices with their start and end apart: 5, of which 5 were waited for; matrix products, arithmetic and copies ran while one was open for 0% of the time, Pallas kernels for 0%

profile of v2, /device:TPU:0, one launch (start us, length us, event | category | flops | bytes accessed | tf_op | source)
XLA Modules:
  0.0 21.3 jit_solution(14453185783062526415)
XLA Ops:
  0.0 0.0 copy-start
  0.0 3.3 %project.1.mine = f32[128,128]{1,0:T(8,128)S(1)} custom-call(s32[2]{0:T(128)} %lengths.1, bf16[128,7168]{1,0:T(8,128)(2,1)} %inputs.1, bf16[128,4096]{1,0:T(8,128)(2,1)} %grads.1, bf16[64,7168]{1,0:T(8,128)(2,1)} %bitcast.3, bf16[64,4096]{1,0:T(8,128)(2,1)} %bitcast.4), custom_call_target="tpu_custom_call" | custom-call | tf_op jit(solution)/shard_map/project/pallas_call | solution.py:170
  3.3 0.5 %collective-permute-start = (f32[128,128]{1,0:T(8,128)S(1)}, f32[128,128]{1,0:T(8,128)S(1)}, u32[]{:S(2)}, u32[]{:S(2)}) collective-permute-start(f32[128,128]{1,0:T(8,128)S(1)} %project.1.mine), channel_id=1, source_target_pairs={{0,1},{1,0},{2,3},{3,2},{4,5},{5,4},{6,7},{7,6},{8,9},{9,8},{10,11... | collective-permute-start | bytes 196616 | tf_op jit(solution)/shard_map/ppermute | solution.py:155
  3.8 0.9 %collective-permute-done.other = f32[128,128]{1,0:T(8,128)S(1)} collective-permute-done((f32[128,128]{1,0:T(8,128)S(1)}, f32[128,128]{1,0:T(8,128)S(1)}, u32[]{:S(2)}, u32[]{:S(2)}) %collective-permute-start) | collective-permute-done | bytes 65568 | tf_op jit(solution)/shard_map/ppermute | solution.py:155
  4.7 0.3 %moments.1 = f32[1,64,128]{2,1,0:T(8,128)S(1)} custom-call(f32[128,128]{1,0:T(8,128)S(1)} %project.1.mine, f32[128,128]{1,0:T(8,128)S(1)} %collective-permute-done.other), custom_call_target="tpu_custom_call" | custom-call | tf_op jit(solution)/shard_map/moments/pallas_call | solution.py:187
  5.0 2.9 %collective-permute-start.1 = (f32[1,64,128]{2,1,0:T(8,128)S(1)}, f32[1,64,128]{2,1,0:T(8,128)S(1)}, u32[]{:S(2)}, u32[]{:S(2)}) collective-permute-start(f32[1,64,128]{2,1,0:T(8,128)S(1)} %moments.1), channel_id=1, source_target_pairs={{0,2},{1,3},{2,0},{3,1},{4,6},{5,7},{6,4},{7,5},{8,10},{9,11},{10,... | collective-permute-start | bytes 98312 | tf_op jit(solution)/shard_map/ppermute | solution.py:160
  7.9 1.9 %collective-permute-done.1 = f32[1,64,128]{2,1,0:T(8,128)S(1)} collective-permute-done((f32[1,64,128]{2,1,0:T(8,128)S(1)}, f32[1,64,128]{2,1,0:T(8,128)S(1)}, u32[]{:S(2)}, u32[]{:S(2)}) %collective-permute-start.1) | collective-permute-done | bytes 32800 | tf_op jit(solution)/shard_map/ppermute | solution.py:160
  9.8 2.1 %collective-permute-start.2 = (f32[1,64,128]{2,1,0:T(8,128)S(1)}, f32[1,64,128]{2,1,0:T(8,128)S(1)}, u32[]{:S(2)}, u32[]{:S(2)}) collective-permute-start(f32[1,64,128]{2,1,0:T(8,128)S(1)} %add.6), channel_id=1, source_target_pairs={{0,4},{1,5},{2,6},{3,7},{4,0},{5,1},{6,2},{7,3},{8,12},{9,13},{10,... | collective-permute-start | bytes 98312 | tf_op jit(solution)/shard_map/ppermute | solution.py:160
  11.9 1.9 %collective-permute-done.2 = f32[1,64,128]{2,1,0:T(8,128)S(1)} collective-permute-done((f32[1,64,128]{2,1,0:T(8,128)S(1)}, f32[1,64,128]{2,1,0:T(8,128)S(1)}, u32[]{:S(2)}, u32[]{:S(2)}) %collective-permute-start.2) | collective-permute-done | bytes 32800 | tf_op jit(solution)/shard_map/ppermute | solution.py:160
  13.8 3.0 %collective-permute-start.3 = (f32[1,64,128]{2,1,0:T(8,128)S(1)}, f32[1,64,128]{2,1,0:T(8,128)S(1)}, u32[]{:S(2)}, u32[]{:S(2)}) collective-permute-start(f32[1,64,128]{2,1,0:T(8,128)S(1)} %add.7.mine), channel_id=1, source_target_pairs={{0,8},{1,9},{2,10},{3,11},{4,12},{5,13},{6,14},{7,15},{8,0},{9,1},... | collective-permute-start | bytes 98312 | tf_op jit(solution)/shard_map/ppermute | solution.py:160
  16.9 1.9 %collective-permute-done.3.other = f32[1,64,128]{2,1,0:T(8,128)S(1)} collective-permute-done((f32[1,64,128]{2,1,0:T(8,128)S(1)}, f32[1,64,128]{2,1,0:T(8,128)S(1)}, u32[]{:S(2)}, u32[]{:S(2)}) %collective-permute-start.3) | collective-permute-done | bytes 32800 | tf_op jit(solution)/shard_map/ppermute | solution.py:160
  18.8 0.0 collective-permute-start.4
  18.8 1.2 %collective-permute-done.4.other = f32[1,64,128]{2,1,0:T(8,128)S(1)} collective-permute-done((f32[1,64,128]{2,1,0:T(8,128)S(1)}, f32[1,64,128]{2,1,0:T(8,128)S(1)}, u32[]{:S(2)}, u32[]{:S(2)}) %collective-permute-start.4) | collective-permute-done | bytes 32800 | tf_op jit(solution)/shard_map/ppermute | solution.py:155
  20.0 0.0 copy-done
  20.0 1.3 %score.1 = f32[2,16]{1,0:T(2,128)} custom-call(f32[1,64,128]{2,1,0:T(8,128)S(1)} %inverses.1.mine, f32[1,64,128]{2,1,0:T(8,128)S(1)} %collective-permute-done.4.other, bf16[16,4096]{1,0:T(8,128)(2,1)S(1)} %copy-done), custom_call_target="tpu_custom_call" | custom-call | tf_op jit(solution)/shard_map/score/pallas_call | solution.py:210
  (3 shorter events, 0.0 us)
Async XLA Ops:
  0.0 20.0 %copy-start = (bf16[16,4096]{1,0:T(8,128)(2,1)S(1)}, bf16[16,4096]{1,0:T(8,128)(2,1)}, u32[]{:S(2)}) copy-start(bf16[16,4096]{1,0:T(8,128)(2,1)} %queries.1) | copy-start | bytes 393220
  3.3 1.4 %collective-permute-start = (f32[128,128]{1,0:T(8,128)S(1)}, f32[128,128]{1,0:T(8,128)S(1)}, u32[]{:S(2)}, u32[]{:S(2)}) collective-permute-start(f32[128,128]{1,0:T(8,128)S(1)} %project.1.mine), channel_id=1, source_target_pairs={{0,1},{1,0},{2,3},{3,2},{4,5},{5,4},{6,7},{7,6},{8,9},{9,8},{10,11... | collective-permute-start | bytes 196616 | tf_op jit(solution)/shard_map/ppermute | solution.py:155
  5.0 4.8 %collective-permute-start.1 = (f32[1,64,128]{2,1,0:T(8,128)S(1)}, f32[1,64,128]{2,1,0:T(8,128)S(1)}, u32[]{:S(2)}, u32[]{:S(2)}) collective-permute-start(f32[1,64,128]{2,1,0:T(8,128)S(1)} %moments.1), channel_id=1, source_target_pairs={{0,2},{1,3},{2,0},{3,1},{4,6},{5,7},{6,4},{7,5},{8,10},{9,11},{10,... | collective-permute-start | bytes 98312 | tf_op jit(solution)/shard_map/ppermute | solution.py:160
  9.8 4.0 %collective-permute-start.2 = (f32[1,64,128]{2,1,0:T(8,128)S(1)}, f32[1,64,128]{2,1,0:T(8,128)S(1)}, u32[]{:S(2)}, u32[]{:S(2)}) collective-permute-start(f32[1,64,128]{2,1,0:T(8,128)S(1)} %add.6), channel_id=1, source_target_pairs={{0,4},{1,5},{2,6},{3,7},{4,0},{5,1},{6,2},{7,3},{8,12},{9,13},{10,... | collective-permute-start | bytes 98312 | tf_op jit(solution)/shard_map/ppermute | solution.py:160
  13.8 4.9 %collective-permute-start.3 = (f32[1,64,128]{2,1,0:T(8,128)S(1)}, f32[1,64,128]{2,1,0:T(8,128)S(1)}, u32[]{:S(2)}, u32[]{:S(2)}) collective-permute-start(f32[1,64,128]{2,1,0:T(8,128)S(1)} %add.7.mine), channel_id=1, source_target_pairs={{0,8},{1,9},{2,10},{3,11},{4,12},{5,13},{6,14},{7,15},{8,0},{9,1},... | collective-permute-start | bytes 98312 | tf_op jit(solution)/shard_map/ppermute | solution.py:160
  18.8 1.2 %collective-permute-start.4 = (f32[1,64,128]{2,1,0:T(8,128)S(1)}, f32[1,64,128]{2,1,0:T(8,128)S(1)}, u32[]{:S(2)}, u32[]{:S(2)}) collective-permute-start(f32[1,64,128]{2,1,0:T(8,128)S(1)} %inverses.1.mine), channel_id=1, source_target_pairs={{0,1},{1,0},{2,3},{3,2},{4,5},{5,4},{6,7},{7,6},{8,9},{9,8},{10,11... | collective-permute-start | bytes 98312 | tf_op jit(solution)/shard_map/ppermute | solution.py:155

commit v3 on v2

v3 whole, which is shorter than its diff:
```python
import functools
import math

import jax
import jax.numpy as jnp
from jax import lax
from jax.experimental import pallas as pl
from jax.experimental.pallas import tpu as pltpu
from jax.sharding import PartitionSpec as P

LEN = 512
DAMPING = 0.1
VMEM = pl.BlockSpec(memory_space=pltpu.VMEM)
HBM = pl.BlockSpec(memory_space=pltpu.HBM)
NT = (((1,), (1,)), ((), ()))
F32 = jnp.float32


def project(chunks, lengths, inputs, grads, proj_in, proj_out, out, *scratch):
    x_buf, g_buf, px_buf, pg_buf, count, sems = scratch
    width, tokens = px_buf.shape[0], x_buf.shape[0]
    jobs, sem = [], 0
    for rows, row_buf, mat, mat_buf, parts, lo in (
        (inputs, x_buf, proj_in, px_buf, chunks[0], 0),
        (grads, g_buf, proj_out, pg_buf, chunks[1], width),
    ):
        step = rows.shape[1] // parts
        for part in range(parts):
            cols = pl.ds(part * step, step)
            pair = []
            for src, dst in ((mat, mat_buf), (rows, row_buf)):
                pair.append(pltpu.make_async_copy(src.at[:, cols], dst.at[:, cols], sems.at[sem]))
                pair[-1].start()
                sem += 1
            jobs.append((pair, mat_buf, row_buf, cols, lo))
    scalars = pltpu.make_async_copy(lengths, count, sems.at[sem])
    scalars.start()
    totals = {}
    for pair, mat_buf, row_buf, cols, lo in jobs:
        for copy in pair:
            copy.wait()
        part = lax.dot_general(mat_buf[:, cols], row_buf[:, cols], NT, preferred_element_type=F32)
        totals[lo] = part if lo not in totals else totals[lo] + part
    scalars.wait()
    first = lax.axis_index("seq") * tokens
    valid = lax.broadcasted_iota(jnp.int32, (width, tokens), 1) + first % LEN < count[first // LEN]
    for lo, total in totals.items():
        out[lo : lo + width, :] = jnp.where(valid, total, 0.0)


def moments(mine, other, out):
    out[...] = jnp.zeros_like(out)

    @pl.when(lax.axis_index("tensor") == 1)
    def _():
        z = mine[...] + other[...]
        square = lax.dot_general(z, z, NT, preferred_element_type=F32, precision=lax.Precision.HIGHEST)
        width = square.shape[0] // 2
        top, bottom = square[:width], pltpu.roll(square[width:], width, 1)
        row = lax.broadcasted_iota(jnp.int32, top.shape, 0)
        lane = lax.broadcasted_iota(jnp.int32, top.shape, 1)
        out[0, :width] = jnp.where(lane < row, bottom, top)
        diagonal = jnp.sum(jnp.where(lane == row, bottom, 0.0), axis=0, keepdims=True)
        out[0, width : width + 1] = diagonal


def unpack(packed, diagonal):
    width = packed.shape[0]
    left = packed[:, :width]
    flipped = left.T
    row = lax.broadcasted_iota(jnp.int32, left.shape, 0)
    lane = lax.broadcasted_iota(jnp.int32, left.shape, 1)
    inner = jnp.where(lane < row, flipped, left)
    outer = jnp.where(lane < row, left, jnp.where(lane == row, diagonal[:, :width], flipped))
    return jnp.concatenate([inner, outer], axis=1)


def invert(matrix):
    width = matrix.shape[0]
    blocks = width // 8
    lane = lax.broadcasted_iota(jnp.int32, (8, 2 * width), 1)
    row_of = lax.broadcasted_iota(jnp.int32, (8, 2 * width), 0)
    column = lane % width
    right = lane - column
    rows = [matrix[8 * b : 8 * b + 8] for b in range(blocks)]
    for panel in range(blocks):
        first = 8 * panel
        cols = []
        for t in range(8):
            index = right + (first + t)
            cols.append([jnp.take_along_axis(rows[b], index, axis=1) for b in range(blocks)])
        inside = (column >= first) & (column < first + 8)
        rows = [jnp.where(inside, 0.0, r) for r in rows]
        for t in range(8):
            unit = jnp.where(column[:1] == first + t, 1.0, 0.0)
            inverse = 1.0 / cols[t][panel][t : t + 1]
            pivot = (rows[panel][t : t + 1] + unit) * inverse
            for b in range(blocks):
                rows[b] = rows[b] - cols[t][b] * pivot
            rows[panel] = jnp.where(row_of == t, pivot, rows[panel])
            for j in range(t + 1, 8):
                scaled = cols[j][panel][t : t + 1] * inverse
                cols[j] = [cols[j][b] - cols[t][b] * scaled for b in range(blocks)]
                cols[j][panel] = jnp.where(row_of == t, scaled, cols[j][panel])
    return jnp.concatenate(rows, axis=0)


def weigh(total, scaling, mine, other, out, rows):
    out[...] = jnp.zeros_like(out)

    @pl.when(lax.axis_index("tensor") == 1)
    def _():
        slabs, _, lanes = mine.shape
        width = lanes // 2
        packed = mine[0] + other[0]
        both = unpack(packed[:width], packed[width : width + 1])
        lane = lax.broadcasted_iota(jnp.int32, both.shape, 1)
        row = lax.broadcasted_iota(jnp.int32, both.shape, 0)
        inv = invert(both * (1.0 / total) + jnp.where(lane % width == row, DAMPING, 0.0))
        inv_in, inv_out = inv[:, :width], jnp.where(lane < width, 0.0, inv)
        exact = dict(preferred_element_type=F32, precision=lax.Precision.HIGHEST)
        devices = lax.axis_size("seq")
        upper = lax.axis_index("seq") // (devices // 2) == 1
        for slab in range(slabs):
            for high in (False, True):
                cross = jnp.where(upper == high, mine[slab, :width], other[slab, :width])
                part = lax.dot_general(inv_out, cross, NT, **exact)
                rows[...] = jnp.dot(part, inv_in, **exact) * scaling
                even, odd = rows[pl.ds(0, width // 2, 2), :], rows[pl.ds(1, width // 2, 2), :]
                out[slabs * high + slab] = jnp.concatenate([even, odd], axis=1)


def score(mine, other, queries, out):
    is_weight = lax.axis_index("tensor") == 1
    count, chunks, lanes = mine.shape
    ones = jnp.ones((8, lanes), F32)
    for s in range(count):
        weights = jnp.where(is_weight, mine[s], other[s])
        sums = jnp.zeros((queries.shape[0], lanes), F32)
        for m in range(chunks):
            sums = sums + queries[:, lanes * m : lanes * (m + 1)].astype(F32) * weights[m : m + 1]
        total = lax.dot_general(ones, sums, NT, preferred_element_type=F32, precision=lax.Precision.HIGHEST)
        out[s : s + 1, :] = total[:1]


def stay(array):
    return pltpu.with_memory_space_constraint(array, pltpu.HBM)


def swap(array):
    return lax.ppermute(array, "tensor", [(0, 1), (1, 0)])


def exchange(array, distance, groups, devices):
    near = 2 if distance == 1 else 1
    pairs = []
    for chip in range(groups * devices):
        pairs.append((2 * chip, 2 * (chip ^ near)))
        pairs.append((2 * chip + 1, 2 * (chip ^ distance) + 1))
    return lax.ppermute(array, ("groups", "seq", "tensor"), pairs)


def gather(mine, other, distance, width):
    high = lax.axis_index("seq") // distance % 2 == 1
    both = jnp.stack([jnp.where(high, other, mine), jnp.where(high, mine, other)])
    left = jnp.arange(mine.shape[-1]) < width
    return jnp.where(left, mine + other, both).reshape((-1,) + mine.shape[1:])


def shards(inputs, out_grads, proj_in, proj_out, queries, lengths):
    width = proj_in.shape[1]
    tokens = inputs.shape[0]
    seq_count = lengths.shape[0]
    chunks = (4, 2)
    params = pltpu.CompilerParams(vmem_limit_bytes=16 << 20)
    partial_z = pl.pallas_call(
        functools.partial(project, chunks),
        out_shape=jax.ShapeDtypeStruct((2 * width, tokens), F32),
        in_specs=[HBM] * 5,
        out_specs=VMEM,
        scratch_shapes=[
            pltpu.VMEM(inputs.shape, inputs.dtype),
            pltpu.VMEM(out_grads.shape, out_grads.dtype),
            pltpu.VMEM(proj_in.shape[::-1], proj_in.dtype),
            pltpu.VMEM(proj_out.shape[::-1], proj_out.dtype),
            pltpu.SMEM(lengths.shape, lengths.dtype),
            pltpu.SemaphoreType.DMA((2 * sum(chunks) + 1,)),
        ],
        compiler_params=params,
        name="project",
    )(*map(stay, (lengths, inputs, out_grads, proj_in.T, proj_out.T)))
    packed_rows = width + 8
    packed = pl.pallas_call(
        moments,
        out_shape=jax.ShapeDtypeStruct((1, packed_rows, 2 * width), F32),
        in_specs=[VMEM] * 2,
        out_specs=VMEM,
        compiler_params=params,
        name="moments",
    )(partial_z, swap(partial_z))
    groups, devices = lax.axis_size("groups"), lax.axis_size("seq")
    holders = devices // seq_count
    distance = 1
    while 2 * distance < devices:
        other = exchange(packed, distance, groups, devices)
        packed = packed + other if distance < holders else gather(packed, other, distance, width)
        distance *= 2
    total = 3 * seq_count * LEN // 4
    scaling = 1.0 / (width * math.sqrt(LEN))
    weights = pl.pallas_call(
        functools.partial(weigh, float(total), scaling),
        out_shape=jax.ShapeDtypeStruct((seq_count, width // 2, 2 * width), F32),
        in_specs=[VMEM] * 2,
        out_specs=VMEM,
        scratch_shapes=[pltpu.VMEM((width, width), F32)],
        compiler_params=params,
        name="weigh",
    )(packed, exchange(packed, distance, groups, devices))
    scores = pl.pallas_call(
        score,
        out_shape=jax.ShapeDtypeStruct((seq_count, queries.shape[0]), F32),
        in_specs=[VMEM] * 3,
        out_specs=VMEM,
        compiler_params=params,
        name="score",
    )(weights, swap(weights), queries)
    return scores.T


def solution(mesh):
    placed = (
        P(("groups", "seq"), "tensor"),
        P(("groups", "seq"), "tensor"),
        P("tensor", None),
        P("tensor", None),
        P(("groups", "seq", "tensor"), None),
        P("groups"),
    )
    return jax.shard_map(
        shards,
        mesh=mesh,
        in_specs=placed,
        out_specs=P(("groups", "seq", "tensor"), None),
        check_vma=False,
    )
```

time: 21.4 us -> 20.9 us (0.977)
  Pallas kernels: 4.89 us -> 4.04 us
  starting transfers between devices: 8.57 us -> 8.93 us
    ppermute x2, starting transfers between devices: 0.53 us -> 2.12 us  [swap(): return lax.ppermute(array, 'tensor', [(0, 1), (1, 0)])]
    ppermute x3, starting transfers between devices: 8.04 us -> 6.8 us  [exchange(): return lax.ppermute(array, ('groups', 'seq', 'tensor'), pairs)]
    pallas_call x3, Pallas kernels: 1.63 us -> 0.78 us  [the longest x1 0.78 us: shards(): pl.pallas_call(score, out_shape=jax.ShapeDtypeStruct((seq_count, queries....]
    ppermute x2, waiting for transfers between devices: 2.1 us -> 1.76 us  [swap(): return lax.ppermute(array, 'tensor', [(0, 1), (1, 0)])]
    ppermute x3, waiting for transfers between devices: 5.68 us -> 5.97 us  [exchange(): return lax.ppermute(array, ('groups', 'seq', 'tensor'), pairs)]
where the time goes in v3:
time: 20.9 us; the launch traced here: 20.7 us
  starting transfers between devices  8.93 us (43%)
  waiting for transfers between devices  7.73 us (37%)
  Pallas kernels  4.04 us (19%)
    ppermute x3, starting transfers between devices, exchange(): return lax.ppermute(array, ('groups', 'seq', 'tensor'), pairs)  6.8 us
    ppermute x3, waiting for transfers between devices, exchange(): return lax.ppermute(array, ('groups', 'seq', 'tensor'), pairs)  5.97 us
    pallas_call x1, Pallas kernels, shards(): pl.pallas_call(functools.partial(project, chunks), out_shape=jax.ShapeDty...  3.26 us
    ppermute x2, starting transfers between devices, swap(): return lax.ppermute(array, 'tensor', [(0, 1), (1, 0)])  2.12 us
    ppermute x2, waiting for transfers between devices, swap(): return lax.ppermute(array, 'tensor', [(0, 1), (1, 0)])  1.76 us
    pallas_call x1, Pallas kernels, shards(): pl.pallas_call(score, out_shape=jax.ShapeDtypeStruct((seq_count, queries....  0.78 us
  transfers between devices with their start and end apart: 5, of which 5 were waited for; matrix products, arithmetic and copies ran while one was open for 0% of the time, Pallas kernels for 0%

profile of v3, /device:TPU:0, one launch (start us, length us, event | category | flops | bytes accessed | tf_op | source)
XLA Modules:
  0.0 20.7 jit_solution(12493124855460816830)
XLA Ops:
  0.0 0.0 copy-start
  0.0 3.3 %project.1.mine = f32[128,128]{1,0:T(8,128)S(1)} custom-call(s32[2]{0:T(128)} %lengths.1, bf16[128,7168]{1,0:T(8,128)(2,1)} %inputs.1, bf16[128,4096]{1,0:T(8,128)(2,1)} %grads.1, bf16[64,7168]{1,0:T(8,128)(2,1)} %bitcast.3, bf16[64,4096]{1,0:T(8,128)(2,1)} %bitcast.4), custom_call_target="tpu_custom_call" | custom-call | tf_op jit(solution)/shard_map/project/pallas_call | solution.py:176
  3.3 0.5 %collective-permute-start = (f32[128,128]{1,0:T(8,128)S(1)}, f32[128,128]{1,0:T(8,128)S(1)}, u32[]{:S(2)}, u32[]{:S(2)}) collective-permute-start(f32[128,128]{1,0:T(8,128)S(1)} %project.1.mine), channel_id=1, source_target_pairs={{0,1},{1,0},{2,3},{3,2},{4,5},{5,4},{6,7},{7,6},{8,9},{9,8},{10,11... | collective-permute-start | bytes 196616 | tf_op jit(solution)/shard_map/ppermute | solution.py:151
  3.8 0.9 %collective-permute-done.other = f32[128,128]{1,0:T(8,128)S(1)} collective-permute-done((f32[128,128]{1,0:T(8,128)S(1)}, f32[128,128]{1,0:T(8,128)S(1)}, u32[]{:S(2)}, u32[]{:S(2)}) %collective-permute-start) | collective-permute-done | bytes 65568 | tf_op jit(solution)/shard_map/ppermute | solution.py:151
  4.7 2.9 %collective-permute-start.1 = (f32[1,72,128]{2,1,0:T(8,128)S(1)}, f32[1,72,128]{2,1,0:T(8,128)S(1)}, u32[]{:S(2)}, u32[]{:S(2)}) collective-permute-start(f32[1,72,128]{2,1,0:T(8,128)S(1)} %moments.1), channel_id=1, source_target_pairs={{0,4},{1,3},{2,6},{3,1},{4,0},{5,7},{6,2},{7,5},{8,12},{9,11},{10,... | collective-permute-start | bytes 110600 | tf_op jit(solution)/shard_map/ppermute | solution.py:160
  7.6 1.9 %collective-permute-done.1 = f32[1,72,128]{2,1,0:T(8,128)S(1)} collective-permute-done((f32[1,72,128]{2,1,0:T(8,128)S(1)}, f32[1,72,128]{2,1,0:T(8,128)S(1)}, u32[]{:S(2)}, u32[]{:S(2)}) %collective-permute-start.1) | collective-permute-done | bytes 36896 | tf_op jit(solution)/shard_map/ppermute | solution.py:160
  9.6 1.9 %collective-permute-start.2 = (f32[1,72,128]{2,1,0:T(8,128)S(1)}, f32[1,72,128]{2,1,0:T(8,128)S(1)}, u32[]{:S(2)}, u32[]{:S(2)}) collective-permute-start(f32[1,72,128]{2,1,0:T(8,128)S(1)} %add.6), channel_id=1, source_target_pairs={{0,2},{1,5},{2,0},{3,7},{4,6},{5,1},{6,4},{7,3},{8,10},{9,13},{10,... | collective-permute-start | bytes 110600 | tf_op jit(solution)/shard_map/ppermute | solution.py:160
  11.5 2.0 %collective-permute-done.2 = f32[1,72,128]{2,1,0:T(8,128)S(1)} collective-permute-done((f32[1,72,128]{2,1,0:T(8,128)S(1)}, f32[1,72,128]{2,1,0:T(8,128)S(1)}, u32[]{:S(2)}, u32[]{:S(2)}) %collective-permute-start.2) | collective-permute-done | bytes 36896 | tf_op jit(solution)/shard_map/ppermute | solution.py:160
  13.5 1.9 %collective-permute-start.3 = (f32[1,72,128]{2,1,0:T(8,128)S(1)}, f32[1,72,128]{2,1,0:T(8,128)S(1)}, u32[]{:S(2)}, u32[]{:S(2)}) collective-permute-start(f32[1,72,128]{2,1,0:T(8,128)S(1)} %add.7.mine), channel_id=1, source_target_pairs={{0,2},{1,9},{2,0},{3,11},{4,6},{5,13},{6,4},{7,15},{8,10},{9,1},{1... | collective-permute-start | bytes 110600 | tf_op jit(solution)/shard_map/ppermute | solution.py:160
  15.5 2.0 %collective-permute-done.3.other = f32[1,72,128]{2,1,0:T(8,128)S(1)} collective-permute-done((f32[1,72,128]{2,1,0:T(8,128)S(1)}, f32[1,72,128]{2,1,0:T(8,128)S(1)}, u32[]{:S(2)}, u32[]{:S(2)}) %collective-permute-start.3) | collective-permute-done | bytes 36896 | tf_op jit(solution)/shard_map/ppermute | solution.py:160
  17.5 1.6 %collective-permute-start.4 = (f32[2,32,128]{2,1,0:T(8,128)S(1)}, f32[2,32,128]{2,1,0:T(8,128)S(1)}, u32[]{:S(2)}, u32[]{:S(2)}) collective-permute-start(f32[2,32,128]{2,1,0:T(8,128)S(1)} %weigh.1.mine), channel_id=1, source_target_pairs={{0,1},{1,0},{2,3},{3,2},{4,5},{5,4},{6,7},{7,6},{8,9},{9,8},{10,11... | collective-permute-start | bytes 98312 | tf_op jit(solution)/shard_map/ppermute | solution.py:151
  19.1 0.9 %collective-permute-done.4.other = f32[2,32,128]{2,1,0:T(8,128)S(1)} collective-permute-done((f32[2,32,128]{2,1,0:T(8,128)S(1)}, f32[2,32,128]{2,1,0:T(8,128)S(1)}, u32[]{:S(2)}, u32[]{:S(2)}) %collective-permute-start.4) | collective-permute-done | bytes 32800 | tf_op jit(solution)/shard_map/ppermute | solution.py:151
  20.0 0.0 copy-done
  20.0 0.8 %score.1 = f32[2,16]{1,0:T(2,128)} custom-call(f32[2,32,128]{2,1,0:T(8,128)S(1)} %weigh.1.mine, f32[2,32,128]{2,1,0:T(8,128)S(1)} %collective-permute-done.4.other, bf16[16,4096]{1,0:T(8,128)(2,1)S(1)} %copy-done), custom_call_target="tpu_custom_call" | custom-call | tf_op jit(solution)/shard_map/score/pallas_call | solution.py:219
  (4 shorter events, 0.0 us)
Async XLA Ops:
  0.0 20.0 %copy-start = (bf16[16,4096]{1,0:T(8,128)(2,1)S(1)}, bf16[16,4096]{1,0:T(8,128)(2,1)}, u32[]{:S(2)}) copy-start(bf16[16,4096]{1,0:T(8,128)(2,1)} %queries.1) | copy-start | bytes 393220
  3.3 1.4 %collective-permute-start = (f32[128,128]{1,0:T(8,128)S(1)}, f32[128,128]{1,0:T(8,128)S(1)}, u32[]{:S(2)}, u32[]{:S(2)}) collective-permute-start(f32[128,128]{1,0:T(8,128)S(1)} %project.1.mine), channel_id=1, source_target_pairs={{0,1},{1,0},{2,3},{3,2},{4,5},{5,4},{6,7},{7,6},{8,9},{9,8},{10,11... | collective-permute-start | bytes 196616 | tf_op jit(solution)/shard_map/ppermute | solution.py:151
  4.7 4.9 %collective-permute-start.1 = (f32[1,72,128]{2,1,0:T(8,128)S(1)}, f32[1,72,128]{2,1,0:T(8,128)S(1)}, u32[]{:S(2)}, u32[]{:S(2)}) collective-permute-start(f32[1,72,128]{2,1,0:T(8,128)S(1)} %moments.1), channel_id=1, source_target_pairs={{0,4},{1,3},{2,6},{3,1},{4,0},{5,7},{6,2},{7,5},{8,12},{9,11},{10,... | collective-permute-start | bytes 110600 | tf_op jit(solution)/shard_map/ppermute | solution.py:160
  9.6 4.0 %collective-permute-start.2 = (f32[1,72,128]{2,1,0:T(8,128)S(1)}, f32[1,72,128]{2,1,0:T(8,128)S(1)}, u32[]{:S(2)}, u32[]{:S(2)}) collective-permute-start(f32[1,72,128]{2,1,0:T(8,128)S(1)} %add.6), channel_id=1, source_target_pairs={{0,2},{1,5},{2,0},{3,7},{4,6},{5,1},{6,4},{7,3},{8,10},{9,13},{10,... | collective-permute-start | bytes 110600 | tf_op jit(solution)/shard_map/ppermute | solution.py:160
  13.5 4.0 %collective-permute-start.3 = (f32[1,72,128]{2,1,0:T(8,128)S(1)}, f32[1,72,128]{2,1,0:T(8,128)S(1)}, u32[]{:S(2)}, u32[]{:S(2)}) collective-permute-start(f32[1,72,128]{2,1,0:T(8,128)S(1)} %add.7.mine), channel_id=1, source_target_pairs={{0,2},{1,9},{2,0},{3,11},{4,6},{5,13},{6,4},{7,15},{8,10},{9,1},{1... | collective-permute-start | bytes 110600 | tf_op jit(solution)/shard_map/ppermute | solution.py:160
  17.5 2.5 %collective-permute-start.4 = (f32[2,32,128]{2,1,0:T(8,128)S(1)}, f32[2,32,128]{2,1,0:T(8,128)S(1)}, u32[]{:S(2)}, u32[]{:S(2)}) collective-permute-start(f32[2,32,128]{2,1,0:T(8,128)S(1)} %weigh.1.mine), channel_id=1, source_target_pairs={{0,1},{1,0},{2,3},{3,2},{4,5},{5,4},{6,7},{7,6},{8,9},{9,8},{10,11... | collective-permute-start | bytes 98312 | tf_op jit(solution)/shard_map/ppermute | solution.py:151

commit v4 on v3

--- a/solution.py
+++ b/solution.py
@@ -12,6 +12,7 @@
 DAMPING = 0.1
 VMEM = pl.BlockSpec(memory_space=pltpu.VMEM)
 HBM = pl.BlockSpec(memory_space=pltpu.HBM)
+NN = (((1,), (0,)), ((), ()))
 NT = (((1,), (1,)), ((), ()))
 F32 = jnp.float32
 
@@ -48,13 +49,23 @@
         out[lo : lo + width, :] = jnp.where(valid, total, 0.0)
 
 
+def dot3(a, b, dims):
+    halves = []
+    for part in (a, b):
+        high = part.astype(jnp.bfloat16)
+        halves.append((high, (part - high.astype(F32)).astype(jnp.bfloat16)))
+    (ah, al), (bh, bl) = halves
+    dot = functools.partial(lax.dot_general, dimension_numbers=dims, preferred_element_type=F32)
+    return dot(ah, bh) + (dot(ah, bl) + dot(al, bh))
+
+
 def moments(mine, other, out):
     out[...] = jnp.zeros_like(out)
 
     @pl.when(lax.axis_index("tensor") == 1)
     def _():
         z = mine[...] + other[...]
-        square = lax.dot_general(z, z, NT, preferred_element_type=F32, precision=lax.Precision.HIGHEST)
+        square = dot3(z, z, NT)
         width = square.shape[0] // 2
         top, bottom = square[:width], pltpu.roll(square[width:], width, 1)
         row = lax.broadcasted_iota(jnp.int32, top.shape, 0)
@@ -75,59 +86,75 @@
     return jnp.concatenate([inner, outer], axis=1)
 
 
-def invert(matrix):
-    width = matrix.shape[0]
+def invert(state):
+    width = state.shape[0]
     blocks = width // 8
     lane = lax.broadcasted_iota(jnp.int32, (8, 2 * width), 1)
     row_of = lax.broadcasted_iota(jnp.int32, (8, 2 * width), 0)
     column = lane % width
     right = lane - column
-    rows = [matrix[8 * b : 8 * b + 8] for b in range(blocks)]
-    for panel in range(blocks):
-        first = 8 * panel
-        cols = []
-        for t in range(8):
-            index = right + (first + t)
-            cols.append([jnp.take_along_axis(rows[b], index, axis=1) for b in range(blocks)])
+
+    def panel(step, carry):
+        first = step * 8
+        own = pl.ds(pl.multiple_of(first, 8), 8)
         inside = (column >= first) & (column < first + 8)
+        index = [right + (first + t) for t in range(8)]
+        rows = [state[8 * b : 8 * b + 8, :] for b in range(blocks)]
+        pivots = state[own, :]
+        heads = [jnp.take_along_axis(pivots, index[t], axis=1) for t in range(8)]
+        cols = [[jnp.take_along_axis(r, index[t], axis=1) for r in rows] for t in range(8)]
+        pivots = jnp.where(inside, jnp.where(column - first == row_of, 1.0, 0.0), pivots)
         rows = [jnp.where(inside, 0.0, r) for r in rows]
         for t in range(8):
-            unit = jnp.where(column[:1] == first + t, 1.0, 0.0)
-            inverse = 1.0 / cols[t][panel][t : t + 1]
-            pivot = (rows[panel][t : t + 1] + unit) * inverse
-            for b in range(blocks):
-                rows[b] = rows[b] - cols[t][b] * pivot
-            rows[panel] = jnp.where(row_of == t, pivot, rows[panel])
+            inverse = 1.0 / heads[t][t : t + 1]
+            pivot = pivots[t : t + 1] * inverse
+            here = row_of == t
+            pivots = jnp.where(here, pivot, pivots - jnp.where(here, 0.0, heads[t]) * pivot)
+            rows = [rows[b] - cols[t][b] * pivot for b in range(blocks)]
             for j in range(t + 1, 8):
-                scaled = cols[j][panel][t : t + 1] * inverse
+                scaled = heads[j][t : t + 1] * inverse
+                heads[j] = jnp.where(here, scaled, heads[j] - heads[t] * scaled)
                 cols[j] = [cols[j][b] - cols[t][b] * scaled for b in range(blocks)]
-                cols[j][panel] = jnp.where(row_of == t, scaled, cols[j][panel])
-    return jnp.concatenate(rows, axis=0)
-
-
-def weigh(total, scaling, mine, other, out, rows):
-    out[...] = jnp.zeros_like(out)
-
+        for b in range(blocks):
+            state[8 * b : 8 * b + 8, :] = rows[b]
+        state[own, :] = pivots
+        return carry
+
+    lax.fori_loop(0, blocks, panel, 0)
+
+
+def inverses(total, mine, other, out):
     @pl.when(lax.axis_index("tensor") == 1)
     def _():
-        slabs, _, lanes = mine.shape
-        width = lanes // 2
+        width = out.shape[0]
         packed = mine[0] + other[0]
         both = unpack(packed[:width], packed[width : width + 1])
         lane = lax.broadcasted_iota(jnp.int32, both.shape, 1)
         row = lax.broadcasted_iota(jnp.int32, both.shape, 0)
-        inv = invert(both * (1.0 / total) + jnp.where(lane % width == row, DAMPING, 0.0))
-        inv_in, inv_out = inv[:, :width], jnp.where(lane < width, 0.0, inv)
+        out[...] = both * (1.0 / total) + jnp.where(lane % width == row, DAMPING, 0.0)
+        invert(out)
+
+
+def weigh(scaling, inv, mine, other, out, rows):
+    @pl.when(lax.axis_index("tensor") == 1)
+    def _():
+        slabs = mine.shape[0]
+        width = inv.shape[0]
+        lane = lax.broadcasted_iota(jnp.int32, inv.shape, 1)
+        inv_in, inv_out = inv[:, :width], jnp.where(lane < width, 0.0, inv[...])
         exact = dict(preferred_element_type=F32, precision=lax.Precision.HIGHEST)
         devices = lax.axis_size("seq")
         upper = lax.axis_index("seq") // (devices // 2) == 1
         for slab in range(slabs):
+            parts = []
             for high in (False, True):
                 cross = jnp.where(upper == high, mine[slab, :width], other[slab, :width])
-                part = lax.dot_general(inv_out, cross, NT, **exact)
-                rows[...] = jnp.dot(part, inv_in, **exact) * scaling
-                even, odd = rows[pl.ds(0, width // 2, 2), :], rows[pl.ds(1, width // 2, 2), :]
-                out[slabs * high + slab] = jnp.concatenate([even, odd], axis=1)
+                parts.append(dot3(inv_out, cross, NT))
+            rows[...] = dot3(jnp.concatenate(parts, axis=0), inv_in, NN) * scaling
+            even, odd = rows[pl.ds(0, width, 2), :], rows[pl.ds(1, width, 2), :]
+            both = jnp.concatenate([even, odd], axis=1)
+            out[slab] = both[: width // 2]
+            out[slabs + slab] = both[width // 2 :]
 
 
 def score(mine, other, queries, out):
@@ -207,15 +234,24 @@
         distance *= 2
     total = 3 * seq_count * LEN // 4
     scaling = 1.0 / (width * math.sqrt(LEN))
+    other = exchange(packed, distance, groups, devices)
+    inverse = pl.pallas_call(
+        functools.partial(inverses, float(total)),
+        out_shape=jax.ShapeDtypeStruct((width, 2 * width), F32),
+        in_specs=[VMEM] * 2,
+        out_specs=VMEM,
+        compiler_params=params,
+        name="inverses",
+    )(packed, other)
     weights = pl.pallas_call(
-        functools.partial(weigh, float(total), scaling),
+        functools.partial(weigh, scaling),
         out_shape=jax.ShapeDtypeStruct((seq_count, width // 2, 2 * width), F32),
-        in_specs=[VMEM] * 2,
-        out_specs=VMEM,
-        scratch_shapes=[pltpu.VMEM((width, width), F32)],
+        in_specs=[VMEM] * 3,
+        out_specs=VMEM,
+        scratch_shapes=[pltpu.VMEM((2 * width, width), F32)],
         compiler_params=params,
         name="weigh",
-    )(packed, exchange(packed, distance, groups, devices))
+    )(inverse, packed, other)
     scores = pl.pallas_call(
         score,
         out_shape=jax.ShapeDtypeStruct((seq_count, queries.shape[0]), F32),

time: 20.9 us -> 20 us (0.957)
  starting transfers between devices: 8.93 us -> 8.06 us
    ppermute x2, starting transfers between devices: 2.12 us -> 1.26 us  [swap(): return lax.ppermute(array, 'tensor', [(0, 1), (1, 0)])]
where the time goes in v4:
time: 20 us; the launch traced here: 19.9 us
  starting transfers between devices  8.06 us (40%)
  waiting for transfers between devices  7.73 us (39%)
  Pallas kernels  4.04 us (20%)
    ppermute x3, starting transfers between devices, exchange(): return lax.ppermute(array, ('groups', 'seq', 'tensor'), pairs)  6.8 us
    ppermute x3, waiting for transfers between devices, exchange(): return lax.ppermute(array, ('groups', 'seq', 'tensor'), pairs)  5.97 us
    pallas_call x1, Pallas kernels, shards(): pl.pallas_call(functools.partial(project, chunks), out_shape=jax.ShapeDty...  3.26 us
    ppermute x2, waiting for transfers between devices, swap(): return lax.ppermute(array, 'tensor', [(0, 1), (1, 0)])  1.76 us
    ppermute x2, starting transfers between devices, swap(): return lax.ppermute(array, 'tensor', [(0, 1), (1, 0)])  1.26 us
    pallas_call x1, Pallas kernels, shards(): pl.pallas_call(score, out_shape=jax.ShapeDtypeStruct((seq_count, queries....  0.77 us
  transfers between devices with their start and end apart: 5, of which 5 were waited for; matrix products, arithmetic and copies ran while one was open for 0% of the time, Pallas kernels for 0%

profile of v4, /device:TPU:0, one launch (start us, length us, event | category | flops | bytes accessed | tf_op | source)
XLA Modules:
  0.0 19.9 jit_solution(9819420788655792670)
XLA Ops:
  0.0 0.0 copy-start
  0.0 3.3 %project.1.mine = f32[128,128]{1,0:T(8,128)S(1)} custom-call(s32[2]{0:T(128)} %lengths.1, bf16[128,7168]{1,0:T(8,128)(2,1)} %inputs.1, bf16[128,4096]{1,0:T(8,128)(2,1)} %grads.1, bf16[64,7168]{1,0:T(8,128)(2,1)} %bitcast.3, bf16[64,4096]{1,0:T(8,128)(2,1)} %bitcast.4), custom_call_target="tpu_custom_call" | custom-call | tf_op jit(solution)/shard_map/project/pallas_call | solution.py:203
  3.3 0.5 %collective-permute-start = (f32[128,128]{1,0:T(8,128)S(1)}, f32[128,128]{1,0:T(8,128)S(1)}, u32[]{:S(2)}, u32[]{:S(2)}) collective-permute-start(f32[128,128]{1,0:T(8,128)S(1)} %project.1.mine), channel_id=1, source_target_pairs={{0,1},{1,0},{2,3},{3,2},{4,5},{5,4},{6,7},{7,6},{8,9},{9,8},{10,11... | collective-permute-start | bytes 196616 | tf_op jit(solution)/shard_map/ppermute | solution.py:178
  3.8 0.9 %collective-permute-done.other = f32[128,128]{1,0:T(8,128)S(1)} collective-permute-done((f32[128,128]{1,0:T(8,128)S(1)}, f32[128,128]{1,0:T(8,128)S(1)}, u32[]{:S(2)}, u32[]{:S(2)}) %collective-permute-start) | collective-permute-done | bytes 65568 | tf_op jit(solution)/shard_map/ppermute | solution.py:178
  4.7 2.9 %collective-permute-start.1 = (f32[1,72,128]{2,1,0:T(8,128)S(1)}, f32[1,72,128]{2,1,0:T(8,128)S(1)}, u32[]{:S(2)}, u32[]{:S(2)}) collective-permute-start(f32[1,72,128]{2,1,0:T(8,128)S(1)} %moments.1), channel_id=1, source_target_pairs={{0,4},{1,3},{2,6},{3,1},{4,0},{5,7},{6,2},{7,5},{8,12},{9,11},{10,... | collective-permute-start | bytes 110600 | tf_op jit(solution)/shard_map/ppermute | solution.py:187
  7.6 1.9 %collective-permute-done.1 = f32[1,72,128]{2,1,0:T(8,128)S(1)} collective-permute-done((f32[1,72,128]{2,1,0:T(8,128)S(1)}, f32[1,72,128]{2,1,0:T(8,128)S(1)}, u32[]{:S(2)}, u32[]{:S(2)}) %collective-permute-start.1) | collective-permute-done | bytes 36896 | tf_op jit(solution)/shard_map/ppermute | solution.py:187
  9.6 1.9 %collective-permute-start.2 = (f32[1,72,128]{2,1,0:T(8,128)S(1)}, f32[1,72,128]{2,1,0:T(8,128)S(1)}, u32[]{:S(2)}, u32[]{:S(2)}) collective-permute-start(f32[1,72,128]{2,1,0:T(8,128)S(1)} %add.6), channel_id=1, source_target_pairs={{0,2},{1,5},{2,0},{3,7},{4,6},{5,1},{6,4},{7,3},{8,10},{9,13},{10,... | collective-permute-start | bytes 110600 | tf_op jit(solution)/shard_map/ppermute | solution.py:187
  11.5 2.0 %collective-permute-done.2 = f32[1,72,128]{2,1,0:T(8,128)S(1)} collective-permute-done((f32[1,72,128]{2,1,0:T(8,128)S(1)}, f32[1,72,128]{2,1,0:T(8,128)S(1)}, u32[]{:S(2)}, u32[]{:S(2)}) %collective-permute-start.2) | collective-permute-done | bytes 36896 | tf_op jit(solution)/shard_map/ppermute | solution.py:187
  13.5 1.9 %collective-permute-start.3 = (f32[1,72,128]{2,1,0:T(8,128)S(1)}, f32[1,72,128]{2,1,0:T(8,128)S(1)}, u32[]{:S(2)}, u32[]{:S(2)}) collective-permute-start(f32[1,72,128]{2,1,0:T(8,128)S(1)} %add.7.mine), channel_id=1, source_target_pairs={{0,2},{1,9},{2,0},{3,11},{4,6},{5,13},{6,4},{7,15},{8,10},{9,1},{1... | collective-permute-start | bytes 110600 | tf_op jit(solution)/shard_map/ppermute | solution.py:187
  15.5 2.0 %collective-permute-done.3.other = f32[1,72,128]{2,1,0:T(8,128)S(1)} collective-permute-done((f32[1,72,128]{2,1,0:T(8,128)S(1)}, f32[1,72,128]{2,1,0:T(8,128)S(1)}, u32[]{:S(2)}, u32[]{:S(2)}) %collective-permute-start.3) | collective-permute-done | bytes 36896 | tf_op jit(solution)/shard_map/ppermute | solution.py:187
  17.5 0.7 %collective-permute-start.4 = (f32[2,32,128]{2,1,0:T(8,128)S(1)}, f32[2,32,128]{2,1,0:T(8,128)S(1)}, u32[]{:S(2)}, u32[]{:S(2)}) collective-permute-start(f32[2,32,128]{2,1,0:T(8,128)S(1)} %weigh.1.mine), channel_id=1, source_target_pairs={{0,1},{1,0},{2,3},{3,2},{4,5},{5,4},{6,7},{7,6},{8,9},{9,8},{10,11... | collective-permute-start | bytes 98312 | tf_op jit(solution)/shard_map/ppermute | solution.py:178
  18.2 0.9 %collective-permute-done.4.other = f32[2,32,128]{2,1,0:T(8,128)S(1)} collective-permute-done((f32[2,32,128]{2,1,0:T(8,128)S(1)}, f32[2,32,128]{2,1,0:T(8,128)S(1)}, u32[]{:S(2)}, u32[]{:S(2)}) %collective-permute-start.4) | collective-permute-done | bytes 32800 | tf_op jit(solution)/shard_map/ppermute | solution.py:178
  19.1 0.0 copy-done
  19.1 0.8 %score.1 = f32[2,16]{1,0:T(2,128)} custom-call(f32[2,32,128]{2,1,0:T(8,128)S(1)} %weigh.1.mine, f32[2,32,128]{2,1,0:T(8,128)S(1)} %collective-permute-done.4.other, bf16[16,4096]{1,0:T(8,128)(2,1)S(1)} %copy-done), custom_call_target="tpu_custom_call" | custom-call | tf_op jit(solution)/shard_map/score/pallas_call | solution.py:255
  (5 shorter events, 0.0 us)
Async XLA Ops:
  0.0 19.1 %copy-start = (bf16[16,4096]{1,0:T(8,128)(2,1)S(1)}, bf16[16,4096]{1,0:T(8,128)(2,1)}, u32[]{:S(2)}) copy-start(bf16[16,4096]{1,0:T(8,128)(2,1)} %queries.1) | copy-start | bytes 393220
  3.3 1.4 %collective-permute-start = (f32[128,128]{1,0:T(8,128)S(1)}, f32[128,128]{1,0:T(8,128)S(1)}, u32[]{:S(2)}, u32[]{:S(2)}) collective-permute-start(f32[128,128]{1,0:T(8,128)S(1)} %project.1.mine), channel_id=1, source_target_pairs={{0,1},{1,0},{2,3},{3,2},{4,5},{5,4},{6,7},{7,6},{8,9},{9,8},{10,11... | collective-permute-start | bytes 196616 | tf_op jit(solution)/shard_map/ppermute | solution.py:178
  4.7 4.9 %collective-permute-start.1 = (f32[1,72,128]{2,1,0:T(8,128)S(1)}, f32[1,72,128]{2,1,0:T(8,128)S(1)}, u32[]{:S(2)}, u32[]{:S(2)}) collective-permute-start(f32[1,72,128]{2,1,0:T(8,128)S(1)} %moments.1), channel_id=1, source_target_pairs={{0,4},{1,3},{2,6},{3,1},{4,0},{5,7},{6,2},{7,5},{8,12},{9,11},{10,... | collective-permute-start | bytes 110600 | tf_op jit(solution)/shard_map/ppermute | solution.py:187
  9.6 4.0 %collective-permute-start.2 = (f32[1,72,128]{2,1,0:T(8,128)S(1)}, f32[1,72,128]{2,1,0:T(8,128)S(1)}, u32[]{:S(2)}, u32[]{:S(2)}) collective-permute-start(f32[1,72,128]{2,1,0:T(8,128)S(1)} %add.6), channel_id=1, source_target_pairs={{0,2},{1,5},{2,0},{3,7},{4,6},{5,1},{6,4},{7,3},{8,10},{9,13},{10,... | collective-permute-start | bytes 110600 | tf_op jit(solution)/shard_map/ppermute | solution.py:187
  13.5 4.0 %collective-permute-start.3 = (f32[1,72,128]{2,1,0:T(8,128)S(1)}, f32[1,72,128]{2,1,0:T(8,128)S(1)}, u32[]{:S(2)}, u32[]{:S(2)}) collective-permute-start(f32[1,72,128]{2,1,0:T(8,128)S(1)} %add.7.mine), channel_id=1, source_target_pairs={{0,2},{1,9},{2,0},{3,11},{4,6},{5,13},{6,4},{7,15},{8,10},{9,1},{1... | collective-permute-start | bytes 110600 | tf_op jit(solution)/shard_map/ppermute | solution.py:187
  17.5 1.6 %collective-permute-start.4 = (f32[2,32,128]{2,1,0:T(8,128)S(1)}, f32[2,32,128]{2,1,0:T(8,128)S(1)}, u32[]{:S(2)}, u32[]{:S(2)}) collective-permute-start(f32[2,32,128]{2,1,0:T(8,128)S(1)} %weigh.1.mine), channel_id=1, source_target_pairs={{0,1},{1,0},{2,3},{3,2},{4,5},{5,4},{6,7},{7,6},{8,9},{9,8},{10,11... | collective-permute-start | bytes 98312 | tf_op jit(solution)/shard_map/ppermute | solution.py:178

commit v5 on v4

--- a/solution.py
+++ b/solution.py
@@ -17,36 +17,56 @@
 F32 = jnp.float32
 
 
-def project(chunks, lengths, inputs, grads, proj_in, proj_out, out, *scratch):
-    x_buf, g_buf, px_buf, pg_buf, count, sems = scratch
-    width, tokens = px_buf.shape[0], x_buf.shape[0]
-    jobs, sem = [], 0
-    for rows, row_buf, mat, mat_buf, parts, lo in (
-        (inputs, x_buf, proj_in, px_buf, chunks[0], 0),
-        (grads, g_buf, proj_out, pg_buf, chunks[1], width),
-    ):
-        step = rows.shape[1] // parts
-        for part in range(parts):
-            cols = pl.ds(part * step, step)
-            pair = []
-            for src, dst in ((mat, mat_buf), (rows, row_buf)):
-                pair.append(pltpu.make_async_copy(src.at[:, cols], dst.at[:, cols], sems.at[sem]))
-                pair[-1].start()
-                sem += 1
-            jobs.append((pair, mat_buf, row_buf, cols, lo))
-    scalars = pltpu.make_async_copy(lengths, count, sems.at[sem])
+def split(lo, hi, parts, unit):
+    units = (hi - lo) // unit
+    edges = [lo + unit * -(-units * part // parts) for part in range(parts + 1)]
+    return list(zip(edges, edges[1:]))
+
+
+def project(spans, lengths, inputs, grads, proj_in, proj_out, out, buf, count, sems):
+    width, tokens = proj_in.shape[0], inputs.shape[0]
+    tile = 2 * tokens
+    outer = grads.shape[1]
+    x_rows, g_rows = pl.ds(width, tokens), pl.ds(width + tokens, tokens)
+    px_rows, pg_rows = pl.ds(0, width), pl.ds(width + tile, width)
+    for part, (lo, hi) in enumerate(spans):
+        cols = pl.ds(lo, hi - lo)
+        for src, rows in ((proj_in, px_rows), (inputs, x_rows), (grads, g_rows), (proj_out, pg_rows)):
+            if lo < src.shape[1]:
+                pltpu.make_async_copy(src.at[:, cols], buf.at[rows, cols], sems.at[part]).start()
+    scalars = pltpu.make_async_copy(lengths, count, sems.at[len(spans)])
     scalars.start()
-    totals = {}
-    for pair, mat_buf, row_buf, cols, lo in jobs:
-        for copy in pair:
-            copy.wait()
-        part = lax.dot_general(mat_buf[:, cols], row_buf[:, cols], NT, preferred_element_type=F32)
-        totals[lo] = part if lo not in totals else totals[lo] + part
-    scalars.wait()
-    first = lax.axis_index("seq") * tokens
-    valid = lax.broadcasted_iota(jnp.int32, (width, tokens), 1) + first % LEN < count[first // LEN]
-    for lo, total in totals.items():
-        out[lo : lo + width, :] = jnp.where(valid, total, 0.0)
+
+    def multiply(*accs):
+        step = 0
+        for part, (lo, hi) in enumerate(spans):
+            rows = buf.shape[0] if lo < outer else width + tokens
+            landed = buf.at[pl.ds(0, rows), pl.ds(lo, hi - lo)]
+            pltpu.make_async_copy(landed, landed, sems.at[part]).wait()
+            tiles = [pl.ds(start, tile) for start in range(lo, hi, tile)]
+            if lo < outer:
+                pairs = [((x_rows, px_rows, cols), (g_rows, pg_rows, cols)) for cols in tiles]
+            else:
+                pairs = [tuple((x_rows, px_rows, cols) for cols in tiles[i : i + 2]) for i in range(0, len(tiles), 2)]
+            for pair in pairs:
+                unit, stage = step % 2, step // 2 % 2
+                step += 1
+                blocks = [buf[rows, cols] for rows, _, cols in pair]
+                both = jnp.concatenate(blocks * (2 // len(blocks)), axis=0)
+                pltpu.matmul_push_rhs(both, stage, unit, transpose=True)
+                for place, (rows, mat_rows, cols) in enumerate(pair):
+                    acc = accs[2 * (place + (place == 1 and rows is x_rows)) + unit]
+                    pltpu.matmul_acc_lhs(acc, buf[mat_rows, cols], load_staged_rhs=None if place else stage)
+        scalars.wait()
+        first = lax.axis_index("seq") * tokens
+        valid = lax.broadcasted_iota(jnp.int32, (width, tokens), 1) + first % LEN < count[first // LEN]
+        x_left, g_right, x_right = (
+            pltpu.matmul_pop(accs[2 * kind]) + pltpu.matmul_pop(accs[2 * kind + 1]) for kind in range(3)
+        )
+        out[:width, :] = jnp.where(valid, x_left[:, :tokens] + x_right[:, tokens:], 0.0)
+        out[width:, :] = jnp.where(valid, g_right[:, tokens:], 0.0)
+
+    pl.run_scoped(multiply, *(pltpu.ACC(mxu_id=unit)((width, tile), F32) for unit in (0, 1, 0, 1, 0, 1)))
 
 
 def dot3(a, b, dims):
@@ -198,20 +218,19 @@
     width = proj_in.shape[1]
     tokens = inputs.shape[0]
     seq_count = lengths.shape[0]
-    chunks = (4, 2)
+    inner, outer = inputs.shape[1], out_grads.shape[1]
+    tile = 2 * tokens
+    spans = split(outer, inner, 2, 2 * tile) + split(0, outer, 3, tile)
     params = pltpu.CompilerParams(vmem_limit_bytes=16 << 20)
     partial_z = pl.pallas_call(
-        functools.partial(project, chunks),
+        functools.partial(project, spans),
         out_shape=jax.ShapeDtypeStruct((2 * width, tokens), F32),
         in_specs=[HBM] * 5,
         out_specs=VMEM,
         scratch_shapes=[
-            pltpu.VMEM(inputs.shape, inputs.dtype),
-            pltpu.VMEM(out_grads.shape, out_grads.dtype),
-            pltpu.VMEM(proj_in.shape[::-1], proj_in.dtype),
-            pltpu.VMEM(proj_out.shape[::-1], proj_out.dtype),
+            pltpu.VMEM((2 * (width + tokens), inner), inputs.dtype),
             pltpu.SMEM(lengths.shape, lengths.dtype),
-            pltpu.SemaphoreType.DMA((2 * sum(chunks) + 1,)),
+            pltpu.SemaphoreType.DMA((len(spans) + 1,)),
         ],
         compiler_params=params,
         name="project",

time: 20 us -> 19.4 us (0.970)
  Pallas kernels: 4.04 us -> 3.47 us
    pallas_call x1, Pallas kernels: 3.26 us -> 2.69 us  [shards(): pl.pallas_call(functools.partial(project, spans), out_shape=jax.ShapeDtyp...]
where the time goes in v5:
time: 19.4 us; the launch traced here: 19.3 us
  starting transfers between devices  8.05 us (41%)
  waiting for transfers between devices  7.73 us (40%)
  Pallas kernels  3.47 us (18%)
    ppermute x3, starting transfers between devices, exchange(): return lax.ppermute(array, ('groups', 'seq', 'tensor'), pairs)  6.8 us
    ppermute x3, waiting for transfers between devices, exchange(): return lax.ppermute(array, ('groups', 'seq', 'tensor'), pairs)  5.97 us
    pallas_call x1, Pallas kernels, shards(): pl.pallas_call(functools.partial(project, spans), out_shape=jax.ShapeDtyp...  2.69 us
    ppermute x2, waiting for transfers between devices, swap(): return lax.ppermute(array, 'tensor', [(0, 1), (1, 0)])  1.76 us
    ppermute x2, starting transfers between devices, swap(): return lax.ppermute(array, 'tensor', [(0, 1), (1, 0)])  1.25 us
    pallas_call x1, Pallas kernels, shards(): pl.pallas_call(score, out_shape=jax.ShapeDtypeStruct((seq_count, queries....  0.77 us
  transfers between devices with their start and end apart: 5, of which 5 were waited for; matrix products, arithmetic and copies ran while one was open for 0% of the time, Pallas kernels for 0%

profile of v5, /device:TPU:0, one launch (start us, length us, event | category | flops | bytes accessed | tf_op | source)
XLA Modules:
  0.0 19.3 jit_solution(17300073418559833025)
XLA Ops:
  0.0 0.0 copy-start
  0.0 2.7 %project.1.mine = f32[128,128]{1,0:T(8,128)S(1)} custom-call(s32[2]{0:T(128)} %lengths.1, bf16[128,7168]{1,0:T(8,128)(2,1)} %inputs.1, bf16[128,4096]{1,0:T(8,128)(2,1)} %grads.1, bf16[64,7168]{1,0:T(8,128)(2,1)} %bitcast.3, bf16[64,4096]{1,0:T(8,128)(2,1)} %bitcast.4), custom_call_target="tpu_custom_call" | custom-call | tf_op jit(solution)/shard_map/project/pallas_call | solution.py:225
  2.7 0.5 %collective-permute-start = (f32[128,128]{1,0:T(8,128)S(1)}, f32[128,128]{1,0:T(8,128)S(1)}, u32[]{:S(2)}, u32[]{:S(2)}) collective-permute-start(f32[128,128]{1,0:T(8,128)S(1)} %project.1.mine), channel_id=1, source_target_pairs={{0,1},{1,0},{2,3},{3,2},{4,5},{5,4},{6,7},{7,6},{8,9},{9,8},{10,11... | collective-permute-start | bytes 196616 | tf_op jit(solution)/shard_map/ppermute | solution.py:198
  3.2 0.9 %collective-permute-done.other = f32[128,128]{1,0:T(8,128)S(1)} collective-permute-done((f32[128,128]{1,0:T(8,128)S(1)}, f32[128,128]{1,0:T(8,128)S(1)}, u32[]{:S(2)}, u32[]{:S(2)}) %collective-permute-start) | collective-permute-done | bytes 65568 | tf_op jit(solution)/shard_map/ppermute | solution.py:198
  4.1 2.9 %collective-permute-start.1 = (f32[1,72,128]{2,1,0:T(8,128)S(1)}, f32[1,72,128]{2,1,0:T(8,128)S(1)}, u32[]{:S(2)}, u32[]{:S(2)}) collective-permute-start(f32[1,72,128]{2,1,0:T(8,128)S(1)} %moments.1), channel_id=1, source_target_pairs={{0,4},{1,3},{2,6},{3,1},{4,0},{5,7},{6,2},{7,5},{8,12},{9,11},{10,... | collective-permute-start | bytes 110600 | tf_op jit(solution)/shard_map/ppermute | solution.py:207
  7.0 1.9 %collective-permute-done.1 = f32[1,72,128]{2,1,0:T(8,128)S(1)} collective-permute-done((f32[1,72,128]{2,1,0:T(8,128)S(1)}, f32[1,72,128]{2,1,0:T(8,128)S(1)}, u32[]{:S(2)}, u32[]{:S(2)}) %collective-permute-start.1) | collective-permute-done | bytes 36896 | tf_op jit(solution)/shard_map/ppermute | solution.py:207
  9.0 1.9 %collective-permute-start.2 = (f32[1,72,128]{2,1,0:T(8,128)S(1)}, f32[1,72,128]{2,1,0:T(8,128)S(1)}, u32[]{:S(2)}, u32[]{:S(2)}) collective-permute-start(f32[1,72,128]{2,1,0:T(8,128)S(1)} %add.6), channel_id=1, source_target_pairs={{0,2},{1,5},{2,0},{3,7},{4,6},{5,1},{6,4},{7,3},{8,10},{9,13},{10,... | collective-permute-start | bytes 110600 | tf_op jit(solution)/shard_map/ppermute | solution.py:207
  10.9 2.0 %collective-permute-done.2 = f32[1,72,128]{2,1,0:T(8,128)S(1)} collective-permute-done((f32[1,72,128]{2,1,0:T(8,128)S(1)}, f32[1,72,128]{2,1,0:T(8,128)S(1)}, u32[]{:S(2)}, u32[]{:S(2)}) %collective-permute-start.2) | collective-permute-done | bytes 36896 | tf_op jit(solution)/shard_map/ppermute | solution.py:207
  13.0 1.9 %collective-permute-start.3 = (f32[1,72,128]{2,1,0:T(8,128)S(1)}, f32[1,72,128]{2,1,0:T(8,128)S(1)}, u32[]{:S(2)}, u32[]{:S(2)}) collective-permute-start(f32[1,72,128]{2,1,0:T(8,128)S(1)} %add.7.mine), channel_id=1, source_target_pairs={{0,2},{1,9},{2,0},{3,11},{4,6},{5,13},{6,4},{7,15},{8,10},{9,1},{1... | collective-permute-start | bytes 110600 | tf_op jit(solution)/shard_map/ppermute | solution.py:207
  14.9 2.0 %collective-permute-done.3.other = f32[1,72,128]{2,1,0:T(8,128)S(1)} collective-permute-done((f32[1,72,128]{2,1,0:T(8,128)S(1)}, f32[1,72,128]{2,1,0:T(8,128)S(1)}, u32[]{:S(2)}, u32[]{:S(2)}) %collective-permute-start.3) | collective-permute-done | bytes 36896 | tf_op jit(solution)/shard_map/ppermute | solution.py:207
  16.9 0.7 %collective-permute-start.4 = (f32[2,32,128]{2,1,0:T(8,128)S(1)}, f32[2,32,128]{2,1,0:T(8,128)S(1)}, u32[]{:S(2)}, u32[]{:S(2)}) collective-permute-start(f32[2,32,128]{2,1,0:T(8,128)S(1)} %weigh.1.mine), channel_id=1, source_target_pairs={{0,1},{1,0},{2,3},{3,2},{4,5},{5,4},{6,7},{7,6},{8,9},{9,8},{10,11... | collective-permute-start | bytes 98312 | tf_op jit(solution)/shard_map/ppermute | solution.py:198
  17.6 0.9 %collective-permute-done.4.other = f32[2,32,128]{2,1,0:T(8,128)S(1)} collective-permute-done((f32[2,32,128]{2,1,0:T(8,128)S(1)}, f32[2,32,128]{2,1,0:T(8,128)S(1)}, u32[]{:S(2)}, u32[]{:S(2)}) %collective-permute-start.4) | collective-permute-done | bytes 32800 | tf_op jit(solution)/shard_map/ppermute | solution.py:198
  18.5 0.0 copy-done
  18.5 0.8 %score.1 = f32[2,16]{1,0:T(2,128)} custom-call(f32[2,32,128]{2,1,0:T(8,128)S(1)} %weigh.1.mine, f32[2,32,128]{2,1,0:T(8,128)S(1)} %collective-permute-done.4.other, bf16[16,4096]{1,0:T(8,128)(2,1)S(1)} %copy-done), custom_call_target="tpu_custom_call" | custom-call | tf_op jit(solution)/shard_map/score/pallas_call | solution.py:274
  (5 shorter events, 0.0 us)
Async XLA Ops:
  0.0 18.5 %copy-start = (bf16[16,4096]{1,0:T(8,128)(2,1)S(1)}, bf16[16,4096]{1,0:T(8,128)(2,1)}, u32[]{:S(2)}) copy-start(bf16[16,4096]{1,0:T(8,128)(2,1)} %queries.1) | copy-start | bytes 393220
  2.7 1.4 %collective-permute-start = (f32[128,128]{1,0:T(8,128)S(1)}, f32[128,128]{1,0:T(8,128)S(1)}, u32[]{:S(2)}, u32[]{:S(2)}) collective-permute-start(f32[128,128]{1,0:T(8,128)S(1)} %project.1.mine), channel_id=1, source_target_pairs={{0,1},{1,0},{2,3},{3,2},{4,5},{5,4},{6,7},{7,6},{8,9},{9,8},{10,11... | collective-permute-start | bytes 196616 | tf_op jit(solution)/shard_map/ppermute | solution.py:198
  4.1 4.9 %collective-permute-start.1 = (f32[1,72,128]{2,1,0:T(8,128)S(1)}, f32[1,72,128]{2,1,0:T(8,128)S(1)}, u32[]{:S(2)}, u32[]{:S(2)}) collective-permute-start(f32[1,72,128]{2,1,0:T(8,128)S(1)} %moments.1), channel_id=1, source_target_pairs={{0,4},{1,3},{2,6},{3,1},{4,0},{5,7},{6,2},{7,5},{8,12},{9,11},{10,... | collective-permute-start | bytes 110600 | tf_op jit(solution)/shard_map/ppermute | solution.py:207
  9.0 4.0 %collective-permute-start.2 = (f32[1,72,128]{2,1,0:T(8,128)S(1)}, f32[1,72,128]{2,1,0:T(8,128)S(1)}, u32[]{:S(2)}, u32[]{:S(2)}) collective-permute-start(f32[1,72,128]{2,1,0:T(8,128)S(1)} %add.6), channel_id=1, source_target_pairs={{0,2},{1,5},{2,0},{3,7},{4,6},{5,1},{6,4},{7,3},{8,10},{9,13},{10,... | collective-permute-start | bytes 110600 | tf_op jit(solution)/shard_map/ppermute | solution.py:207
  13.0 4.0 %collective-permute-start.3 = (f32[1,72,128]{2,1,0:T(8,128)S(1)}, f32[1,72,128]{2,1,0:T(8,128)S(1)}, u32[]{:S(2)}, u32[]{:S(2)}) collective-permute-start(f32[1,72,128]{2,1,0:T(8,128)S(1)} %add.7.mine), channel_id=1, source_target_pairs={{0,2},{1,9},{2,0},{3,11},{4,6},{5,13},{6,4},{7,15},{8,10},{9,1},{1... | collective-permute-start | bytes 110600 | tf_op jit(solution)/shard_map/ppermute | solution.py:207
  16.9 1.6 %collective-permute-start.4 = (f32[2,32,128]{2,1,0:T(8,128)S(1)}, f32[2,32,128]{2,1,0:T(8,128)S(1)}, u32[]{:S(2)}, u32[]{:S(2)}) collective-permute-start(f32[2,32,128]{2,1,0:T(8,128)S(1)} %weigh.1.mine), channel_id=1, source_target_pairs={{0,1},{1,0},{2,3},{3,2},{4,5},{5,4},{6,7},{7,6},{8,9},{9,8},{10,11... | collective-permute-start | bytes 98312 | tf_op jit(solution)/shard_map/ppermute | solution.py:198

commit v6 on v5

--- a/solution.py
+++ b/solution.py
@@ -10,6 +10,7 @@
 
 LEN = 512
 DAMPING = 0.1
+PANEL = 16
 VMEM = pl.BlockSpec(memory_space=pltpu.VMEM)
 HBM = pl.BlockSpec(memory_space=pltpu.HBM)
 NN = (((1,), (0,)), ((), ()))
@@ -108,39 +109,45 @@
 
 def invert(state):
     width = state.shape[0]
-    blocks = width // 8
     lane = lax.broadcasted_iota(jnp.int32, (8, 2 * width), 1)
     row_of = lax.broadcasted_iota(jnp.int32, (8, 2 * width), 0)
     column = lane % width
     right = lane - column
 
     def panel(step, carry):
-        first = step * 8
-        own = pl.ds(pl.multiple_of(first, 8), 8)
-        inside = (column >= first) & (column < first + 8)
-        index = [right + (first + t) for t in range(8)]
-        rows = [state[8 * b : 8 * b + 8, :] for b in range(blocks)]
-        pivots = state[own, :]
-        heads = [jnp.take_along_axis(pivots, index[t], axis=1) for t in range(8)]
-        cols = [[jnp.take_along_axis(r, index[t], axis=1) for r in rows] for t in range(8)]
-        pivots = jnp.where(inside, jnp.where(column - first == row_of, 1.0, 0.0), pivots)
-        rows = [jnp.where(inside, 0.0, r) for r in rows]
-        for t in range(8):
-            inverse = 1.0 / heads[t][t : t + 1]
-            pivot = pivots[t : t + 1] * inverse
-            here = row_of == t
-            pivots = jnp.where(here, pivot, pivots - jnp.where(here, 0.0, heads[t]) * pivot)
-            rows = [rows[b] - cols[t][b] * pivot for b in range(blocks)]
-            for j in range(t + 1, 8):
-                scaled = heads[j][t : t + 1] * inverse
-                heads[j] = jnp.where(here, scaled, heads[j] - heads[t] * scaled)
-                cols[j] = [cols[j][b] - cols[t][b] * scaled for b in range(blocks)]
-        for b in range(blocks):
-            state[8 * b : 8 * b + 8, :] = rows[b]
-        state[own, :] = pivots
+        first = step * PANEL
+        own = pl.ds(pl.multiple_of(first, PANEL), PANEL)
+        inside = (column >= first) & (column < first + PANEL)
+        index = [right + (first + t) for t in range(PANEL)]
+        block = state[own, :]
+        pivots = [block[8 * i : 8 * i + 8] for i in range(PANEL // 8)]
+        heads = [[jnp.take_along_axis(p, index[t], axis=1) for p in pivots] for t in range(PANEL)]
+        rows = [state[8 * b : 8 * b + 8, :] for b in range(width // 8)]
+        cols = [[jnp.take_along_axis(r, index[t], axis=1) for r in rows] for t in range(PANEL)]
+        for i in range(PANEL // 8):
+            unit = jnp.where(column - first == row_of + 8 * i, 1.0, 0.0)
+            pivots[i] = jnp.where(inside, unit, pivots[i])
+        for t in range(PANEL):
+            at, sub = t // 8, t % 8
+            here = row_of == sub
+            inverse = 1.0 / heads[t][at][sub : sub + 1]
+            rest = [jnp.where(here, 0.0, h) if i == at else h for i, h in enumerate(heads[t])]
+
+            def step_rows(tiles):
+                scaled = tiles[at][sub : sub + 1] * inverse
+                return [(jnp.where(here, scaled, x) if i == at else x) - rest[i] * scaled for i, x in enumerate(tiles)]
+
+            pivots = step_rows(pivots)
+            heads[t + 1 :] = [step_rows(head) for head in heads[t + 1 :]]
+        for b in range(width // 8):
+            total = jnp.where(inside, 0.0, rows[b])
+            for t in range(PANEL):
+                total = total - cols[t][b] * pivots[t // 8][t % 8 : t % 8 + 1]
+            state[8 * b : 8 * b + 8, :] = total
+        state[own, :] = jnp.concatenate(pivots, axis=0)
         return carry
 
-    lax.fori_loop(0, blocks, panel, 0)
+    lax.fori_loop(0, width // PANEL, panel, 0)
 
 
 def inverses(total, mine, other, out):
@@ -199,7 +206,7 @@
 
 
 def exchange(array, distance, groups, devices):
-    near = 2 if distance == 1 else 1
+    near = distance if distance < 4 else 1
     pairs = []
     for chip in range(groups * devices):
         pairs.append((2 * chip, 2 * (chip ^ near)))
@@ -246,10 +253,10 @@
     )(partial_z, swap(partial_z))
     groups, devices = lax.axis_size("groups"), lax.axis_size("seq")
     holders = devices // seq_count
-    distance = 1
+    packed = packed + sum(exchange(packed, near, groups, devices) for near in range(1, holders))
+    distance = holders
     while 2 * distance < devices:
-        other = exchange(packed, distance, groups, devices)
-        packed = packed + other if distance < holders else gather(packed, other, distance, width)
+        packed = gather(packed, exchange(packed, distance, groups, devices), distance, width)
         distance *= 2
     total = 3 * seq_count * LEN // 4
     scaling = 1.0 / (width * math.sqrt(LEN))

time: 19.4 us -> 18.7 us (0.964)
  starting transfers between devices: 8.05 us -> 5.82 us
  waiting for transfers between devices: 7.73 us -> 9.27 us
    ppermute x3 -> x4, starting transfers between devices: 6.8 us -> 4.77 us  [exchange(): return lax.ppermute(array, ('groups', 'seq', 'tensor'), pairs)]
    ppermute x3 -> x4, waiting for transfers between devices: 5.97 us -> 7.51 us  [exchange(): return lax.ppermute(array, ('groups', 'seq', 'tensor'), pairs)]
  transfers between devices with their start and end apart: 5 -> 6, of which waited for: 5 -> 6; matrix products, arithmetic and copies ran while one was open for 0% -> 0% of each run, Pallas kernels for 0% -> 0%
where the time goes in v6:
time: 18.7 us; the launch traced here: 18.6 us
  waiting for transfers between devices  9.27 us (50%)
  starting transfers between devices  5.82 us (31%)
  Pallas kernels  3.47 us (19%)
    ppermute x4, waiting for transfers between devices, exchange(): return lax.ppermute(array, ('groups', 'seq', 'tensor'), pairs)  7.51 us
    ppermute x4, starting transfers between devices, exchange(): return lax.ppermute(array, ('groups', 'seq', 'tensor'), pairs)  4.77 us
    pallas_call x1, Pallas kernels, shards(): pl.pallas_call(functools.partial(project, spans), out_shape=jax.ShapeDtyp...  2.69 us
    ppermute x2, waiting for transfers between devices, swap(): return lax.ppermute(array, 'tensor', [(0, 1), (1, 0)])  1.76 us
    ppermute x2, starting transfers between devices, swap(): return lax.ppermute(array, 'tensor', [(0, 1), (1, 0)])  1.05 us
    pallas_call x1, Pallas kernels, shards(): pl.pallas_call(score, out_shape=jax.ShapeDtypeStruct((seq_count, queries....  0.77 us
  transfers between devices with their start and end apart: 6, of which 6 were waited for; matrix products, arithmetic and copies ran while one was open for 0% of the time, Pallas kernels for 0%

profile of v6, /device:TPU:0, one launch (start us, length us, event | category | flops | bytes accessed | tf_op | source)
XLA Modules:
  0.0 18.6 jit_solution(360340032354678378)
XLA Ops:
  0.0 0.0 copy-start
  0.0 2.7 %project.1.mine = f32[128,128]{1,0:T(8,128)S(1)} custom-call(s32[2]{0:T(128)} %lengths.1, bf16[128,7168]{1,0:T(8,128)(2,1)} %inputs.1, bf16[128,4096]{1,0:T(8,128)(2,1)} %grads.1, bf16[64,7168]{1,0:T(8,128)(2,1)} %bitcast.3, bf16[64,4096]{1,0:T(8,128)(2,1)} %bitcast.4), custom_call_target="tpu_custom_call" | custom-call | tf_op jit(solution)/shard_map/project/pallas_call | solution.py:232
  2.7 0.5 %collective-permute-start = (f32[128,128]{1,0:T(8,128)S(1)}, f32[128,128]{1,0:T(8,128)S(1)}, u32[]{:S(2)}, u32[]{:S(2)}) collective-permute-start(f32[128,128]{1,0:T(8,128)S(1)} %project.1.mine), channel_id=1, source_target_pairs={{0,1},{1,0},{2,3},{3,2},{4,5},{5,4},{6,7},{7,6},{8,9},{9,8},{10,11... | collective-permute-start | bytes 196616 | tf_op jit(solution)/shard_map/ppermute | solution.py:205
  3.2 0.9 %collective-permute-done.other = f32[128,128]{1,0:T(8,128)S(1)} collective-permute-done((f32[128,128]{1,0:T(8,128)S(1)}, f32[128,128]{1,0:T(8,128)S(1)}, u32[]{:S(2)}, u32[]{:S(2)}) %collective-permute-start) | collective-permute-done | bytes 65568 | tf_op jit(solution)/shard_map/ppermute | solution.py:205
  4.1 3.9 %collective-permute-start.3 = (f32[1,72,128]{2,1,0:T(8,128)S(1)}, f32[1,72,128]{2,1,0:T(8,128)S(1)}, u32[]{:S(2)}, u32[]{:S(2)}) collective-permute-start(f32[1,72,128]{2,1,0:T(8,128)S(1)} %moments.1), channel_id=1, source_target_pairs={{0,6},{1,7},{2,4},{3,5},{4,2},{5,3},{6,0},{7,1},{8,14},{9,15},{10,... | collective-permute-start | bytes 110600 | tf_op jit(solution)/shard_map/ppermute | solution.py:214
  8.0 0.4 %collective-permute-start.2 = (f32[1,72,128]{2,1,0:T(8,128)S(1)}, f32[1,72,128]{2,1,0:T(8,128)S(1)}, u32[]{:S(2)}, u32[]{:S(2)}) collective-permute-start(f32[1,72,128]{2,1,0:T(8,128)S(1)} %moments.1), channel_id=1, source_target_pairs={{0,4},{1,5},{2,6},{3,7},{4,0},{5,1},{6,2},{7,3},{8,12},{9,13},{10,... | collective-permute-start | bytes 110600 | tf_op jit(solution)/shard_map/ppermute | solution.py:214
  8.4 0.2 collective-permute-start.1
  8.6 1.5 %collective-permute-done.3 = f32[1,72,128]{2,1,0:T(8,128)S(1)} collective-permute-done((f32[1,72,128]{2,1,0:T(8,128)S(1)}, f32[1,72,128]{2,1,0:T(8,128)S(1)}, u32[]{:S(2)}, u32[]{:S(2)}) %collective-permute-start.3) | collective-permute-done | bytes 36896 | tf_op jit(solution)/shard_map/ppermute | solution.py:214
  10.1 1.8 %collective-permute-done.2 = f32[1,72,128]{2,1,0:T(8,128)S(1)} collective-permute-done((f32[1,72,128]{2,1,0:T(8,128)S(1)}, f32[1,72,128]{2,1,0:T(8,128)S(1)}, u32[]{:S(2)}, u32[]{:S(2)}) %collective-permute-start.2) | collective-permute-done | bytes 36896 | tf_op jit(solution)/shard_map/ppermute | solution.py:214
  11.9 0.4 %collective-permute-done.1 = f32[1,72,128]{2,1,0:T(8,128)S(1)} collective-permute-done((f32[1,72,128]{2,1,0:T(8,128)S(1)}, f32[1,72,128]{2,1,0:T(8,128)S(1)}, u32[]{:S(2)}, u32[]{:S(2)}) %collective-permute-start.1) | collective-permute-done | bytes 36896 | tf_op jit(solution)/shard_map/ppermute | solution.py:214
  12.4 0.3 %collective-permute-start.4 = (f32[1,72,128]{2,1,0:T(8,128)S(1)}, f32[1,72,128]{2,1,0:T(8,128)S(1)}, u32[]{:S(2)}, u32[]{:S(2)}) collective-permute-start(f32[1,72,128]{2,1,0:T(8,128)S(1)} %add_add_fusion.mine), channel_id=1, source_target_pairs={{0,2},{1,9},{2,0},{3,11},{4,6},{5,13},{6,4},{7,15},{8,10},{9,1},{1... | collective-permute-start | bytes 110600 | tf_op jit(solution)/shard_map/ppermute | solution.py:214
  12.7 3.7 %collective-permute-done.4.other = f32[1,72,128]{2,1,0:T(8,128)S(1)} collective-permute-done((f32[1,72,128]{2,1,0:T(8,128)S(1)}, f32[1,72,128]{2,1,0:T(8,128)S(1)}, u32[]{:S(2)}, u32[]{:S(2)}) %collective-permute-start.4) | collective-permute-done | bytes 36896 | tf_op jit(solution)/shard_map/ppermute | solution.py:214
  16.4 0.5 %collective-permute-start.5 = (f32[2,32,128]{2,1,0:T(8,128)S(1)}, f32[2,32,128]{2,1,0:T(8,128)S(1)}, u32[]{:S(2)}, u32[]{:S(2)}) collective-permute-start(f32[2,32,128]{2,1,0:T(8,128)S(1)} %weigh.1.mine), channel_id=1, source_target_pairs={{0,1},{1,0},{2,3},{3,2},{4,5},{5,4},{6,7},{7,6},{8,9},{9,8},{10,11... | collective-permute-start | bytes 98312 | tf_op jit(solution)/shard_map/ppermute | solution.py:205
  17.0 0.9 %collective-permute-done.5.other = f32[2,32,128]{2,1,0:T(8,128)S(1)} collective-permute-done((f32[2,32,128]{2,1,0:T(8,128)S(1)}, f32[2,32,128]{2,1,0:T(8,128)S(1)}, u32[]{:S(2)}, u32[]{:S(2)}) %collective-permute-start.5) | collective-permute-done | bytes 32800 | tf_op jit(solution)/shard_map/ppermute | solution.py:205
  17.8 0.0 copy-done
  17.8 0.8 %score.1 = f32[2,16]{1,0:T(2,128)} custom-call(f32[2,32,128]{2,1,0:T(8,128)S(1)} %weigh.1.mine, f32[2,32,128]{2,1,0:T(8,128)S(1)} %collective-permute-done.5.other, bf16[16,4096]{1,0:T(8,128)(2,1)S(1)} %copy-done), custom_call_target="tpu_custom_call" | custom-call | tf_op jit(solution)/shard_map/score/pallas_call | solution.py:281
  (4 shorter events, 0.0 us)
Async XLA Ops:
  0.0 17.8 %copy-start = (bf16[16,4096]{1,0:T(8,128)(2,1)S(1)}, bf16[16,4096]{1,0:T(8,128)(2,1)}, u32[]{:S(2)}) copy-start(bf16[16,4096]{1,0:T(8,128)(2,1)} %queries.1) | copy-start | bytes 393220
  2.7 1.4 %collective-permute-start = (f32[128,128]{1,0:T(8,128)S(1)}, f32[128,128]{1,0:T(8,128)S(1)}, u32[]{:S(2)}, u32[]{:S(2)}) collective-permute-start(f32[128,128]{1,0:T(8,128)S(1)} %project.1.mine), channel_id=1, source_target_pairs={{0,1},{1,0},{2,3},{3,2},{4,5},{5,4},{6,7},{7,6},{8,9},{9,8},{10,11... | collective-permute-start | bytes 196616 | tf_op jit(solution)/shard_map/ppermute | solution.py:205
  4.1 6.0 %collective-permute-start.3 = (f32[1,72,128]{2,1,0:T(8,128)S(1)}, f32[1,72,128]{2,1,0:T(8,128)S(1)}, u32[]{:S(2)}, u32[]{:S(2)}) collective-permute-start(f32[1,72,128]{2,1,0:T(8,128)S(1)} %moments.1), channel_id=1, source_target_pairs={{0,6},{1,7},{2,4},{3,5},{4,2},{5,3},{6,0},{7,1},{8,14},{9,15},{10,... | collective-permute-start | bytes 110600 | tf_op jit(solution)/shard_map/ppermute | solution.py:214
  8.0 4.0 %collective-permute-start.2 = (f32[1,72,128]{2,1,0:T(8,128)S(1)}, f32[1,72,128]{2,1,0:T(8,128)S(1)}, u32[]{:S(2)}, u32[]{:S(2)}) collective-permute-start(f32[1,72,128]{2,1,0:T(8,128)S(1)} %moments.1), channel_id=1, source_target_pairs={{0,4},{1,5},{2,6},{3,7},{4,0},{5,1},{6,2},{7,3},{8,12},{9,13},{10,... | collective-permute-start | bytes 110600 | tf_op jit(solution)/shard_map/ppermute | solution.py:214
  8.4 4.0 %collective-permute-start.1 = (f32[1,72,128]{2,1,0:T(8,128)S(1)}, f32[1,72,128]{2,1,0:T(8,128)S(1)}, u32[]{:S(2)}, u32[]{:S(2)}) collective-permute-start(f32[1,72,128]{2,1,0:T(8,128)S(1)} %moments.1), channel_id=1, source_target_pairs={{0,2},{1,3},{2,0},{3,1},{4,6},{5,7},{6,4},{7,5},{8,10},{9,11},{10,... | collective-permute-start | bytes 110600 | tf_op jit(solution)/shard_map/ppermute | solution.py:214
  12.4 4.0 %collective-permute-start.4 = (f32[1,72,128]{2,1,0:T(8,128)S(1)}, f32[1,72,128]{2,1,0:T(8,128)S(1)}, u32[]{:S(2)}, u32[]{:S(2)}) collective-permute-start(f32[1,72,128]{2,1,0:T(8,128)S(1)} %add_add_fusion.mine), channel_id=1, source_target_pairs={{0,2},{1,9},{2,0},{3,11},{4,6},{5,13},{6,4},{7,15},{8,10},{9,1},{1... | collective-permute-start | bytes 110600 | tf_op jit(solution)/shard_map/ppermute | solution.py:214
  16.4 1.4 %collective-permute-start.5 = (f32[2,32,128]{2,1,0:T(8,128)S(1)}, f32[2,32,128]{2,1,0:T(8,128)S(1)}, u32[]{:S(2)}, u32[]{:S(2)}) collective-permute-start(f32[2,32,128]{2,1,0:T(8,128)S(1)} %weigh.1.mine), channel_id=1, source_target_pairs={{0,1},{1,0},{2,3},{3,2},{4,5},{5,4},{6,7},{7,6},{8,9},{9,8},{10,11... | collective-permute-start | bytes 98312 | tf_op jit(solution)/shard_map/ppermute | solution.py:205

commit v7 on v6

--- a/solution.py
+++ b/solution.py
@@ -162,38 +162,49 @@
         invert(out)
 
 
-def weigh(scaling, inv, mine, other, out, rows):
+def weigh(scaling, inv, mine, other, out):
     @pl.when(lax.axis_index("tensor") == 1)
     def _():
         slabs = mine.shape[0]
         width = inv.shape[0]
-        lane = lax.broadcasted_iota(jnp.int32, inv.shape, 1)
-        inv_in, inv_out = inv[:, :width], jnp.where(lane < width, 0.0, inv[...])
-        exact = dict(preferred_element_type=F32, precision=lax.Precision.HIGHEST)
+        half = width // 2
+        left = lax.broadcasted_iota(jnp.int32, inv.shape, 1) < width
+        rows = jnp.concatenate([inv[pl.ds(0, half, 2), :], inv[pl.ds(1, half, 2), :]], axis=0)
+        inv_out = jnp.where(left, 0.0, rows * scaling)
+        inv_in = inv[...]
+        diagonal = jnp.concatenate(
+            [jnp.where(left, inv_in, 0.0), jnp.where(left, 0.0, pltpu.roll(inv_in, width, 1))], axis=0
+        )
         devices = lax.axis_size("seq")
         upper = lax.axis_index("seq") // (devices // 2) == 1
         for slab in range(slabs):
-            parts = []
-            for high in (False, True):
-                cross = jnp.where(upper == high, mine[slab, :width], other[slab, :width])
-                parts.append(dot3(inv_out, cross, NT))
-            rows[...] = dot3(jnp.concatenate(parts, axis=0), inv_in, NN) * scaling
-            even, odd = rows[pl.ds(0, width, 2), :], rows[pl.ds(1, width, 2), :]
-            both = jnp.concatenate([even, odd], axis=1)
-            out[slab] = both[: width // 2]
-            out[slabs + slab] = both[width // 2 :]
+            first, second = mine[slab, :width], other[slab, :width]
+            cross = jnp.concatenate([jnp.where(upper, second, first), jnp.where(upper, first, second)], axis=0)
+            both = dot3(dot3(inv_out, cross, NT), diagonal, NN)
+            even, odd = both[:half], both[half:]
+            out[slab] = jnp.where(left[:half], even, pltpu.roll(odd, width, 1)).astype(out.dtype)
+            out[slabs + slab] = jnp.where(left[:half], pltpu.roll(even, width, 1), odd).astype(out.dtype)
 
 
 def score(mine, other, queries, out):
     is_weight = lax.axis_index("tensor") == 1
     count, chunks, lanes = mine.shape
-    ones = jnp.ones((8, lanes), F32)
+    ones = jnp.ones((8, lanes), jnp.bfloat16)
+    blocks = [queries[:, lanes * m : lanes * (m + 1)].astype(F32) for m in range(chunks)]
     for s in range(count):
-        weights = jnp.where(is_weight, mine[s], other[s])
-        sums = jnp.zeros((queries.shape[0], lanes), F32)
-        for m in range(chunks):
-            sums = sums + queries[:, lanes * m : lanes * (m + 1)].astype(F32) * weights[m : m + 1]
-        total = lax.dot_general(ones, sums, NT, preferred_element_type=F32, precision=lax.Precision.HIGHEST)
+        weights = jnp.where(is_weight, mine[s], other[s]).astype(F32)
+        terms = [block * weights[m : m + 1] for m, block in enumerate(blocks)]
+        while len(terms) > 1:
+            terms = [x + y for x, y in zip(terms[::2], terms[1::2])]
+        sums = terms[0]
+        if sums.shape[0] == 1:
+            out[s : s + 1, :] = jnp.sum(sums, axis=1, keepdims=True)
+            continue
+        total = 0.0
+        for _ in range(3):
+            part = sums.astype(jnp.bfloat16)
+            sums = sums - part.astype(F32)
+            total = total + lax.dot_general(ones, part, NT, preferred_element_type=F32)
         out[s : s + 1, :] = total[:1]
 
 
@@ -206,7 +217,7 @@
 
 
 def exchange(array, distance, groups, devices):
-    near = distance if distance < 4 else 1
+    near = {1: 2, 2: 2, 3: 3}.get(distance, 1)
     pairs = []
     for chip in range(groups * devices):
         pairs.append((2 * chip, 2 * (chip ^ near)))
@@ -227,7 +238,7 @@
     seq_count = lengths.shape[0]
     inner, outer = inputs.shape[1], out_grads.shape[1]
     tile = 2 * tokens
-    spans = split(outer, inner, 2, 2 * tile) + split(0, outer, 3, tile)
+    spans = split(outer, inner, 1, 2 * tile) + split(0, outer, 3, tile)
     params = pltpu.CompilerParams(vmem_limit_bytes=16 << 20)
     partial_z = pl.pallas_call(
         functools.partial(project, spans),
@@ -271,10 +282,9 @@
     )(packed, other)
     weights = pl.pallas_call(
         functools.partial(weigh, scaling),
-        out_shape=jax.ShapeDtypeStruct((seq_count, width // 2, 2 * width), F32),
+        out_shape=jax.ShapeDtypeStruct((seq_count, width // 2, 2 * width), jnp.bfloat16),
         in_specs=[VMEM] * 3,
         out_specs=VMEM,
-        scratch_shapes=[pltpu.VMEM((2 * width, width), F32)],
         compiler_params=params,
         name="weigh",
     )(inverse, packed, other)

time: 18.7 us -> 18.6 us (level)
  waiting for transfers between devices: 9.27 us -> 7.6 us
  starting transfers between devices: 5.82 us -> 7.43 us
    ppermute x4, starting transfers between devices: 4.77 us -> 6.42 us  [exchange(): return lax.ppermute(array, ('groups', 'seq', 'tensor'), pairs)]
    ppermute x4, waiting for transfers between devices: 7.51 us -> 5.86 us  [exchange(): return lax.ppermute(array, ('groups', 'seq', 'tensor'), pairs)]
where the time goes in v7:
time: 18.6 us; the launch traced here: 18.5 us
  waiting for transfers between devices  7.6 us (41%)
  starting transfers between devices  7.43 us (40%)
  Pallas kernels  3.41 us (18%)
    ppermute x4, starting transfers between devices, exchange(): return lax.ppermute(array, ('groups', 'seq', 'tensor'), pairs)  6.42 us
    ppermute x4, waiting for transfers between devices, exchange(): return lax.ppermute(array, ('groups', 'seq', 'tensor'), pairs)  5.86 us
    pallas_call x1, Pallas kernels, shards(): pl.pallas_call(functools.partial(project, spans), out_shape=jax.ShapeDtyp...  2.64 us
    ppermute x2, waiting for transfers between devices, swap(): return lax.ppermute(array, 'tensor', [(0, 1), (1, 0)])  1.74 us
    ppermute x2, starting transfers between devices, swap(): return lax.ppermute(array, 'tensor', [(0, 1), (1, 0)])  1.01 us
    pallas_call x1, Pallas kernels, shards(): pl.pallas_call(score, out_shape=jax.ShapeDtypeStruct((seq_count, queries....  0.77 us
  transfers between devices with their start and end apart: 6, of which 6 were waited for; matrix products, arithmetic and copies ran while one was open for 0% of the time, Pallas kernels for 0%

profile of v7, /device:TPU:0, one launch (start us, length us, event | category | flops | bytes accessed | tf_op | source)
XLA Modules:
  0.0 18.5 jit_solution(1200788843637153619)
XLA Ops:
  0.0 0.0 copy-start
  0.0 2.6 %project.1.mine = f32[128,128]{1,0:T(8,128)S(1)} custom-call(s32[2]{0:T(128)} %lengths.1, bf16[128,7168]{1,0:T(8,128)(2,1)} %inputs.1, bf16[128,4096]{1,0:T(8,128)(2,1)} %grads.1, bf16[64,7168]{1,0:T(8,128)(2,1)} %bitcast.3, bf16[64,4096]{1,0:T(8,128)(2,1)} %bitcast.4), custom_call_target="tpu_custom_call" | custom-call | tf_op jit(solution)/shard_map/project/pallas_call | solution.py:243
  2.6 0.5 %collective-permute-start = (f32[128,128]{1,0:T(8,128)S(1)}, f32[128,128]{1,0:T(8,128)S(1)}, u32[]{:S(2)}, u32[]{:S(2)}) collective-permute-start(f32[128,128]{1,0:T(8,128)S(1)} %project.1.mine), channel_id=1, source_target_pairs={{0,1},{1,0},{2,3},{3,2},{4,5},{5,4},{6,7},{7,6},{8,9},{9,8},{10,11... | collective-permute-start | bytes 196616 | tf_op jit(solution)/shard_map/ppermute | solution.py:216
  3.2 0.9 %collective-permute-done.other = f32[128,128]{1,0:T(8,128)S(1)} collective-permute-done((f32[128,128]{1,0:T(8,128)S(1)}, f32[128,128]{1,0:T(8,128)S(1)}, u32[]{:S(2)}, u32[]{:S(2)}) %collective-permute-start) | collective-permute-done | bytes 65568 | tf_op jit(solution)/shard_map/ppermute | solution.py:216
  4.1 3.9 %collective-permute-start.3 = (f32[1,72,128]{2,1,0:T(8,128)S(1)}, f32[1,72,128]{2,1,0:T(8,128)S(1)}, u32[]{:S(2)}, u32[]{:S(2)}) collective-permute-start(f32[1,72,128]{2,1,0:T(8,128)S(1)} %moments.1), channel_id=1, source_target_pairs={{0,6},{1,7},{2,4},{3,5},{4,2},{5,3},{6,0},{7,1},{8,14},{9,15},{10,... | collective-permute-start | bytes 110600 | tf_op jit(solution)/shard_map/ppermute | solution.py:225
  7.9 0.4 %collective-permute-start.2 = (f32[1,72,128]{2,1,0:T(8,128)S(1)}, f32[1,72,128]{2,1,0:T(8,128)S(1)}, u32[]{:S(2)}, u32[]{:S(2)}) collective-permute-start(f32[1,72,128]{2,1,0:T(8,128)S(1)} %moments.1), channel_id=1, source_target_pairs={{0,4},{1,5},{2,6},{3,7},{4,0},{5,1},{6,2},{7,3},{8,12},{9,13},{10,... | collective-permute-start | bytes 110600 | tf_op jit(solution)/shard_map/ppermute | solution.py:225
  8.4 1.6 %collective-permute-start.1 = (f32[1,72,128]{2,1,0:T(8,128)S(1)}, f32[1,72,128]{2,1,0:T(8,128)S(1)}, u32[]{:S(2)}, u32[]{:S(2)}) collective-permute-start(f32[1,72,128]{2,1,0:T(8,128)S(1)} %moments.1), channel_id=1, source_target_pairs={{0,4},{1,3},{2,6},{3,1},{4,0},{5,7},{6,2},{7,5},{8,12},{9,11},{10,... | collective-permute-start | bytes 110600 | tf_op jit(solution)/shard_map/ppermute | solution.py:225
  10.0 0.1 collective-permute-done.3
  10.1 1.8 %collective-permute-done.2 = f32[1,72,128]{2,1,0:T(8,128)S(1)} collective-permute-done((f32[1,72,128]{2,1,0:T(8,128)S(1)}, f32[1,72,128]{2,1,0:T(8,128)S(1)}, u32[]{:S(2)}, u32[]{:S(2)}) %collective-permute-start.2) | collective-permute-done | bytes 36896 | tf_op jit(solution)/shard_map/ppermute | solution.py:225
  11.9 0.4 %collective-permute-done.1 = f32[1,72,128]{2,1,0:T(8,128)S(1)} collective-permute-done((f32[1,72,128]{2,1,0:T(8,128)S(1)}, f32[1,72,128]{2,1,0:T(8,128)S(1)}, u32[]{:S(2)}, u32[]{:S(2)}) %collective-permute-start.1) | collective-permute-done | bytes 36896 | tf_op jit(solution)/shard_map/ppermute | solution.py:225
  12.3 0.5 %collective-permute-start.4 = (f32[1,72,128]{2,1,0:T(8,128)S(1)}, f32[1,72,128]{2,1,0:T(8,128)S(1)}, u32[]{:S(2)}, u32[]{:S(2)}) collective-permute-start(f32[1,72,128]{2,1,0:T(8,128)S(1)} %add_add_fusion.mine), channel_id=1, source_target_pairs={{0,2},{1,9},{2,0},{3,11},{4,6},{5,13},{6,4},{7,15},{8,10},{9,1},{1... | collective-permute-start | bytes 110600 | tf_op jit(solution)/shard_map/ppermute | solution.py:225
  12.9 3.5 %collective-permute-done.4.other = f32[1,72,128]{2,1,0:T(8,128)S(1)} collective-permute-done((f32[1,72,128]{2,1,0:T(8,128)S(1)}, f32[1,72,128]{2,1,0:T(8,128)S(1)}, u32[]{:S(2)}, u32[]{:S(2)}) %collective-permute-start.4) | collective-permute-done | bytes 36896 | tf_op jit(solution)/shard_map/ppermute | solution.py:225
  16.4 0.5 %collective-permute-start.5 = (bf16[2,32,128]{2,1,0:T(8,128)(2,1)S(1)}, bf16[2,32,128]{2,1,0:T(8,128)(2,1)S(1)}, u32[]{:S(2)}, u32[]{:S(2)}) collective-permute-start(bf16[2,32,128]{2,1,0:T(8,128)(2,1)S(1)} %weigh.1.mine), channel_id=1, source_target_pairs={{0,1},{1,0},{2,3},{3,2},{4,5},{5,4},{6,7},{7,6},{8,9},{9,8},{10,11... | collective-permute-start | bytes 49160 | tf_op jit(solution)/shard_map/ppermute | solution.py:216
  16.9 0.8 %collective-permute-done.5.other = bf16[2,32,128]{2,1,0:T(8,128)(2,1)S(1)} collective-permute-done((bf16[2,32,128]{2,1,0:T(8,128)(2,1)S(1)}, bf16[2,32,128]{2,1,0:T(8,128)(2,1)S(1)}, u32[]{:S(2)}, u32[]{:S(2)}) %collective-permute-start.5) | collective-permute-done | bytes 16416 | tf_op jit(solution)/shard_map/ppermute | solution.py:216
  17.7 0.0 copy-done
  17.7 0.8 %score.1 = f32[2,16]{1,0:T(2,128)} custom-call(bf16[2,32,128]{2,1,0:T(8,128)(2,1)S(1)} %weigh.1.mine, bf16[2,32,128]{2,1,0:T(8,128)(2,1)S(1)} %collective-permute-done.5.other, bf16[16,4096]{1,0:T(8,128)(2,1)S(1)} %copy-done), custom_call_target="tpu_custom_call" | custom-call | tf_op jit(solution)/shard_map/score/pallas_call | solution.py:291
  (4 shorter events, 0.0 us)
Async XLA Ops:
  0.0 17.7 %copy-start = (bf16[16,4096]{1,0:T(8,128)(2,1)S(1)}, bf16[16,4096]{1,0:T(8,128)(2,1)}, u32[]{:S(2)}) copy-start(bf16[16,4096]{1,0:T(8,128)(2,1)} %queries.1) | copy-start | bytes 393220
  2.6 1.4 %collective-permute-start = (f32[128,128]{1,0:T(8,128)S(1)}, f32[128,128]{1,0:T(8,128)S(1)}, u32[]{:S(2)}, u32[]{:S(2)}) collective-permute-start(f32[128,128]{1,0:T(8,128)S(1)} %project.1.mine), channel_id=1, source_target_pairs={{0,1},{1,0},{2,3},{3,2},{4,5},{5,4},{6,7},{7,6},{8,9},{9,8},{10,11... | collective-permute-start | bytes 196616 | tf_op jit(solution)/shard_map/ppermute | solution.py:216
  4.1 6.0 %collective-permute-start.3 = (f32[1,72,128]{2,1,0:T(8,128)S(1)}, f32[1,72,128]{2,1,0:T(8,128)S(1)}, u32[]{:S(2)}, u32[]{:S(2)}) collective-permute-start(f32[1,72,128]{2,1,0:T(8,128)S(1)} %moments.1), channel_id=1, source_target_pairs={{0,6},{1,7},{2,4},{3,5},{4,2},{5,3},{6,0},{7,1},{8,14},{9,15},{10,... | collective-permute-start | bytes 110600 | tf_op jit(solution)/shard_map/ppermute | solution.py:225
  7.9 4.0 %collective-permute-start.2 = (f32[1,72,128]{2,1,0:T(8,128)S(1)}, f32[1,72,128]{2,1,0:T(8,128)S(1)}, u32[]{:S(2)}, u32[]{:S(2)}) collective-permute-start(f32[1,72,128]{2,1,0:T(8,128)S(1)} %moments.1), channel_id=1, source_target_pairs={{0,4},{1,5},{2,6},{3,7},{4,0},{5,1},{6,2},{7,3},{8,12},{9,13},{10,... | collective-permute-start | bytes 110600 | tf_op jit(solution)/shard_map/ppermute | solution.py:225
  8.4 4.0 %collective-permute-start.1 = (f32[1,72,128]{2,1,0:T(8,128)S(1)}, f32[1,72,128]{2,1,0:T(8,128)S(1)}, u32[]{:S(2)}, u32[]{:S(2)}) collective-permute-start(f32[1,72,128]{2,1,0:T(8,128)S(1)} %moments.1), channel_id=1, source_target_pairs={{0,4},{1,3},{2,6},{3,1},{4,0},{5,7},{6,2},{7,5},{8,12},{9,11},{10,... | collective-permute-start | bytes 110600 | tf_op jit(solution)/shard_map/ppermute | solution.py:225
  12.3 4.0 %collective-permute-start.4 = (f32[1,72,128]{2,1,0:T(8,128)S(1)}, f32[1,72,128]{2,1,0:T(8,128)S(1)}, u32[]{:S(2)}, u32[]{:S(2)}) collective-permute-start(f32[1,72,128]{2,1,0:T(8,128)S(1)} %add_add_fusion.mine), channel_id=1, source_target_pairs={{0,2},{1,9},{2,0},{3,11},{4,6},{5,13},{6,4},{7,15},{8,10},{9,1},{1... | collective-permute-start | bytes 110600 | tf_op jit(solution)/shard_map/ppermute | solution.py:225
  16.4 1.3 %collective-permute-start.5 = (bf16[2,32,128]{2,1,0:T(8,128)(2,1)S(1)}, bf16[2,32,128]{2,1,0:T(8,128)(2,1)S(1)}, u32[]{:S(2)}, u32[]{:S(2)}) collective-permute-start(bf16[2,32,128]{2,1,0:T(8,128)(2,1)S(1)} %weigh.1.mine), channel_id=1, source_target_pairs={{0,1},{1,0},{2,3},{3,2},{4,5},{5,4},{6,7},{7,6},{8,9},{9,8},{10,11... | collective-permute-start | bytes 49160 | tf_op jit(solution)/shard_map/ppermute | solution.py:216

commit v8 on v7

--- a/solution.py
+++ b/solution.py
@@ -24,7 +24,7 @@
     return list(zip(edges, edges[1:]))
 
 
-def project(spans, lengths, inputs, grads, proj_in, proj_out, out, buf, count, sems):
+def project(spans, lengths, inputs, grads, proj_in, proj_out, out, sent, buf, count, sems):
     width, tokens = proj_in.shape[0], inputs.shape[0]
     tile = 2 * tokens
     outer = grads.shape[1]
@@ -66,6 +66,7 @@
         )
         out[:width, :] = jnp.where(valid, x_left[:, :tokens] + x_right[:, tokens:], 0.0)
         out[width:, :] = jnp.where(valid, g_right[:, tokens:], 0.0)
+        sent[...] = out[...].astype(sent.dtype)
 
     pl.run_scoped(multiply, *(pltpu.ACC(mxu_id=unit)((width, tile), F32) for unit in (0, 1, 0, 1, 0, 1)))
 
@@ -85,8 +86,9 @@
 
     @pl.when(lax.axis_index("tensor") == 1)
     def _():
-        z = mine[...] + other[...]
-        square = dot3(z, z, NT)
+        z = mine[...] + other[...].astype(F32)
+        z = z.astype(jnp.bfloat16)
+        square = lax.dot_general(z, z, NT, preferred_element_type=F32)
         width = square.shape[0] // 2
         top, bottom = square[:width], pltpu.roll(square[width:], width, 1)
         row = lax.broadcasted_iota(jnp.int32, top.shape, 0)
@@ -240,11 +242,11 @@
     tile = 2 * tokens
     spans = split(outer, inner, 1, 2 * tile) + split(0, outer, 3, tile)
     params = pltpu.CompilerParams(vmem_limit_bytes=16 << 20)
-    partial_z = pl.pallas_call(
+    partial_z, sent = pl.pallas_call(
         functools.partial(project, spans),
-        out_shape=jax.ShapeDtypeStruct((2 * width, tokens), F32),
+        out_shape=[jax.ShapeDtypeStruct((2 * width, tokens), kind) for kind in (F32, jnp.bfloat16)],
         in_specs=[HBM] * 5,
-        out_specs=VMEM,
+        out_specs=[VMEM] * 2,
         scratch_shapes=[
             pltpu.VMEM((2 * (width + tokens), inner), inputs.dtype),
             pltpu.SMEM(lengths.shape, lengths.dtype),
@@ -253,7 +255,7 @@
         compiler_params=params,
         name="project",
     )(*map(stay, (lengths, inputs, out_grads, proj_in.T, proj_out.T)))
-    packed_rows = width + 8
+    packed_rows = width + 1
     packed = pl.pallas_call(
         moments,
         out_shape=jax.ShapeDtypeStruct((1, packed_rows, 2 * width), F32),
@@ -261,7 +263,7 @@
         out_specs=VMEM,
         compiler_params=params,
         name="moments",
-    )(partial_z, swap(partial_z))
+    )(partial_z, swap(sent))
     groups, devices = lax.axis_size("groups"), lax.axis_size("seq")
     holders = devices // seq_count
     packed = packed + sum(exchange(packed, near, groups, devices) for near in range(1, holders))

time: 18.6 us -> 18.5 us (level)
  no operation moved by 1% of the time
where the time goes in v8:
time: 18.5 us; the launch traced here: 18.4 us
  waiting for transfers between devices  7.56 us (41%)
  starting transfers between devices  7.4 us (40%)
  Pallas kernels  3.41 us (18%)
    ppermute x4, starting transfers between devices, exchange(): return lax.ppermute(array, ('groups', 'seq', 'tensor'), pairs)  6.42 us
    ppermute x4, waiting for transfers between devices, exchange(): return lax.ppermute(array, ('groups', 'seq', 'tensor'), pairs)  5.86 us
    pallas_call x1, Pallas kernels, shards(): pl.pallas_call(functools.partial(project, spans), out_shape=[jax.ShapeDty...  2.64 us
    ppermute x2, waiting for transfers between devices, swap(): return lax.ppermute(array, 'tensor', [(0, 1), (1, 0)])  1.7 us
    ppermute x2, starting transfers between devices, swap(): return lax.ppermute(array, 'tensor', [(0, 1), (1, 0)])  0.98 us
    pallas_call x1, Pallas kernels, shards(): pl.pallas_call(score, out_shape=jax.ShapeDtypeStruct((seq_count, queries....  0.77 us
  transfers between devices with their start and end apart: 6, of which 6 were waited for; matrix products, arithmetic and copies ran while one was open for 0% of the time, Pallas kernels for 0%

profile of v8, /device:TPU:0, one launch (start us, length us, event | category | flops | bytes accessed | tf_op | source)
XLA Modules:
  0.0 18.4 jit_solution(15781193083847833115)
XLA Ops:
  0.0 0.0 copy-start
  0.0 2.6 %project.1 = (f32[128,128]{1,0:T(8,128)S(1)}, bf16[128,128]{1,0:T(8,128)(2,1)S(1)}) custom-call(s32[2]{0:T(128)} %lengths.1, bf16[128,7168]{1,0:T(8,128)(2,1)} %inputs.1, bf16[128,4096]{1,0:T(8,128)(2,1)} %grads.1, bf16[64,7168]{1,0:T(8,128)(2,1)} %bitcast.3, bf16[64,4096]{1,0:T(8,128)(2,1)} %bitcast.4), custom_call_target="tpu_custom_call" | custom-call | tf_op jit(solution)/shard_map/project/pallas_call | solution.py:245
  2.6 0.5 %collective-permute-start = (bf16[128,128]{1,0:T(8,128)(2,1)S(1)}, bf16[128,128]{1,0:T(8,128)(2,1)S(1)}, u32[]{:S(2)}, u32[]{:S(2)}) collective-permute-start(bf16[128,128]{1,0:T(8,128)(2,1)S(1)} %get-tuple-element.8), channel_id=1, source_target_pairs={{0,1},{1,0},{2,3},{3,2},{4,5},{5,4},{6,7},{7,6},{8,9},{9,8},{10,11... | collective-permute-start | bytes 98312 | tf_op jit(solution)/shard_map/ppermute | solution.py:218
  3.2 0.9 %collective-permute-done.other = bf16[128,128]{1,0:T(8,128)(2,1)S(1)} collective-permute-done((bf16[128,128]{1,0:T(8,128)(2,1)S(1)}, bf16[128,128]{1,0:T(8,128)(2,1)S(1)}, u32[]{:S(2)}, u32[]{:S(2)}) %collective-permute-start) | collective-permute-done | bytes 32800 | tf_op jit(solution)/shard_map/ppermute | solution.py:218
  4.0 3.8 %collective-permute-start.3 = (f32[1,65,128]{2,1,0:T(8,128)S(1)}, f32[1,65,128]{2,1,0:T(8,128)S(1)}, u32[]{:S(2)}, u32[]{:S(2)}) collective-permute-start(f32[1,65,128]{2,1,0:T(8,128)S(1)} %moments.1), channel_id=1, source_target_pairs={{0,6},{1,7},{2,4},{3,5},{4,2},{5,3},{6,0},{7,1},{8,14},{9,15},{10,... | collective-permute-start | bytes 99848 | tf_op jit(solution)/shard_map/ppermute | solution.py:227
  7.9 0.4 %collective-permute-start.2 = (f32[1,65,128]{2,1,0:T(8,128)S(1)}, f32[1,65,128]{2,1,0:T(8,128)S(1)}, u32[]{:S(2)}, u32[]{:S(2)}) collective-permute-start(f32[1,65,128]{2,1,0:T(8,128)S(1)} %moments.1), channel_id=1, source_target_pairs={{0,4},{1,5},{2,6},{3,7},{4,0},{5,1},{6,2},{7,3},{8,12},{9,13},{10,... | collective-permute-start | bytes 99848 | tf_op jit(solution)/shard_map/ppermute | solution.py:227
  8.3 1.6 %collective-permute-start.1 = (f32[1,65,128]{2,1,0:T(8,128)S(1)}, f32[1,65,128]{2,1,0:T(8,128)S(1)}, u32[]{:S(2)}, u32[]{:S(2)}) collective-permute-start(f32[1,65,128]{2,1,0:T(8,128)S(1)} %moments.1), channel_id=1, source_target_pairs={{0,4},{1,3},{2,6},{3,1},{4,0},{5,7},{6,2},{7,5},{8,12},{9,11},{10,... | collective-permute-start | bytes 99848 | tf_op jit(solution)/shard_map/ppermute | solution.py:227
  9.9 0.1 collective-permute-done.3
  10.0 1.9 %collective-permute-done.2 = f32[1,65,128]{2,1,0:T(8,128)S(1)} collective-permute-done((f32[1,65,128]{2,1,0:T(8,128)S(1)}, f32[1,65,128]{2,1,0:T(8,128)S(1)}, u32[]{:S(2)}, u32[]{:S(2)}) %collective-permute-start.2) | collective-permute-done | bytes 33312 | tf_op jit(solution)/shard_map/ppermute | solution.py:227
  11.8 0.4 %collective-permute-done.1 = f32[1,65,128]{2,1,0:T(8,128)S(1)} collective-permute-done((f32[1,65,128]{2,1,0:T(8,128)S(1)}, f32[1,65,128]{2,1,0:T(8,128)S(1)}, u32[]{:S(2)}, u32[]{:S(2)}) %collective-permute-start.1) | collective-permute-done | bytes 33312 | tf_op jit(solution)/shard_map/ppermute | solution.py:227
  12.3 0.5 %collective-permute-start.4 = (f32[1,65,128]{2,1,0:T(8,128)S(1)}, f32[1,65,128]{2,1,0:T(8,128)S(1)}, u32[]{:S(2)}, u32[]{:S(2)}) collective-permute-start(f32[1,65,128]{2,1,0:T(8,128)S(1)} %add_add_fusion.mine), channel_id=1, source_target_pairs={{0,2},{1,9},{2,0},{3,11},{4,6},{5,13},{6,4},{7,15},{8,10},{9,1},{1... | collective-permute-start | bytes 99848 | tf_op jit(solution)/shard_map/ppermute | solution.py:227
  12.8 3.5 %collective-permute-done.4.other = f32[1,65,128]{2,1,0:T(8,128)S(1)} collective-permute-done((f32[1,65,128]{2,1,0:T(8,128)S(1)}, f32[1,65,128]{2,1,0:T(8,128)S(1)}, u32[]{:S(2)}, u32[]{:S(2)}) %collective-permute-start.4) | collective-permute-done | bytes 33312 | tf_op jit(solution)/shard_map/ppermute | solution.py:227
  16.3 0.5 %collective-permute-start.5 = (bf16[2,32,128]{2,1,0:T(8,128)(2,1)S(1)}, bf16[2,32,128]{2,1,0:T(8,128)(2,1)S(1)}, u32[]{:S(2)}, u32[]{:S(2)}) collective-permute-start(bf16[2,32,128]{2,1,0:T(8,128)(2,1)S(1)} %weigh.1.mine), channel_id=1, source_target_pairs={{0,1},{1,0},{2,3},{3,2},{4,5},{5,4},{6,7},{7,6},{8,9},{9,8},{10,11... | collective-permute-start | bytes 49160 | tf_op jit(solution)/shard_map/ppermute | solution.py:218
  16.8 0.8 %collective-permute-done.5.other = bf16[2,32,128]{2,1,0:T(8,128)(2,1)S(1)} collective-permute-done((bf16[2,32,128]{2,1,0:T(8,128)(2,1)S(1)}, bf16[2,32,128]{2,1,0:T(8,128)(2,1)S(1)}, u32[]{:S(2)}, u32[]{:S(2)}) %collective-permute-start.5) | collective-permute-done | bytes 16416 | tf_op jit(solution)/shard_map/ppermute | solution.py:218
  17.6 0.0 copy-done
  17.6 0.8 %score.1 = f32[2,16]{1,0:T(2,128)} custom-call(bf16[2,32,128]{2,1,0:T(8,128)(2,1)S(1)} %weigh.1.mine, bf16[2,32,128]{2,1,0:T(8,128)(2,1)S(1)} %collective-permute-done.5.other, bf16[16,4096]{1,0:T(8,128)(2,1)S(1)} %copy-done), custom_call_target="tpu_custom_call" | custom-call | tf_op jit(solution)/shard_map/score/pallas_call | solution.py:293
  (4 shorter events, 0.0 us)
Async XLA Ops:
  0.0 17.6 %copy-start = (bf16[16,4096]{1,0:T(8,128)(2,1)S(1)}, bf16[16,4096]{1,0:T(8,128)(2,1)}, u32[]{:S(2)}) copy-start(bf16[16,4096]{1,0:T(8,128)(2,1)} %queries.1) | copy-start | bytes 393220
  2.6 1.4 %collective-permute-start = (bf16[128,128]{1,0:T(8,128)(2,1)S(1)}, bf16[128,128]{1,0:T(8,128)(2,1)S(1)}, u32[]{:S(2)}, u32[]{:S(2)}) collective-permute-start(bf16[128,128]{1,0:T(8,128)(2,1)S(1)} %get-tuple-element.8), channel_id=1, source_target_pairs={{0,1},{1,0},{2,3},{3,2},{4,5},{5,4},{6,7},{7,6},{8,9},{9,8},{10,11... | collective-permute-start | bytes 98312 | tf_op jit(solution)/shard_map/ppermute | solution.py:218
  4.0 6.0 %collective-permute-start.3 = (f32[1,65,128]{2,1,0:T(8,128)S(1)}, f32[1,65,128]{2,1,0:T(8,128)S(1)}, u32[]{:S(2)}, u32[]{:S(2)}) collective-permute-start(f32[1,65,128]{2,1,0:T(8,128)S(1)} %moments.1), channel_id=1, source_target_pairs={{0,6},{1,7},{2,4},{3,5},{4,2},{5,3},{6,0},{7,1},{8,14},{9,15},{10,... | collective-permute-start | bytes 99848 | tf_op jit(solution)/shard_map/ppermute | solution.py:227
  7.9 4.0 %collective-permute-start.2 = (f32[1,65,128]{2,1,0:T(8,128)S(1)}, f32[1,65,128]{2,1,0:T(8,128)S(1)}, u32[]{:S(2)}, u32[]{:S(2)}) collective-permute-start(f32[1,65,128]{2,1,0:T(8,128)S(1)} %moments.1), channel_id=1, source_target_pairs={{0,4},{1,5},{2,6},{3,7},{4,0},{5,1},{6,2},{7,3},{8,12},{9,13},{10,... | collective-permute-start | bytes 99848 | tf_op jit(solution)/shard_map/ppermute | solution.py:227
  8.3 4.0 %collective-permute-start.1 = (f32[1,65,128]{2,1,0:T(8,128)S(1)}, f32[1,65,128]{2,1,0:T(8,128)S(1)}, u32[]{:S(2)}, u32[]{:S(2)}) collective-permute-start(f32[1,65,128]{2,1,0:T(8,128)S(1)} %moments.1), channel_id=1, source_target_pairs={{0,4},{1,3},{2,6},{3,1},{4,0},{5,7},{6,2},{7,5},{8,12},{9,11},{10,... | collective-permute-start | bytes 99848 | tf_op jit(solution)/shard_map/ppermute | solution.py:227
  12.3 4.0 %collective-permute-start.4 = (f32[1,65,128]{2,1,0:T(8,128)S(1)}, f32[1,65,128]{2,1,0:T(8,128)S(1)}, u32[]{:S(2)}, u32[]{:S(2)}) collective-permute-start(f32[1,65,128]{2,1,0:T(8,128)S(1)} %add_add_fusion.mine), channel_id=1, source_target_pairs={{0,2},{1,9},{2,0},{3,11},{4,6},{5,13},{6,4},{7,15},{8,10},{9,1},{1... | collective-permute-start | bytes 99848 | tf_op jit(solution)/shard_map/ppermute | solution.py:227
  16.3 1.3 %collective-permute-start.5 = (bf16[2,32,128]{2,1,0:T(8,128)(2,1)S(1)}, bf16[2,32,128]{2,1,0:T(8,128)(2,1)S(1)}, u32[]{:S(2)}, u32[]{:S(2)}) collective-permute-start(bf16[2,32,128]{2,1,0:T(8,128)(2,1)S(1)} %weigh.1.mine), channel_id=1, source_target_pairs={{0,1},{1,0},{2,3},{3,2},{4,5},{5,4},{6,7},{7,6},{8,9},{9,8},{10,11... | collective-permute-start | bytes 49160 | tf_op jit(solution)/shard_map/ppermute | solution.py:218

commit v9 on v8

--- a/solution.py
+++ b/solution.py
@@ -150,6 +150,11 @@
         return carry
 
     lax.fori_loop(0, width // PANEL, panel, 0)
+
+
+def solve(total, scaling, mine, other, out, inv):
+    inverses(total, mine, other, inv)
+    weigh(scaling, inv, mine, other, out)
 
 
 def inverses(total, mine, other, out):
@@ -274,22 +279,15 @@
     total = 3 * seq_count * LEN // 4
     scaling = 1.0 / (width * math.sqrt(LEN))
     other = exchange(packed, distance, groups, devices)
-    inverse = pl.pallas_call(
-        functools.partial(inverses, float(total)),
-        out_shape=jax.ShapeDtypeStruct((width, 2 * width), F32),
+    weights = pl.pallas_call(
+        functools.partial(solve, float(total), scaling),
+        out_shape=jax.ShapeDtypeStruct((seq_count, width // 2, 2 * width), jnp.bfloat16),
         in_specs=[VMEM] * 2,
         out_specs=VMEM,
+        scratch_shapes=[pltpu.VMEM((width, 2 * width), F32)],
         compiler_params=params,
-        name="inverses",
+        name="solve",
     )(packed, other)
-    weights = pl.pallas_call(
-        functools.partial(weigh, scaling),
-        out_shape=jax.ShapeDtypeStruct((seq_count, width // 2, 2 * width), jnp.bfloat16),
-        in_specs=[VMEM] * 3,
-        out_specs=VMEM,
-        compiler_params=params,
-        name="weigh",
-    )(inverse, packed, other)
     scores = pl.pallas_call(
         score,
         out_shape=jax.ShapeDtypeStruct((seq_count, queries.shape[0]), F32),

time: 18.5 us -> 18.5 us (level)
  no operation moved by 1% of the time
where the time goes in v9:
time: 18.5 us; the launch traced here: 18.4 us
  waiting for transfers between devices  7.56 us (41%)
  starting transfers between devices  7.38 us (40%)
  Pallas kernels  3.41 us (18%)
    ppermute x4, starting transfers between devices, exchange(): return lax.ppermute(array, ('groups', 'seq', 'tensor'), pairs)  6.42 us
    ppermute x4, waiting for transfers between devices, exchange(): return lax.ppermute(array, ('groups', 'seq', 'tensor'), pairs)  5.86 us
    pallas_call x1, Pallas kernels, shards(): pl.pallas_call(functools.partial(project, spans), out_shape=[jax.ShapeDty...  2.64 us
    ppermute x2, waiting for transfers between devices, swap(): return lax.ppermute(array, 'tensor', [(0, 1), (1, 0)])  1.7 us
    ppermute x2, starting transfers between devices, swap(): return lax.ppermute(array, 'tensor', [(0, 1), (1, 0)])  0.96 us
    pallas_call x1, Pallas kernels, shards(): pl.pallas_call(score, out_shape=jax.ShapeDtypeStruct((seq_count, queries....  0.77 us
  transfers between devices with their start and end apart: 6, of which 6 were waited for; matrix products, arithmetic and copies ran while one was open for 0% of the time, Pallas kernels for 0%

profile of v9, /device:TPU:0, one launch (start us, length us, event | category | flops | bytes accessed | tf_op | source)
XLA Modules:
  0.0 18.4 jit_solution(11727643888579229251)
XLA Ops:
  0.0 0.0 copy-start
  0.0 2.6 %project.1 = (f32[128,128]{1,0:T(8,128)S(1)}, bf16[128,128]{1,0:T(8,128)(2,1)S(1)}) custom-call(s32[2]{0:T(128)} %lengths.1, bf16[128,7168]{1,0:T(8,128)(2,1)} %inputs.1, bf16[128,4096]{1,0:T(8,128)(2,1)} %grads.1, bf16[64,7168]{1,0:T(8,128)(2,1)} %bitcast.3, bf16[64,4096]{1,0:T(8,128)(2,1)} %bitcast.4), custom_call_target="tpu_custom_call" | custom-call | tf_op jit(solution)/shard_map/project/pallas_call | solution.py:250
  2.6 0.5 %collective-permute-start = (bf16[128,128]{1,0:T(8,128)(2,1)S(1)}, bf16[128,128]{1,0:T(8,128)(2,1)S(1)}, u32[]{:S(2)}, u32[]{:S(2)}) collective-permute-start(bf16[128,128]{1,0:T(8,128)(2,1)S(1)} %get-tuple-element.8), channel_id=1, source_target_pairs={{0,1},{1,0},{2,3},{3,2},{4,5},{5,4},{6,7},{7,6},{8,9},{9,8},{10,11... | collective-permute-start | bytes 98312 | tf_op jit(solution)/shard_map/ppermute | solution.py:223
  3.2 0.9 %collective-permute-done.other = bf16[128,128]{1,0:T(8,128)(2,1)S(1)} collective-permute-done((bf16[128,128]{1,0:T(8,128)(2,1)S(1)}, bf16[128,128]{1,0:T(8,128)(2,1)S(1)}, u32[]{:S(2)}, u32[]{:S(2)}) %collective-permute-start) | collective-permute-done | bytes 32800 | tf_op jit(solution)/shard_map/ppermute | solution.py:223
  4.0 3.8 %collective-permute-start.3 = (f32[1,65,128]{2,1,0:T(8,128)S(1)}, f32[1,65,128]{2,1,0:T(8,128)S(1)}, u32[]{:S(2)}, u32[]{:S(2)}) collective-permute-start(f32[1,65,128]{2,1,0:T(8,128)S(1)} %moments.1), channel_id=1, source_target_pairs={{0,6},{1,7},{2,4},{3,5},{4,2},{5,3},{6,0},{7,1},{8,14},{9,15},{10,... | collective-permute-start | bytes 99848 | tf_op jit(solution)/shard_map/ppermute | solution.py:232
  7.9 0.4 %collective-permute-start.2 = (f32[1,65,128]{2,1,0:T(8,128)S(1)}, f32[1,65,128]{2,1,0:T(8,128)S(1)}, u32[]{:S(2)}, u32[]{:S(2)}) collective-permute-start(f32[1,65,128]{2,1,0:T(8,128)S(1)} %moments.1), channel_id=1, source_target_pairs={{0,4},{1,5},{2,6},{3,7},{4,0},{5,1},{6,2},{7,3},{8,12},{9,13},{10,... | collective-permute-start | bytes 99848 | tf_op jit(solution)/shard_map/ppermute | solution.py:232
  8.3 1.6 %collective-permute-start.1 = (f32[1,65,128]{2,1,0:T(8,128)S(1)}, f32[1,65,128]{2,1,0:T(8,128)S(1)}, u32[]{:S(2)}, u32[]{:S(2)}) collective-permute-start(f32[1,65,128]{2,1,0:T(8,128)S(1)} %moments.1), channel_id=1, source_target_pairs={{0,4},{1,3},{2,6},{3,1},{4,0},{5,7},{6,2},{7,5},{8,12},{9,11},{10,... | collective-permute-start | bytes 99848 | tf_op jit(solution)/shard_map/ppermute | solution.py:232
  9.9 0.1 collective-permute-done.3
  10.0 1.9 %collective-permute-done.2 = f32[1,65,128]{2,1,0:T(8,128)S(1)} collective-permute-done((f32[1,65,128]{2,1,0:T(8,128)S(1)}, f32[1,65,128]{2,1,0:T(8,128)S(1)}, u32[]{:S(2)}, u32[]{:S(2)}) %collective-permute-start.2) | collective-permute-done | bytes 33312 | tf_op jit(solution)/shard_map/ppermute | solution.py:232
  11.8 0.4 %collective-permute-done.1 = f32[1,65,128]{2,1,0:T(8,128)S(1)} collective-permute-done((f32[1,65,128]{2,1,0:T(8,128)S(1)}, f32[1,65,128]{2,1,0:T(8,128)S(1)}, u32[]{:S(2)}, u32[]{:S(2)}) %collective-permute-start.1) | collective-permute-done | bytes 33312 | tf_op jit(solution)/shard_map/ppermute | solution.py:232
  12.3 0.5 %collective-permute-start.4 = (f32[1,65,128]{2,1,0:T(8,128)S(1)}, f32[1,65,128]{2,1,0:T(8,128)S(1)}, u32[]{:S(2)}, u32[]{:S(2)}) collective-permute-start(f32[1,65,128]{2,1,0:T(8,128)S(1)} %add_add_fusion.mine), channel_id=1, source_target_pairs={{0,2},{1,9},{2,0},{3,11},{4,6},{5,13},{6,4},{7,15},{8,10},{9,1},{1... | collective-permute-start | bytes 99848 | tf_op jit(solution)/shard_map/ppermute | solution.py:232
  12.8 3.5 %collective-permute-done.4.other = f32[1,65,128]{2,1,0:T(8,128)S(1)} collective-permute-done((f32[1,65,128]{2,1,0:T(8,128)S(1)}, f32[1,65,128]{2,1,0:T(8,128)S(1)}, u32[]{:S(2)}, u32[]{:S(2)}) %collective-permute-start.4) | collective-permute-done | bytes 33312 | tf_op jit(solution)/shard_map/ppermute | solution.py:232
  16.3 0.4 %collective-permute-start.5 = (bf16[2,32,128]{2,1,0:T(8,128)(2,1)S(1)}, bf16[2,32,128]{2,1,0:T(8,128)(2,1)S(1)}, u32[]{:S(2)}, u32[]{:S(2)}) collective-permute-start(bf16[2,32,128]{2,1,0:T(8,128)(2,1)S(1)} %solve.1.mine), channel_id=1, source_target_pairs={{0,1},{1,0},{2,3},{3,2},{4,5},{5,4},{6,7},{7,6},{8,9},{9,8},{10,11... | collective-permute-start | bytes 49160 | tf_op jit(solution)/shard_map/ppermute | solution.py:223
  16.8 0.8 %collective-permute-done.5.other = bf16[2,32,128]{2,1,0:T(8,128)(2,1)S(1)} collective-permute-done((bf16[2,32,128]{2,1,0:T(8,128)(2,1)S(1)}, bf16[2,32,128]{2,1,0:T(8,128)(2,1)S(1)}, u32[]{:S(2)}, u32[]{:S(2)}) %collective-permute-start.5) | collective-permute-done | bytes 16416 | tf_op jit(solution)/shard_map/ppermute | solution.py:223
  17.6 0.0 copy-done
  17.6 0.8 %score.1 = f32[2,16]{1,0:T(2,128)} custom-call(bf16[2,32,128]{2,1,0:T(8,128)(2,1)S(1)} %solve.1.mine, bf16[2,32,128]{2,1,0:T(8,128)(2,1)S(1)} %collective-permute-done.5.other, bf16[16,4096]{1,0:T(8,128)(2,1)S(1)} %copy-done), custom_call_target="tpu_custom_call" | custom-call | tf_op jit(solution)/shard_map/score/pallas_call | solution.py:291
  (3 shorter events, 0.0 us)
Async XLA Ops:
  0.0 17.6 %copy-start = (bf16[16,4096]{1,0:T(8,128)(2,1)S(1)}, bf16[16,4096]{1,0:T(8,128)(2,1)}, u32[]{:S(2)}) copy-start(bf16[16,4096]{1,0:T(8,128)(2,1)} %queries.1) | copy-start | bytes 393220
  2.6 1.4 %collective-permute-start = (bf16[128,128]{1,0:T(8,128)(2,1)S(1)}, bf16[128,128]{1,0:T(8,128)(2,1)S(1)}, u32[]{:S(2)}, u32[]{:S(2)}) collective-permute-start(bf16[128,128]{1,0:T(8,128)(2,1)S(1)} %get-tuple-element.8), channel_id=1, source_target_pairs={{0,1},{1,0},{2,3},{3,2},{4,5},{5,4},{6,7},{7,6},{8,9},{9,8},{10,11... | collective-permute-start | bytes 98312 | tf_op jit(solution)/shard_map/ppermute | solution.py:223
  4.0 6.0 %collective-permute-start.3 = (f32[1,65,128]{2,1,0:T(8,128)S(1)}, f32[1,65,128]{2,1,0:T(8,128)S(1)}, u32[]{:S(2)}, u32[]{:S(2)}) collective-permute-start(f32[1,65,128]{2,1,0:T(8,128)S(1)} %moments.1), channel_id=1, source_target_pairs={{0,6},{1,7},{2,4},{3,5},{4,2},{5,3},{6,0},{7,1},{8,14},{9,15},{10,... | collective-permute-start | bytes 99848 | tf_op jit(solution)/shard_map/ppermute | solution.py:232
  7.9 4.0 %collective-permute-start.2 = (f32[1,65,128]{2,1,0:T(8,128)S(1)}, f32[1,65,128]{2,1,0:T(8,128)S(1)}, u32[]{:S(2)}, u32[]{:S(2)}) collective-permute-start(f32[1,65,128]{2,1,0:T(8,128)S(1)} %moments.1), channel_id=1, source_target_pairs={{0,4},{1,5},{2,6},{3,7},{4,0},{5,1},{6,2},{7,3},{8,12},{9,13},{10,... | collective-permute-start | bytes 99848 | tf_op jit(solution)/shard_map/ppermute | solution.py:232
  8.3 4.0 %collective-permute-start.1 = (f32[1,65,128]{2,1,0:T(8,128)S(1)}, f32[1,65,128]{2,1,0:T(8,128)S(1)}, u32[]{:S(2)}, u32[]{:S(2)}) collective-permute-start(f32[1,65,128]{2,1,0:T(8,128)S(1)} %moments.1), channel_id=1, source_target_pairs={{0,4},{1,3},{2,6},{3,1},{4,0},{5,7},{6,2},{7,5},{8,12},{9,11},{10,... | collective-permute-start | bytes 99848 | tf_op jit(solution)/shard_map/ppermute | solution.py:232
  12.3 4.0 %collective-permute-start.4 = (f32[1,65,128]{2,1,0:T(8,128)S(1)}, f32[1,65,128]{2,1,0:T(8,128)S(1)}, u32[]{:S(2)}, u32[]{:S(2)}) collective-permute-start(f32[1,65,128]{2,1,0:T(8,128)S(1)} %add_add_fusion.mine), channel_id=1, source_target_pairs={{0,2},{1,9},{2,0},{3,11},{4,6},{5,13},{6,4},{7,15},{8,10},{9,1},{1... | collective-permute-start | bytes 99848 | tf_op jit(solution)/shard_map/ppermute | solution.py:232
  16.3 1.3 %collective-permute-start.5 = (bf16[2,32,128]{2,1,0:T(8,128)(2,1)S(1)}, bf16[2,32,128]{2,1,0:T(8,128)(2,1)S(1)}, u32[]{:S(2)}, u32[]{:S(2)}) collective-permute-start(bf16[2,32,128]{2,1,0:T(8,128)(2,1)S(1)} %solve.1.mine), channel_id=1, source_target_pairs={{0,1},{1,0},{2,3},{3,2},{4,5},{5,4},{6,7},{7,6},{8,9},{9,8},{10,11... | collective-permute-start | bytes 49160 | tf_op jit(solution)/shard_map/ppermute | solution.py:223

commit v10 on v8

--- a/solution.py
+++ b/solution.py
@@ -203,7 +203,7 @@
             out[s : s + 1, :] = jnp.sum(sums, axis=1, keepdims=True)
             continue
         total = 0.0
-        for _ in range(3):
+        for _ in range(2):
             part = sums.astype(jnp.bfloat16)
             sums = sums - part.astype(F32)
             total = total + lax.dot_general(ones, part, NT, preferred_element_type=F32)

time: 18.5 us -> 18.5 us (level)
  no operation moved by 1% of the time
where the time goes in v10:
time: 18.5 us; the launch traced here: 18.4 us
  waiting for transfers between devices  7.56 us (41%)
  starting transfers between devices  7.4 us (40%)
  Pallas kernels  3.41 us (18%)
    ppermute x4, starting transfers between devices, exchange(): return lax.ppermute(array, ('groups', 'seq', 'tensor'), pairs)  6.42 us
    ppermute x4, waiting for transfers between devices, exchange(): return lax.ppermute(array, ('groups', 'seq', 'tensor'), pairs)  5.86 us
    pallas_call x1, Pallas kernels, shards(): pl.pallas_call(functools.partial(project, spans), out_shape=[jax.ShapeDty...  2.64 us
    ppermute x2, waiting for transfers between devices, swap(): return lax.ppermute(array, 'tensor', [(0, 1), (1, 0)])  1.7 us
    ppermute x2, starting transfers between devices, swap(): return lax.ppermute(array, 'tensor', [(0, 1), (1, 0)])  0.98 us
    pallas_call x1, Pallas kernels, shards(): pl.pallas_call(score, out_shape=jax.ShapeDtypeStruct((seq_count, queries....  0.76 us
  transfers between devices with their start and end apart: 6, of which 6 were waited for; matrix products, arithmetic and copies ran while one was open for 0% of the time, Pallas kernels for 0%

profile of v10, /device:TPU:0, one launch (start us, length us, event | category | flops | bytes accessed | tf_op | source)
XLA Modules:
  0.0 18.4 jit_solution(16937954478937027613)
XLA Ops:
  0.0 0.0 copy-start
  0.0 2.6 %project.1 = (f32[128,128]{1,0:T(8,128)S(1)}, bf16[128,128]{1,0:T(8,128)(2,1)S(1)}) custom-call(s32[2]{0:T(128)} %lengths.1, bf16[128,7168]{1,0:T(8,128)(2,1)} %inputs.1, bf16[128,4096]{1,0:T(8,128)(2,1)} %grads.1, bf16[64,7168]{1,0:T(8,128)(2,1)} %bitcast.3, bf16[64,4096]{1,0:T(8,128)(2,1)} %bitcast.4), custom_call_target="tpu_custom_call" | custom-call | tf_op jit(solution)/shard_map/project/pallas_call | solution.py:245
  2.6 0.5 %collective-permute-start = (bf16[128,128]{1,0:T(8,128)(2,1)S(1)}, bf16[128,128]{1,0:T(8,128)(2,1)S(1)}, u32[]{:S(2)}, u32[]{:S(2)}) collective-permute-start(bf16[128,128]{1,0:T(8,128)(2,1)S(1)} %get-tuple-element.8), channel_id=1, source_target_pairs={{0,1},{1,0},{2,3},{3,2},{4,5},{5,4},{6,7},{7,6},{8,9},{9,8},{10,11... | collective-permute-start | bytes 98312 | tf_op jit(solution)/shard_map/ppermute | solution.py:218
  3.2 0.9 %collective-permute-done.other = bf16[128,128]{1,0:T(8,128)(2,1)S(1)} collective-permute-done((bf16[128,128]{1,0:T(8,128)(2,1)S(1)}, bf16[128,128]{1,0:T(8,128)(2,1)S(1)}, u32[]{:S(2)}, u32[]{:S(2)}) %collective-permute-start) | collective-permute-done | bytes 32800 | tf_op jit(solution)/shard_map/ppermute | solution.py:218
  4.0 3.8 %collective-permute-start.3 = (f32[1,65,128]{2,1,0:T(8,128)S(1)}, f32[1,65,128]{2,1,0:T(8,128)S(1)}, u32[]{:S(2)}, u32[]{:S(2)}) collective-permute-start(f32[1,65,128]{2,1,0:T(8,128)S(1)} %moments.1), channel_id=1, source_target_pairs={{0,6},{1,7},{2,4},{3,5},{4,2},{5,3},{6,0},{7,1},{8,14},{9,15},{10,... | collective-permute-start | bytes 99848 | tf_op jit(solution)/shard_map/ppermute | solution.py:227
  7.9 0.4 %collective-permute-start.2 = (f32[1,65,128]{2,1,0:T(8,128)S(1)}, f32[1,65,128]{2,1,0:T(8,128)S(1)}, u32[]{:S(2)}, u32[]{:S(2)}) collective-permute-start(f32[1,65,128]{2,1,0:T(8,128)S(1)} %moments.1), channel_id=1, source_target_pairs={{0,4},{1,5},{2,6},{3,7},{4,0},{5,1},{6,2},{7,3},{8,12},{9,13},{10,... | collective-permute-start | bytes 99848 | tf_op jit(solution)/shard_map/ppermute | solution.py:227
  8.3 1.6 %collective-permute-start.1 = (f32[1,65,128]{2,1,0:T(8,128)S(1)}, f32[1,65,128]{2,1,0:T(8,128)S(1)}, u32[]{:S(2)}, u32[]{:S(2)}) collective-permute-start(f32[1,65,128]{2,1,0:T(8,128)S(1)} %moments.1), channel_id=1, source_target_pairs={{0,4},{1,3},{2,6},{3,1},{4,0},{5,7},{6,2},{7,5},{8,12},{9,11},{10,... | collective-permute-start | bytes 99848 | tf_op jit(solution)/shard_map/ppermute | solution.py:227
  9.9 0.1 collective-permute-done.3
  10.0 1.9 %collective-permute-done.2 = f32[1,65,128]{2,1,0:T(8,128)S(1)} collective-permute-done((f32[1,65,128]{2,1,0:T(8,128)S(1)}, f32[1,65,128]{2,1,0:T(8,128)S(1)}, u32[]{:S(2)}, u32[]{:S(2)}) %collective-permute-start.2) | collective-permute-done | bytes 33312 | tf_op jit(solution)/shard_map/ppermute | solution.py:227
  11.8 0.4 %collective-permute-done.1 = f32[1,65,128]{2,1,0:T(8,128)S(1)} collective-permute-done((f32[1,65,128]{2,1,0:T(8,128)S(1)}, f32[1,65,128]{2,1,0:T(8,128)S(1)}, u32[]{:S(2)}, u32[]{:S(2)}) %collective-permute-start.1) | collective-permute-done | bytes 33312 | tf_op jit(solution)/shard_map/ppermute | solution.py:227
  12.3 0.5 %collective-permute-start.4 = (f32[1,65,128]{2,1,0:T(8,128)S(1)}, f32[1,65,128]{2,1,0:T(8,128)S(1)}, u32[]{:S(2)}, u32[]{:S(2)}) collective-permute-start(f32[1,65,128]{2,1,0:T(8,128)S(1)} %add_add_fusion.mine), channel_id=1, source_target_pairs={{0,2},{1,9},{2,0},{3,11},{4,6},{5,13},{6,4},{7,15},{8,10},{9,1},{1... | collective-permute-start | bytes 99848 | tf_op jit(solution)/shard_map/ppermute | solution.py:227
  12.8 3.5 %collective-permute-done.4.other = f32[1,65,128]{2,1,0:T(8,128)S(1)} collective-permute-done((f32[1,65,128]{2,1,0:T(8,128)S(1)}, f32[1,65,128]{2,1,0:T(8,128)S(1)}, u32[]{:S(2)}, u32[]{:S(2)}) %collective-permute-start.4) | collective-permute-done | bytes 33312 | tf_op jit(solution)/shard_map/ppermute | solution.py:227
  16.3 0.5 %collective-permute-start.5 = (bf16[2,32,128]{2,1,0:T(8,128)(2,1)S(1)}, bf16[2,32,128]{2,1,0:T(8,128)(2,1)S(1)}, u32[]{:S(2)}, u32[]{:S(2)}) collective-permute-start(bf16[2,32,128]{2,1,0:T(8,128)(2,1)S(1)} %weigh.1.mine), channel_id=1, source_target_pairs={{0,1},{1,0},{2,3},{3,2},{4,5},{5,4},{6,7},{7,6},{8,9},{9,8},{10,11... | collective-permute-start | bytes 49160 | tf_op jit(solution)/shard_map/ppermute | solution.py:218
  16.8 0.8 %collective-permute-done.5.other = bf16[2,32,128]{2,1,0:T(8,128)(2,1)S(1)} collective-permute-done((bf16[2,32,128]{2,1,0:T(8,128)(2,1)S(1)}, bf16[2,32,128]{2,1,0:T(8,128)(2,1)S(1)}, u32[]{:S(2)}, u32[]{:S(2)}) %collective-permute-start.5) | collective-permute-done | bytes 16416 | tf_op jit(solution)/shard_map/ppermute | solution.py:218
  17.6 0.0 copy-done
  17.6 0.8 %score.1 = f32[2,16]{1,0:T(2,128)} custom-call(bf16[2,32,128]{2,1,0:T(8,128)(2,1)S(1)} %weigh.1.mine, bf16[2,32,128]{2,1,0:T(8,128)(2,1)S(1)} %collective-permute-done.5.other, bf16[16,4096]{1,0:T(8,128)(2,1)S(1)} %copy-done), custom_call_target="tpu_custom_call" | custom-call | tf_op jit(solution)/shard_map/score/pallas_call | solution.py:293
  (4 shorter events, 0.0 us)
Async XLA Ops:
  0.0 17.6 %copy-start = (bf16[16,4096]{1,0:T(8,128)(2,1)S(1)}, bf16[16,4096]{1,0:T(8,128)(2,1)}, u32[]{:S(2)}) copy-start(bf16[16,4096]{1,0:T(8,128)(2,1)} %queries.1) | copy-start | bytes 393220
  2.6 1.4 %collective-permute-start = (bf16[128,128]{1,0:T(8,128)(2,1)S(1)}, bf16[128,128]{1,0:T(8,128)(2,1)S(1)}, u32[]{:S(2)}, u32[]{:S(2)}) collective-permute-start(bf16[128,128]{1,0:T(8,128)(2,1)S(1)} %get-tuple-element.8), channel_id=1, source_target_pairs={{0,1},{1,0},{2,3},{3,2},{4,5},{5,4},{6,7},{7,6},{8,9},{9,8},{10,11... | collective-permute-start | bytes 98312 | tf_op jit(solution)/shard_map/ppermute | solution.py:218
  4.0 6.0 %collective-permute-start.3 = (f32[1,65,128]{2,1,0:T(8,128)S(1)}, f32[1,65,128]{2,1,0:T(8,128)S(1)}, u32[]{:S(2)}, u32[]{:S(2)}) collective-permute-start(f32[1,65,128]{2,1,0:T(8,128)S(1)} %moments.1), channel_id=1, source_target_pairs={{0,6},{1,7},{2,4},{3,5},{4,2},{5,3},{6,0},{7,1},{8,14},{9,15},{10,... | collective-permute-start | bytes 99848 | tf_op jit(solution)/shard_map/ppermute | solution.py:227
  7.9 4.0 %collective-permute-start.2 = (f32[1,65,128]{2,1,0:T(8,128)S(1)}, f32[1,65,128]{2,1,0:T(8,128)S(1)}, u32[]{:S(2)}, u32[]{:S(2)}) collective-permute-start(f32[1,65,128]{2,1,0:T(8,128)S(1)} %moments.1), channel_id=1, source_target_pairs={{0,4},{1,5},{2,6},{3,7},{4,0},{5,1},{6,2},{7,3},{8,12},{9,13},{10,... | collective-permute-start | bytes 99848 | tf_op jit(solution)/shard_map/ppermute | solution.py:227
  8.3 4.0 %collective-permute-start.1 = (f32[1,65,128]{2,1,0:T(8,128)S(1)}, f32[1,65,128]{2,1,0:T(8,128)S(1)}, u32[]{:S(2)}, u32[]{:S(2)}) collective-permute-start(f32[1,65,128]{2,1,0:T(8,128)S(1)} %moments.1), channel_id=1, source_target_pairs={{0,4},{1,3},{2,6},{3,1},{4,0},{5,7},{6,2},{7,5},{8,12},{9,11},{10,... | collective-permute-start | bytes 99848 | tf_op jit(solution)/shard_map/ppermute | solution.py:227
  12.3 4.0 %collective-permute-start.4 = (f32[1,65,128]{2,1,0:T(8,128)S(1)}, f32[1,65,128]{2,1,0:T(8,128)S(1)}, u32[]{:S(2)}, u32[]{:S(2)}) collective-permute-start(f32[1,65,128]{2,1,0:T(8,128)S(1)} %add_add_fusion.mine), channel_id=1, source_target_pairs={{0,2},{1,9},{2,0},{3,11},{4,6},{5,13},{6,4},{7,15},{8,10},{9,1},{1... | collective-permute-start | bytes 99848 | tf_op jit(solution)/shard_map/ppermute | solution.py:227
  16.3 1.3 %collective-permute-start.5 = (bf16[2,32,128]{2,1,0:T(8,128)(2,1)S(1)}, bf16[2,32,128]{2,1,0:T(8,128)(2,1)S(1)}, u32[]{:S(2)}, u32[]{:S(2)}) collective-permute-start(bf16[2,32,128]{2,1,0:T(8,128)(2,1)S(1)} %weigh.1.mine), channel_id=1, source_target_pairs={{0,1},{1,0},{2,3},{3,2},{4,5},{5,4},{6,7},{7,6},{8,9},{9,8},{10,11... | collective-permute-start | bytes 49160 | tf_op jit(solution)/shard_map/ppermute | solution.py:218

commit v11 on v8

--- a/solution.py
+++ b/solution.py
@@ -219,7 +219,7 @@
 
 
 def exchange(array, distance, groups, devices):
-    near = {1: 2, 2: 2, 3: 3}.get(distance, 1)
+    near = {1: devices, 2: devices, 3: 2}.get(distance, 1)
     pairs = []
     for chip in range(groups * devices):
         pairs.append((2 * chip, 2 * (chip ^ near)))

time: 18.5 us -> 18.6 us (level)
  transfers between devices with their start and end apart: 6 -> 6, of which waited for: 6 -> 5; matrix products, arithmetic and copies ran while one was open for 0% -> 0% of each run, Pallas kernels for 0% -> 0%
where the time goes in v11:
time: 18.6 us; the launch traced here: 18.4 us
  waiting for transfers between devices  7.65 us (41%)
  starting transfers between devices  7.33 us (39%)
  Pallas kernels  3.42 us (18%)
    ppermute x4, starting transfers between devices, exchange(): return lax.ppermute(array, ('groups', 'seq', 'tensor'), pairs)  6.5 us
    ppermute x4, waiting for transfers between devices, exchange(): return lax.ppermute(array, ('groups', 'seq', 'tensor'), pairs)  5.92 us
    pallas_call x1, Pallas kernels, shards(): pl.pallas_call(functools.partial(project, spans), out_shape=[jax.ShapeDty...  2.64 us
    ppermute x2, waiting for transfers between devices, swap(): return lax.ppermute(array, 'tensor', [(0, 1), (1, 0)])  1.73 us
    ppermute x2, starting transfers between devices, swap(): return lax.ppermute(array, 'tensor', [(0, 1), (1, 0)])  0.83 us
    pallas_call x1, Pallas kernels, shards(): pl.pallas_call(score, out_shape=jax.ShapeDtypeStruct((seq_count, queries....  0.77 us
  transfers between devices with their start and end apart: 6, of which 5 were waited for; matrix products, arithmetic and copies ran while one was open for 0% of the time, Pallas kernels for 0%

profile of v11, /device:TPU:0, one launch (start us, length us, event | category | flops | bytes accessed | tf_op | source)
XLA Modules:
  0.0 18.4 jit_solution(14734577765577344541)
XLA Ops:
  0.0 0.0 copy-start
  0.0 2.6 %project.1 = (f32[128,128]{1,0:T(8,128)S(1)}, bf16[128,128]{1,0:T(8,128)(2,1)S(1)}) custom-call(s32[2]{0:T(128)} %lengths.1, bf16[128,7168]{1,0:T(8,128)(2,1)} %inputs.1, bf16[128,4096]{1,0:T(8,128)(2,1)} %grads.1, bf16[64,7168]{1,0:T(8,128)(2,1)} %bitcast.3, bf16[64,4096]{1,0:T(8,128)(2,1)} %bitcast.4), custom_call_target="tpu_custom_call" | custom-call | tf_op jit(solution)/shard_map/project/pallas_call | solution.py:245
  2.6 0.5 %collective-permute-start = (bf16[128,128]{1,0:T(8,128)(2,1)S(1)}, bf16[128,128]{1,0:T(8,128)(2,1)S(1)}, u32[]{:S(2)}, u32[]{:S(2)}) collective-permute-start(bf16[128,128]{1,0:T(8,128)(2,1)S(1)} %get-tuple-element.8), channel_id=1, source_target_pairs={{0,1},{1,0},{2,3},{3,2},{4,5},{5,4},{6,7},{7,6},{8,9},{9,8},{10,11... | collective-permute-start | bytes 98312 | tf_op jit(solution)/shard_map/ppermute | solution.py:218
  3.2 0.9 %collective-permute-done.other = bf16[128,128]{1,0:T(8,128)(2,1)S(1)} collective-permute-done((bf16[128,128]{1,0:T(8,128)(2,1)S(1)}, bf16[128,128]{1,0:T(8,128)(2,1)S(1)}, u32[]{:S(2)}, u32[]{:S(2)}) %collective-permute-start) | collective-permute-done | bytes 32800 | tf_op jit(solution)/shard_map/ppermute | solution.py:218
  4.0 2.9 %collective-permute-start.3 = (f32[1,65,128]{2,1,0:T(8,128)S(1)}, f32[1,65,128]{2,1,0:T(8,128)S(1)}, u32[]{:S(2)}, u32[]{:S(2)}) collective-permute-start(f32[1,65,128]{2,1,0:T(8,128)S(1)} %moments.1), channel_id=1, source_target_pairs={{0,4},{1,7},{2,6},{3,5},{4,0},{5,3},{6,2},{7,1},{8,12},{9,15},{10,... | collective-permute-start | bytes 99848 | tf_op jit(solution)/shard_map/ppermute | solution.py:227
  7.0 1.5 %collective-permute-start.2 = (f32[1,65,128]{2,1,0:T(8,128)S(1)}, f32[1,65,128]{2,1,0:T(8,128)S(1)}, u32[]{:S(2)}, u32[]{:S(2)}) collective-permute-start(f32[1,65,128]{2,1,0:T(8,128)S(1)} %moments.1), channel_id=1, source_target_pairs={{0,16},{1,5},{2,18},{3,7},{4,20},{5,1},{6,22},{7,3},{8,24},{9,13},... | collective-permute-start | bytes 99848 | tf_op jit(solution)/shard_map/ppermute | solution.py:227
  8.5 0.5 %collective-permute-start.1 = (f32[1,65,128]{2,1,0:T(8,128)S(1)}, f32[1,65,128]{2,1,0:T(8,128)S(1)}, u32[]{:S(2)}, u32[]{:S(2)}) collective-permute-start(f32[1,65,128]{2,1,0:T(8,128)S(1)} %moments.1), channel_id=1, source_target_pairs={{0,16},{1,3},{2,18},{3,1},{4,20},{5,7},{6,22},{7,5},{8,24},{9,11},... | collective-permute-start | bytes 99848 | tf_op jit(solution)/shard_map/ppermute | solution.py:227
  9.0 0.0 collective-permute-done.3
  9.0 1.9 %collective-permute-done.2 = f32[1,65,128]{2,1,0:T(8,128)S(1)} collective-permute-done((f32[1,65,128]{2,1,0:T(8,128)S(1)}, f32[1,65,128]{2,1,0:T(8,128)S(1)}, u32[]{:S(2)}, u32[]{:S(2)}) %collective-permute-start.2) | collective-permute-done | bytes 33312 | tf_op jit(solution)/shard_map/ppermute | solution.py:227
  10.9 1.5 %collective-permute-done.1 = f32[1,65,128]{2,1,0:T(8,128)S(1)} collective-permute-done((f32[1,65,128]{2,1,0:T(8,128)S(1)}, f32[1,65,128]{2,1,0:T(8,128)S(1)}, u32[]{:S(2)}, u32[]{:S(2)}) %collective-permute-start.1) | collective-permute-done | bytes 33312 | tf_op jit(solution)/shard_map/ppermute | solution.py:227
  12.4 1.6 %collective-permute-start.4 = (f32[1,65,128]{2,1,0:T(8,128)S(1)}, f32[1,65,128]{2,1,0:T(8,128)S(1)}, u32[]{:S(2)}, u32[]{:S(2)}) collective-permute-start(f32[1,65,128]{2,1,0:T(8,128)S(1)} %add_add_fusion.mine), channel_id=1, source_target_pairs={{0,2},{1,9},{2,0},{3,11},{4,6},{5,13},{6,4},{7,15},{8,10},{9,1},{1... | collective-permute-start | bytes 99848 | tf_op jit(solution)/shard_map/ppermute | solution.py:227
  14.0 2.5 %collective-permute-done.4.other = f32[1,65,128]{2,1,0:T(8,128)S(1)} collective-permute-done((f32[1,65,128]{2,1,0:T(8,128)S(1)}, f32[1,65,128]{2,1,0:T(8,128)S(1)}, u32[]{:S(2)}, u32[]{:S(2)}) %collective-permute-start.4) | collective-permute-done | bytes 33312 | tf_op jit(solution)/shard_map/ppermute | solution.py:227
  16.5 0.3 %collective-permute-start.5 = (bf16[2,32,128]{2,1,0:T(8,128)(2,1)S(1)}, bf16[2,32,128]{2,1,0:T(8,128)(2,1)S(1)}, u32[]{:S(2)}, u32[]{:S(2)}) collective-permute-start(bf16[2,32,128]{2,1,0:T(8,128)(2,1)S(1)} %weigh.1.mine), channel_id=1, source_target_pairs={{0,1},{1,0},{2,3},{3,2},{4,5},{5,4},{6,7},{7,6},{8,9},{9,8},{10,11... | collective-permute-start | bytes 49160 | tf_op jit(solution)/shard_map/ppermute | solution.py:218
  16.8 0.9 %collective-permute-done.5.other = bf16[2,32,128]{2,1,0:T(8,128)(2,1)S(1)} collective-permute-done((bf16[2,32,128]{2,1,0:T(8,128)(2,1)S(1)}, bf16[2,32,128]{2,1,0:T(8,128)(2,1)S(1)}, u32[]{:S(2)}, u32[]{:S(2)}) %collective-permute-start.5) | collective-permute-done | bytes 16416 | tf_op jit(solution)/shard_map/ppermute | solution.py:218
  17.7 0.0 copy-done
  17.7 0.8 %score.1 = f32[2,16]{1,0:T(2,128)} custom-call(bf16[2,32,128]{2,1,0:T(8,128)(2,1)S(1)} %weigh.1.mine, bf16[2,32,128]{2,1,0:T(8,128)(2,1)S(1)} %collective-permute-done.5.other, bf16[16,4096]{1,0:T(8,128)(2,1)S(1)} %copy-done), custom_call_target="tpu_custom_call" | custom-call | tf_op jit(solution)/shard_map/score/pallas_call | solution.py:293
  (4 shorter events, 0.0 us)
Async XLA Ops:
  0.0 17.7 %copy-start = (bf16[16,4096]{1,0:T(8,128)(2,1)S(1)}, bf16[16,4096]{1,0:T(8,128)(2,1)}, u32[]{:S(2)}) copy-start(bf16[16,4096]{1,0:T(8,128)(2,1)} %queries.1) | copy-start | bytes 393220
  2.6 1.4 %collective-permute-start = (bf16[128,128]{1,0:T(8,128)(2,1)S(1)}, bf16[128,128]{1,0:T(8,128)(2,1)S(1)}, u32[]{:S(2)}, u32[]{:S(2)}) collective-permute-start(bf16[128,128]{1,0:T(8,128)(2,1)S(1)} %get-tuple-element.8), channel_id=1, source_target_pairs={{0,1},{1,0},{2,3},{3,2},{4,5},{5,4},{6,7},{7,6},{8,9},{9,8},{10,11... | collective-permute-start | bytes 98312 | tf_op jit(solution)/shard_map/ppermute | solution.py:218
  4.0 5.0 %collective-permute-start.3 = (f32[1,65,128]{2,1,0:T(8,128)S(1)}, f32[1,65,128]{2,1,0:T(8,128)S(1)}, u32[]{:S(2)}, u32[]{:S(2)}) collective-permute-start(f32[1,65,128]{2,1,0:T(8,128)S(1)} %moments.1), channel_id=1, source_target_pairs={{0,4},{1,7},{2,6},{3,5},{4,0},{5,3},{6,2},{7,1},{8,12},{9,15},{10,... | collective-permute-start | bytes 99848 | tf_op jit(solution)/shard_map/ppermute | solution.py:227
  7.0 4.0 %collective-permute-start.2 = (f32[1,65,128]{2,1,0:T(8,128)S(1)}, f32[1,65,128]{2,1,0:T(8,128)S(1)}, u32[]{:S(2)}, u32[]{:S(2)}) collective-permute-start(f32[1,65,128]{2,1,0:T(8,128)S(1)} %moments.1), channel_id=1, source_target_pairs={{0,16},{1,5},{2,18},{3,7},{4,20},{5,1},{6,22},{7,3},{8,24},{9,13},... | collective-permute-start | bytes 99848 | tf_op jit(solution)/shard_map/ppermute | solution.py:227
  8.5 4.0 %collective-permute-start.1 = (f32[1,65,128]{2,1,0:T(8,128)S(1)}, f32[1,65,128]{2,1,0:T(8,128)S(1)}, u32[]{:S(2)}, u32[]{:S(2)}) collective-permute-start(f32[1,65,128]{2,1,0:T(8,128)S(1)} %moments.1), channel_id=1, source_target_pairs={{0,16},{1,3},{2,18},{3,1},{4,20},{5,7},{6,22},{7,5},{8,24},{9,11},... | collective-permute-start | bytes 99848 | tf_op jit(solution)/shard_map/ppermute | solution.py:227
  12.4 4.0 %collective-permute-start.4 = (f32[1,65,128]{2,1,0:T(8,128)S(1)}, f32[1,65,128]{2,1,0:T(8,128)S(1)}, u32[]{:S(2)}, u32[]{:S(2)}) collective-permute-start(f32[1,65,128]{2,1,0:T(8,128)S(1)} %add_add_fusion.mine), channel_id=1, source_target_pairs={{0,2},{1,9},{2,0},{3,11},{4,6},{5,13},{6,4},{7,15},{8,10},{9,1},{1... | collective-permute-start | bytes 99848 | tf_op jit(solution)/shard_map/ppermute | solution.py:227
  16.5 1.2 %collective-permute-start.5 = (bf16[2,32,128]{2,1,0:T(8,128)(2,1)S(1)}, bf16[2,32,128]{2,1,0:T(8,128)(2,1)S(1)}, u32[]{:S(2)}, u32[]{:S(2)}) collective-permute-start(bf16[2,32,128]{2,1,0:T(8,128)(2,1)S(1)} %weigh.1.mine), channel_id=1, source_target_pairs={{0,1},{1,0},{2,3},{3,2},{4,5},{5,4},{6,7},{7,6},{8,9},{9,8},{10,11... | collective-permute-start | bytes 49160 | tf_op jit(solution)/shard_map/ppermute | solution.py:218

commit v12 on v7

--- a/solution.py
+++ b/solution.py
@@ -64,8 +64,8 @@
         x_left, g_right, x_right = (
             pltpu.matmul_pop(accs[2 * kind]) + pltpu.matmul_pop(accs[2 * kind + 1]) for kind in range(3)
         )
-        out[:width, :] = jnp.where(valid, x_left[:, :tokens] + x_right[:, tokens:], 0.0)
-        out[width:, :] = jnp.where(valid, g_right[:, tokens:], 0.0)
+        out[:width, :] = jnp.where(valid, x_left[:, :tokens] + x_right[:, tokens:], 0.0).astype(out.dtype)
+        out[width:, :] = jnp.where(valid, g_right[:, tokens:], 0.0).astype(out.dtype)
 
     pl.run_scoped(multiply, *(pltpu.ACC(mxu_id=unit)((width, tile), F32) for unit in (0, 1, 0, 1, 0, 1)))
 
@@ -85,8 +85,9 @@
 
     @pl.when(lax.axis_index("tensor") == 1)
     def _():
-        z = mine[...] + other[...]
-        square = dot3(z, z, NT)
+        z = mine[...].astype(F32) + other[...].astype(F32)
+        zb = z.astype(jnp.bfloat16)
+        square = lax.dot_general(zb, zb, NT, preferred_element_type=F32)
         width = square.shape[0] // 2
         top, bottom = square[:width], pltpu.roll(square[width:], width, 1)
         row = lax.broadcasted_iota(jnp.int32, top.shape, 0)
@@ -242,7 +243,7 @@
     params = pltpu.CompilerParams(vmem_limit_bytes=16 << 20)
     partial_z = pl.pallas_call(
         functools.partial(project, spans),
-        out_shape=jax.ShapeDtypeStruct((2 * width, tokens), F32),
+        out_shape=jax.ShapeDtypeStruct((2 * width, tokens), jnp.bfloat16),
         in_specs=[HBM] * 5,
         out_specs=VMEM,
         scratch_shapes=[
@@ -253,7 +254,7 @@
         compiler_params=params,
         name="project",
     )(*map(stay, (lengths, inputs, out_grads, proj_in.T, proj_out.T)))
-    packed_rows = width + 8
+    packed_rows = width + 1
     packed = pl.pallas_call(
         moments,
         out_shape=jax.ShapeDtypeStruct((1, packed_rows, 2 * width), F32),

time: 18.6 us -> 18.5 us (level)
  no operation moved by 1% of the time
where the time goes in v12:
time: 18.5 us; the launch traced here: 18.4 us
  waiting for transfers between devices  7.56 us (41%)
  starting transfers between devices  7.39 us (40%)
  Pallas kernels  3.41 us (18%)
    ppermute x4, starting transfers between devices, exchange(): return lax.ppermute(array, ('groups', 'seq', 'tensor'), pairs)  6.42 us
    ppermute x4, waiting for transfers between devices, exchange(): return lax.ppermute(array, ('groups', 'seq', 'tensor'), pairs)  5.86 us
    pallas_call x1, Pallas kernels, shards(): pl.pallas_call(functools.partial(project, spans), out_shape=jax.ShapeDtyp...  2.64 us
    ppermute x2, waiting for transfers between devices, swap(): return lax.ppermute(array, 'tensor', [(0, 1), (1, 0)])  1.7 us
    ppermute x2, starting transfers between devices, swap(): return lax.ppermute(array, 'tensor', [(0, 1), (1, 0)])  0.97 us
    pallas_call x1, Pallas kernels, shards(): pl.pallas_call(score, out_shape=jax.ShapeDtypeStruct((seq_count, queries....  0.77 us
  transfers between devices with their start and end apart: 6, of which 6 were waited for; matrix products, arithmetic and copies ran while one was open for 0% of the time, Pallas kernels for 0%

profile of v12, /device:TPU:0, one launch (start us, length us, event | category | flops | bytes accessed | tf_op | source)
XLA Modules:
  0.0 18.4 jit_solution(15741092172811492967)
XLA Ops:
  0.0 0.0 copy-start
  0.0 2.6 %project.1.mine = bf16[128,128]{1,0:T(8,128)(2,1)S(1)} custom-call(s32[2]{0:T(128)} %lengths.1, bf16[128,7168]{1,0:T(8,128)(2,1)} %inputs.1, bf16[128,4096]{1,0:T(8,128)(2,1)} %grads.1, bf16[64,7168]{1,0:T(8,128)(2,1)} %bitcast.3, bf16[64,4096]{1,0:T(8,128)(2,1)} %bitcast.4), custom_call_target="tpu_custom_call" | custom-call | tf_op jit(solution)/shard_map/project/pallas_call | solution.py:244
  2.6 0.5 %collective-permute-start = (bf16[128,128]{1,0:T(8,128)(2,1)S(1)}, bf16[128,128]{1,0:T(8,128)(2,1)S(1)}, u32[]{:S(2)}, u32[]{:S(2)}) collective-permute-start(bf16[128,128]{1,0:T(8,128)(2,1)S(1)} %project.1.mine), channel_id=1, source_target_pairs={{0,1},{1,0},{2,3},{3,2},{4,5},{5,4},{6,7},{7,6},{8,9},{9,8},{10,11... | collective-permute-start | bytes 98312 | tf_op jit(solution)/shard_map/ppermute | solution.py:217
  3.2 0.9 %collective-permute-done.other = bf16[128,128]{1,0:T(8,128)(2,1)S(1)} collective-permute-done((bf16[128,128]{1,0:T(8,128)(2,1)S(1)}, bf16[128,128]{1,0:T(8,128)(2,1)S(1)}, u32[]{:S(2)}, u32[]{:S(2)}) %collective-permute-start) | collective-permute-done | bytes 32800 | tf_op jit(solution)/shard_map/ppermute | solution.py:217
  4.0 3.8 %collective-permute-start.3 = (f32[1,65,128]{2,1,0:T(8,128)S(1)}, f32[1,65,128]{2,1,0:T(8,128)S(1)}, u32[]{:S(2)}, u32[]{:S(2)}) collective-permute-start(f32[1,65,128]{2,1,0:T(8,128)S(1)} %moments.1), channel_id=1, source_target_pairs={{0,6},{1,7},{2,4},{3,5},{4,2},{5,3},{6,0},{7,1},{8,14},{9,15},{10,... | collective-permute-start | bytes 99848 | tf_op jit(solution)/shard_map/ppermute | solution.py:226
  7.9 0.4 %collective-permute-start.2 = (f32[1,65,128]{2,1,0:T(8,128)S(1)}, f32[1,65,128]{2,1,0:T(8,128)S(1)}, u32[]{:S(2)}, u32[]{:S(2)}) collective-permute-start(f32[1,65,128]{2,1,0:T(8,128)S(1)} %moments.1), channel_id=1, source_target_pairs={{0,4},{1,5},{2,6},{3,7},{4,0},{5,1},{6,2},{7,3},{8,12},{9,13},{10,... | collective-permute-start | bytes 99848 | tf_op jit(solution)/shard_map/ppermute | solution.py:226
  8.3 1.6 %collective-permute-start.1 = (f32[1,65,128]{2,1,0:T(8,128)S(1)}, f32[1,65,128]{2,1,0:T(8,128)S(1)}, u32[]{:S(2)}, u32[]{:S(2)}) collective-permute-start(f32[1,65,128]{2,1,0:T(8,128)S(1)} %moments.1), channel_id=1, source_target_pairs={{0,4},{1,3},{2,6},{3,1},{4,0},{5,7},{6,2},{7,5},{8,12},{9,11},{10,... | collective-permute-start | bytes 99848 | tf_op jit(solution)/shard_map/ppermute | solution.py:226
  9.9 0.1 collective-permute-done.3
  10.0 1.9 %collective-permute-done.2 = f32[1,65,128]{2,1,0:T(8,128)S(1)} collective-permute-done((f32[1,65,128]{2,1,0:T(8,128)S(1)}, f32[1,65,128]{2,1,0:T(8,128)S(1)}, u32[]{:S(2)}, u32[]{:S(2)}) %collective-permute-start.2) | collective-permute-done | bytes 33312 | tf_op jit(solution)/shard_map/ppermute | solution.py:226
  11.8 0.4 %collective-permute-done.1 = f32[1,65,128]{2,1,0:T(8,128)S(1)} collective-permute-done((f32[1,65,128]{2,1,0:T(8,128)S(1)}, f32[1,65,128]{2,1,0:T(8,128)S(1)}, u32[]{:S(2)}, u32[]{:S(2)}) %collective-permute-start.1) | collective-permute-done | bytes 33312 | tf_op jit(solution)/shard_map/ppermute | solution.py:226
  12.3 0.5 %collective-permute-start.4 = (f32[1,65,128]{2,1,0:T(8,128)S(1)}, f32[1,65,128]{2,1,0:T(8,128)S(1)}, u32[]{:S(2)}, u32[]{:S(2)}) collective-permute-start(f32[1,65,128]{2,1,0:T(8,128)S(1)} %add_add_fusion.mine), channel_id=1, source_target_pairs={{0,2},{1,9},{2,0},{3,11},{4,6},{5,13},{6,4},{7,15},{8,10},{9,1},{1... | collective-permute-start | bytes 99848 | tf_op jit(solution)/shard_map/ppermute | solution.py:226
  12.8 3.5 %collective-permute-done.4.other = f32[1,65,128]{2,1,0:T(8,128)S(1)} collective-permute-done((f32[1,65,128]{2,1,0:T(8,128)S(1)}, f32[1,65,128]{2,1,0:T(8,128)S(1)}, u32[]{:S(2)}, u32[]{:S(2)}) %collective-permute-start.4) | collective-permute-done | bytes 33312 | tf_op jit(solution)/shard_map/ppermute | solution.py:226
  16.3 0.5 %collective-permute-start.5 = (bf16[2,32,128]{2,1,0:T(8,128)(2,1)S(1)}, bf16[2,32,128]{2,1,0:T(8,128)(2,1)S(1)}, u32[]{:S(2)}, u32[]{:S(2)}) collective-permute-start(bf16[2,32,128]{2,1,0:T(8,128)(2,1)S(1)} %weigh.1.mine), channel_id=1, source_target_pairs={{0,1},{1,0},{2,3},{3,2},{4,5},{5,4},{6,7},{7,6},{8,9},{9,8},{10,11... | collective-permute-start | bytes 49160 | tf_op jit(solution)/shard_map/ppermute | solution.py:217
  16.8 0.8 %collective-permute-done.5.other = bf16[2,32,128]{2,1,0:T(8,128)(2,1)S(1)} collective-permute-done((bf16[2,32,128]{2,1,0:T(8,128)(2,1)S(1)}, bf16[2,32,128]{2,1,0:T(8,128)(2,1)S(1)}, u32[]{:S(2)}, u32[]{:S(2)}) %collective-permute-start.5) | collective-permute-done | bytes 16416 | tf_op jit(solution)/shard_map/ppermute | solution.py:217
  17.6 0.0 copy-done
  17.6 0.8 %score.1 = f32[2,16]{1,0:T(2,128)} custom-call(bf16[2,32,128]{2,1,0:T(8,128)(2,1)S(1)} %weigh.1.mine, bf16[2,32,128]{2,1,0:T(8,128)(2,1)S(1)} %collective-permute-done.5.other, bf16[16,4096]{1,0:T(8,128)(2,1)S(1)} %copy-done), custom_call_target="tpu_custom_call" | custom-call | tf_op jit(solution)/shard_map/score/pallas_call | solution.py:292
  (4 shorter events, 0.0 us)
Async XLA Ops:
  0.0 17.6 %copy-start = (bf16[16,4096]{1,0:T(8,128)(2,1)S(1)}, bf16[16,4096]{1,0:T(8,128)(2,1)}, u32[]{:S(2)}) copy-start(bf16[16,4096]{1,0:T(8,128)(2,1)} %queries.1) | copy-start | bytes 393220
  2.6 1.4 %collective-permute-start = (bf16[128,128]{1,0:T(8,128)(2,1)S(1)}, bf16[128,128]{1,0:T(8,128)(2,1)S(1)}, u32[]{:S(2)}, u32[]{:S(2)}) collective-permute-start(bf16[128,128]{1,0:T(8,128)(2,1)S(1)} %project.1.mine), channel_id=1, source_target_pairs={{0,1},{1,0},{2,3},{3,2},{4,5},{5,4},{6,7},{7,6},{8,9},{9,8},{10,11... | collective-permute-start | bytes 98312 | tf_op jit(solution)/shard_map/ppermute | solution.py:217
  4.0 6.0 %collective-permute-start.3 = (f32[1,65,128]{2,1,0:T(8,128)S(1)}, f32[1,65,128]{2,1,0:T(8,128)S(1)}, u32[]{:S(2)}, u32[]{:S(2)}) collective-permute-start(f32[1,65,128]{2,1,0:T(8,128)S(1)} %moments.1), channel_id=1, source_target_pairs={{0,6},{1,7},{2,4},{3,5},{4,2},{5,3},{6,0},{7,1},{8,14},{9,15},{10,... | collective-permute-start | bytes 99848 | tf_op jit(solution)/shard_map/ppermute | solution.py:226
  7.9 4.0 %collective-permute-start.2 = (f32[1,65,128]{2,1,0:T(8,128)S(1)}, f32[1,65,128]{2,1,0:T(8,128)S(1)}, u32[]{:S(2)}, u32[]{:S(2)}) collective-permute-start(f32[1,65,128]{2,1,0:T(8,128)S(1)} %moments.1), channel_id=1, source_target_pairs={{0,4},{1,5},{2,6},{3,7},{4,0},{5,1},{6,2},{7,3},{8,12},{9,13},{10,... | collective-permute-start | bytes 99848 | tf_op jit(solution)/shard_map/ppermute | solution.py:226
  8.3 4.0 %collective-permute-start.1 = (f32[1,65,128]{2,1,0:T(8,128)S(1)}, f32[1,65,128]{2,1,0:T(8,128)S(1)}, u32[]{:S(2)}, u32[]{:S(2)}) collective-permute-start(f32[1,65,128]{2,1,0:T(8,128)S(1)} %moments.1), channel_id=1, source_target_pairs={{0,4},{1,3},{2,6},{3,1},{4,0},{5,7},{6,2},{7,5},{8,12},{9,11},{10,... | collective-permute-start | bytes 99848 | tf_op jit(solution)/shard_map/ppermute | solution.py:226
  12.3 4.0 %collective-permute-start.4 = (f32[1,65,128]{2,1,0:T(8,128)S(1)}, f32[1,65,128]{2,1,0:T(8,128)S(1)}, u32[]{:S(2)}, u32[]{:S(2)}) collective-permute-start(f32[1,65,128]{2,1,0:T(8,128)S(1)} %add_add_fusion.mine), channel_id=1, source_target_pairs={{0,2},{1,9},{2,0},{3,11},{4,6},{5,13},{6,4},{7,15},{8,10},{9,1},{1... | collective-permute-start | bytes 99848 | tf_op jit(solution)/shard_map/ppermute | solution.py:226
  16.3 1.3 %collective-permute-start.5 = (bf16[2,32,128]{2,1,0:T(8,128)(2,1)S(1)}, bf16[2,32,128]{2,1,0:T(8,128)(2,1)S(1)}, u32[]{:S(2)}, u32[]{:S(2)}) collective-permute-start(bf16[2,32,128]{2,1,0:T(8,128)(2,1)S(1)} %weigh.1.mine), channel_id=1, source_target_pairs={{0,1},{1,0},{2,3},{3,2},{4,5},{5,4},{6,7},{7,6},{8,9},{9,8},{10,11... | collective-permute-start | bytes 49160 | tf_op jit(solution)/shard_map/ppermute | solution.py:217
